TPU v7x, 128 devices: a whole 4x4x4 slice. The times are simulated.
128 devices in a mesh: box: 16 (over y, x), grp: 8 (over z, core).
Axes of the slice: x: 4, y: 4, z: 4, core: 2. Of those that a mesh axis runs over, the one named last changes fastest.
Arguments:
- density: float32 [512, 768, 128], P('box', 'grp'), may hold values from 0.5 to 2
- momentum: float32 [3, 512, 768, 128], P(None, 'box', 'grp'), may hold values from -0.65 to 0.65
- energy: float32 [512, 768, 128], P('box', 'grp'), may hold values from 2 to 4
- dm_density: float32 [512, 768, 128], P('box', 'grp'), may hold values from 0.1 to 2
- box_dest: int32 [8, 16, 12, 1], P('grp', 'box'), may hold values from 0 to 15; in each aligned block of 12 rows (0 to 11, 12 to 23, ..., all dimensions but the last counted through in order) at most 2 rows name the same one
Outputs:
- new_density: float32 [512, 768, 128], P('box', 'grp')
- new_momentum: float32 [3, 512, 768, 128], P(None, 'box', 'grp')
- new_energy: float32 [512, 768, 128], P('box', 'grp')
- kd_density: float32 [8, 16, 16, 2, 32, 1024], P('grp', 'box')
Inputs may be any that keep to these rules, and one draw needn't show every extreme that they name: `box_dest`: of the 12 boxes of one device, at most 2 name the same owner; every owner is named by some box of the whole array.
All inputs are finite; a program needn't handle non-finite values.
Results may differ from a plain program's by a relative error of at most 0.0003.
Values sent between devices are 32-bit elements; how exact they have to be, the bound alone decides.
No kernel may reach another device: no remote copies, remote signals or barrier semaphores. Data moves between devices by JAX's collectives and lax.ppermute only.
A program may use at most 192 MiB of HBM per device.

v0:
```python
import jax
import jax.numpy as jnp
from jax import lax
from jax.sharding import PartitionSpec as P

BOX = 32
BOX_Y = 3
BOX_Z = 4
RADIUS = 2


gamma_gas = 5.0 / 3.0
step_ratio = 0.06


def with_halo(value, sides, width):
    for axis, dim in sides:
        size, length = (lax.axis_size(axis), value.shape[dim])
        up = [(i, (i + 1) % size) for i in range(size)]
        down = [(j, i) for i, j in up]
        last = lax.slice_in_dim(value, length - width, length, axis=dim)
        first = lax.slice_in_dim(value, 0, width, axis=dim)
        before = lax.ppermute(last, axis, up)
        after = lax.ppermute(first, axis, down)
        value = jnp.concatenate([before, value, after], axis=dim)
    return value


def cut_along(values, offset, length, sweep_axis):
    return lax.slice_in_dim(values, offset, offset + length, axis=sweep_axis)


def flux_of(conserved, normal):
    density = conserved[0]
    energy = conserved[4]
    kinetic = (
        0.5
        * (conserved[1] * conserved[1] + conserved[2] * conserved[2] + conserved[3] * conserved[3])
        / density
    )
    pressure = (gamma_gas - 1.0) * (energy - kinetic)
    velocity = conserved[normal] / density
    rows_added = [jnp.zeros_like(pressure)]
    for component in range(1, 4):
        rows_added.append(pressure if component == normal else jnp.zeros_like(pressure))
    rows_added.append(pressure * velocity)
    fluxes = conserved * velocity[None] + jnp.stack(rows_added)
    sound_speed = jnp.sqrt(gamma_gas * pressure / density)
    return (fluxes, jnp.abs(velocity) + sound_speed)


def sweep_line(padded, sweep_axis, normal):
    length = padded.shape[sweep_axis] - 6
    cell_prev = cut_along(padded, 0, length + 3, sweep_axis)
    cell_here = cut_along(padded, 1, length + 3, sweep_axis)
    cell_next = cut_along(padded, 2, length + 3, sweep_axis)
    cell_far = cut_along(padded, 3, length + 3, sweep_axis)
    interface = (7.0 * (cell_here + cell_next) - (cell_prev + cell_far)) / 12.0
    interface = jnp.minimum(
        jnp.maximum(interface, jnp.minimum(cell_here, cell_next)), jnp.maximum(cell_here, cell_next)
    )
    centre = cut_along(padded, 2, length + 2, sweep_axis)
    dev_left = cut_along(interface, 0, length + 2, sweep_axis) - centre
    dev_right = cut_along(interface, 1, length + 2, sweep_axis) - centre
    edge_left = centre + jnp.clip(dev_left, -2.0 * jnp.abs(dev_right), 2.0 * jnp.abs(dev_right))
    edge_right = centre + jnp.clip(dev_right, -2.0 * jnp.abs(dev_left), 2.0 * jnp.abs(dev_left))
    state_left = cut_along(edge_right, 0, length + 1, sweep_axis)
    state_right = cut_along(edge_left, 1, length + 1, sweep_axis)
    flux_left, reach_left = flux_of(state_left, normal)
    flux_right, reach_right = flux_of(state_right, normal)
    wave_speed = jnp.maximum(reach_left, reach_right)
    face_flux = 0.5 * (flux_left + flux_right) - 0.5 * wave_speed[None] * (state_right - state_left)
    inside = cut_along(padded, 3, length, sweep_axis)
    return inside - step_ratio * (
        cut_along(face_flux, 1, length, sweep_axis) - cut_along(face_flux, 0, length, sweep_axis)
    )


def sweep_blocks(padded, sweep_axis, normal, block_axis, block_size):
    out_shape = list(padded.shape)
    out_shape[sweep_axis] -= 6
    block_count = padded.shape[block_axis] // block_size

    def one_block(block_index, result):
        offset = (block_index * block_size).astype(jnp.int32)
        portion = lax.dynamic_slice_in_dim(padded, offset, block_size, block_axis)
        swept = sweep_line(portion, sweep_axis, normal)
        return lax.dynamic_update_slice_in_dim(result, swept, offset, block_axis)

    return lax.fori_loop(0, block_count, one_block, jnp.zeros(out_shape, padded.dtype))


def wrap_pad(values, margin, pad_axis):
    extent = values.shape[pad_axis]
    return jnp.concatenate(
        [
            cut_along(values, extent - margin, margin, pad_axis),
            values,
            cut_along(values, 0, margin, pad_axis),
        ],
        axis=pad_axis,
    )


def box_filter(padded, radius):
    result = padded
    for filter_axis in range(padded.ndim - 3, padded.ndim):
        extent = result.shape[filter_axis] - 2 * radius
        summed = cut_along(result, 0, extent, filter_axis)
        for shift_by in range(1, 2 * radius + 1):
            summed = summed + cut_along(result, shift_by, extent, filter_axis)
        result = summed
    return result / float((2 * radius + 1) ** 3)


def slot_selector(destination, owners, capacity):
    box_total = destination.shape[-1]
    positions = jnp.arange(box_total, dtype=jnp.int32)
    earlier = positions[None, :] < positions[:, None]
    same_dest = destination[..., :, None] == destination[..., None, :]
    slot_rank = jnp.sum((same_dest & earlier).astype(jnp.int32), axis=-1)
    owner_ids = jnp.arange(owners, dtype=jnp.int32)
    slot_ids = jnp.arange(capacity, dtype=jnp.int32)
    chosen = (destination[..., None, None, :] == owner_ids[:, None, None]) & (
        slot_rank[..., None, None, :] == slot_ids[None, :, None]
    )
    return chosen.astype(jnp.float32)


def body(density, momentum, energy, dm_density, box_dest):
    conserved = jnp.concatenate([density[None], momentum, energy[None]], axis=0)
    padded = with_halo(conserved, (("box", 1),), 3)
    conserved = sweep_blocks(padded, 1, 1, 2, 8)
    padded = with_halo(conserved, (("grp", 2),), 3)
    conserved = sweep_blocks(padded, 2, 2, 1, 8)
    conserved = sweep_blocks(wrap_pad(conserved, 3, 3), 3, 3, 1, 8)
    total_density = conserved[0] + dm_density
    rimmed = with_halo(total_density, (("box", 0), ("grp", 1)), RADIUS)
    rimmed = wrap_pad(rimmed, RADIUS, 2)
    owners = lax.axis_size("box")
    box_count = box_dest.shape[2]
    capacity = max(2, (box_count + owners - 1) // owners)
    selector = slot_selector(box_dest[0, 0, :, 0], owners, capacity)
    ghosted = BOX + 2 * RADIUS
    windows = []
    for row_box in range(BOX_Y):
        for col_box in range(BOX_Z):
            window = rimmed[
                :, row_box * BOX : row_box * BOX + ghosted, col_box * BOX : col_box * BOX + ghosted
            ]
            windows.append(window.reshape(ghosted, ghosted * ghosted))
    box_cells = jnp.stack(windows)
    send_buffer = jnp.einsum("jck,kab->jcab", selector, box_cells, precision=lax.Precision.HIGHEST)
    arriving = lax.all_to_all(send_buffer, "box", split_axis=0, concat_axis=0, tiled=True)
    cubes = arriving.reshape(arriving.shape[0], arriving.shape[1], ghosted, ghosted, ghosted)
    received = box_filter(cubes, RADIUS).reshape(
        arriving.shape[0], arriving.shape[1], BOX, BOX * BOX
    )
    return (conserved[0], conserved[1:4], conserved[4], received[None, None])


def solution(mesh):
    in_specs = (
        P("box", "grp", None),
        P(None, "box", "grp", None),
        P("box", "grp", None),
        P("box", "grp", None),
        P("grp", "box", None, None),
    )
    out_specs = (
        P("box", "grp", None),
        P(None, "box", "grp", None),
        P("box", "grp", None),
        P("grp", "box", None, None, None, None),
    )
    return jax.shard_map(body, mesh=mesh, in_specs=in_specs, out_specs=out_specs, check_vma=False)
```

profile of v0, /device:TPU:32, one launch (start us, length us, event | category | flops | bytes accessed | tf_op | source)
XLA Modules:
  0.0 656.6 jit_solution(9727355039770951309)
XLA Ops:
  0.7 2.7 pad_maximum_fusion.32
  4.9 3.9 collective-permute-start.1
  8.7 16.7 %collective-permute-done = f32[5,3,96,128]{3,2,1,0:T(8,128)} collective-permute-done((f32[5,3,96,128]{3,2,1,0:T(8,128)}, f32[5,3,96,128]{3,2,1,0:T(8,128)}, u32[]{:S(2)}, u32[]{:S(2)}) %collective-permute-start) | collective-permute-done | bytes 737312 | tf_op jit(solution)/shard_map/ppermute | solution.py:23
  25.4 7.4 %pad_maximum_fusion.2 = f32[5,38,96,128]{3,2,1,0:T(8,128)} fusion(f32[5,3,96,128]{3,2,1,0:T(8,128)} %collective-permute-done.1, f32[1,32,96,128]{3,2,1,0:T(8,128)S(1)} %bitcast.64, f32[3,32,96,128]{3,2,1,0:T(8,128)} %param.12, f32[1,32,96,128]{3,2,1,0:T(8,128)S(1)} %bitcast.66, f32[5,3,96,128]{3,2,1,0:T(8,128)} %collective-permute-done), kind=kLoop, calls=%fused_computation.138 | loop fusion | flops 9338880 | bytes 18677760 | tf_op jit(solution)/shard_map/concatenate | solution.py:25
  32.8 4.1 broadcast.547.clone.1
  36.9 83.1 %while.48 = (s32[]{:T(128)}, f32[5,32,96,128]{3,2,1,0:T(8,128)}, f32[5,38,96,128]{3,2,1,0:T(8,128)}, s32[]{:T(128)}, s32[]{:T(128)}, /*index=5*/s32[]{:T(128)}, ...) while((s32[]{:T(128)}, f32[5,32,96,128]{3,2,1,0:T(8,128)}, f32[5,38,96,128]{3,2,1,0:T(8,128)}, ...), condition=%wide.region_1.2_spmd, body=%wide.region_0.1_spmd.sunk | while | flops 8224777 | bytes 16040279 | solution.py:90
  43.8 2.7 fusion.103
  50.8 3.0 fusion.103
  78.3 2.7 fusion.103
  92.0 2.7 fusion.103
  99.0 3.0 fusion.103
  106.3 2.6 fusion.103
  113.3 2.6 fusion.103
  123.8 4.2 collective-permute-done.2
  128.0 6.1 pad_maximum_fusion.3
  134.1 4.1 broadcast.547.clone
  138.2 52.4 %while.49 = (s32[]{:T(128)}, f32[5,32,96,128]{3,2,1,0:T(8,128)}, f32[5,32,102,128]{3,2,1,0:T(8,128)}, s32[]{:T(128)}, s32[]{:T(128)}, /*index=5*/s32[]{:T(128)},...) while((s32[]{:T(128)}, f32[5,32,96,128]{3,2,1,0:T(8,128)}, f32[5,32,102,128]{3,2,1,0:T(8,128)}, ...), condition=%wide.region_3.4_spmd, body=%wide.region_2.3_spmd.sunk | while | flops 23887880 | bytes 46711128 | solution.py:90
  138.3 4.9 fusion.107
  143.1 2.9 minimum_add_fusion.10
  147.9 3.4 fusion.110
  151.4 4.8 fusion.107
  156.2 2.9 minimum_add_fusion.10
  161.0 3.5 fusion.110
  164.5 4.8 fusion.107
  169.4 2.9 minimum_add_fusion.10
  174.1 3.5 fusion.110
  177.7 4.8 fusion.107
  182.5 2.9 minimum_add_fusion.10
  187.2 3.4 fusion.110
  190.6 13.4 %fusion.87 = (f32[5,32,96,3]{3,2,1,0:T(8,128)}, f32[5,32,96,3]{3,2,1,0:T(8,128)}) fusion(f32[5,32,96,128]{3,2,1,0:T(8,128)} %get-tuple-element.305), kind=kLoop, calls=%fused_computation.185 | loop fusion | bytes 737280 | tf_op jit(solution)/shard_map/slice | solution.py:30
  204.0 16.0 %pad_maximum_fusion.1 = f32[5,32,96,134]{3,2,1,0:T(8,128)} fusion(f32[5,32,96,3]{3,2,1,0:T(8,128)} %get-tuple-element.386, f32[5,32,96,128]{3,2,1,0:T(8,128)} %get-tuple-element.305, f32[5,32,96,3]{3,2,1,0:T(8,128)} %get-tuple-element.385), kind=kLoop, calls=%fused_computation.137 | loop fusion | flops 4116480 | bytes 16465920 | tf_op jit(solution)/shard_map/concatenate | solution.py:95
  220.0 4.1 broadcast.547
  224.1 84.9 %while.50 = (s32[]{:T(128)}, f32[5,32,96,128]{3,2,1,0:T(8,128)}, f32[5,32,96,134]{3,2,1,0:T(8,128)}, s32[]{:T(128)}, s32[]{:T(128)}, /*index=5*/s32[]{:T(128)}, s32[]{:T(128)}, s32[]{}, s32[]{}, s32[]{}, /*index=10*/f32[]{:T(128)}) while((s32[]{:T(128)}, f32[5,32,96,128]{3,2,1,0:T(8,128)}, f32[5,32,96,134]{3,2,1,0:T(8,128)}, s32[]{:T(128)}, ...), condition=%wide.region_5.6_spmd, body=%wide.region_4.5_spmd.sunk | while | flops 22798860 | bytes 46534944 | solution.py:90
  224.2 9.4 %fusion.111 = f32[5,8,96,131]{3,2,1,0:T(8,128)S(1)} fusion(f32[5,32,96,134]{3,2,1,0:T(8,128)} %get-tuple-element.628, s32[]{:T(128)S(6)} %select_n.41, s32[]{:T(128)S(6)} %add.989, s32[]{:T(128)S(6)} %add.988, s32[]{:T(128)S(6)} %add.990), kind=kLoop, calls=%fused_computation.88.clone.1 | loop fusion | flops 4527360 | bytes 10060816 | tf_op jit(solution)/shard_map/while/body/eval_jaxpr/min | solution.py:59
  233.6 3.9 minimum_add_fusion.11
  241.1 4.5 fusion.114
  245.7 9.2 %fusion.111 = f32[5,8,96,131]{3,2,1,0:T(8,128)S(1)} fusion(f32[5,32,96,134]{3,2,1,0:T(8,128)} %get-tuple-element.628, s32[]{:T(128)S(6)} %select_n.41, s32[]{:T(128)S(6)} %add.989, s32[]{:T(128)S(6)} %add.988, s32[]{:T(128)S(6)} %add.990), kind=kLoop, calls=%fused_computation.88.clone.1 | loop fusion | flops 4527360 | bytes 10060816 | tf_op jit(solution)/shard_map/while/body/eval_jaxpr/min | solution.py:59
  254.9 3.9 minimum_add_fusion.11
  262.4 4.5 fusion.114
  267.0 8.9 %fusion.111 = f32[5,8,96,131]{3,2,1,0:T(8,128)S(1)} fusion(f32[5,32,96,134]{3,2,1,0:T(8,128)} %get-tuple-element.628, s32[]{:T(128)S(6)} %select_n.41, s32[]{:T(128)S(6)} %add.989, s32[]{:T(128)S(6)} %add.988, s32[]{:T(128)S(6)} %add.990), kind=kLoop, calls=%fused_computation.88.clone.1 | loop fusion | flops 4527360 | bytes 10060816 | tf_op jit(solution)/shard_map/while/body/eval_jaxpr/min | solution.py:59
  275.9 3.9 minimum_add_fusion.11
  283.4 4.5 fusion.114
  288.0 9.0 %fusion.111 = f32[5,8,96,131]{3,2,1,0:T(8,128)S(1)} fusion(f32[5,32,96,134]{3,2,1,0:T(8,128)} %get-tuple-element.628, s32[]{:T(128)S(6)} %select_n.41, s32[]{:T(128)S(6)} %add.989, s32[]{:T(128)S(6)} %add.988, s32[]{:T(128)S(6)} %add.990), kind=kLoop, calls=%fused_computation.88.clone.1 | loop fusion | flops 4527360 | bytes 10060816 | tf_op jit(solution)/shard_map/while/body/eval_jaxpr/min | solution.py:59
  297.0 3.9 minimum_add_fusion.11
  304.5 4.5 fusion.114
  309.0 2.8 fusion.86
  311.8 5.7 collective-permute-start.5
  328.1 2.7 pad_maximum_fusion.5
  337.7 3.0 pad_maximum_fusion.14
  347.7 3.0 pad_maximum_fusion.10
  357.9 9.7 %stack.105 = f32[12,36,1296]{2,0,1:T(8,128)S(1)} concatenate(f32[1,36,1296]{2,0,1:T(1,128)} %stack_reshape.36, f32[1,36,1296]{2,0,1:T(1,128)} %stack_reshape.37, f32[1,36,1296]{2,0,1:T(1,128)S(1)} %copy-done.7, f32[1,36,1296]{2,0,1:T(1,128)} %stack_reshape.39, f32[1,36,1296]{2,0,1:T(1,128)} %stack_reshape.40, f32[1,36,1296]{2,0,1:T(1,128)} %stack_reshape.41, ...), dimensions={0} | concatenate | bytes 4478976 | tf_op jit(solution)/shard_map/stack | solution.py:152
  367.6 4.6 fusion.73
  372.1 10.6 %copy.17 = f32[16,2,36,1296]{3,1,2,0:T(2,128)} copy(f32[16,2,36,1296]{3,0,2,1:T(8,128)} %fusion.73) | data formatting | bytes 11943936 | tf_op jit(solution)/shard_map/jck,kab->jcab/dot_general | solution.py:153
  382.7 7.5 %all-to-all-start = ((f32[16,2,36,1296]{3,1,2,0:T(2,128)}), f32[16,2,36,1296]{3,1,2,0:T(2,128)}, u32[]{:S(2)}, u32[]{:S(2)}) async-start(f32[16,2,36,1296]{3,1,2,0:T(2,128)} %copy.17), calls=%async_computation | async-start | bytes 12976128 | tf_op jit(solution)/shard_map/all_to_all | solution.py:154
  390.2 4.8 slice.924
  395.1 2.7 slice_bitcast_fusion
  397.7 89.3 %all-to-all-done = f32[16,2,36,1296]{3,1,2,0:T(2,128)} async-done(((f32[16,2,36,1296]{3,1,2,0:T(2,128)}), f32[16,2,36,1296]{3,1,2,0:T(2,128)}, u32[]{:S(2)}, u32[]{:S(2)}) %all-to-all-start) | async-done | bytes 5972000 | tf_op jit(solution)/shard_map/all_to_all | solution.py:154
  487.0 6.9 %copy.18 = f32[16,2,36,1296]{3,0,2,1:T(8,128)} copy(f32[16,2,36,1296]{3,1,2,0:T(2,128)} %all-to-all-done) | data formatting | bytes 11943936 | tf_op jit(solution)/shard_map/all_to_all | solution.py:154
  493.8 15.9 %reshape.65 = f32[16,2,36,36,36]{4,3,0,2,1:T(8,128)} reshape(f32[16,2,36,1296]{3,0,2,1:T(8,128)} %copy.18) | data formatting | bytes 11943936 | tf_op jit(solution)/shard_map/reshape | solution.py:155
  509.7 42.5 %slice_add_fusion = f32[16,2,32,36,36]{4,3,0,2,1:T(8,128)} fusion(f32[16,2,36,36,36]{4,3,0,2,1:T(8,128)} %reshape.65), kind=kLoop, calls=%fused_computation.124 | loop fusion | flops 5308416 | bytes 31850496 | tf_op jit(solution)/shard_map/add | solution.py:111
  552.2 40.8 %slice_add_fusion.8 = f32[16,2,32,32,36]{4,3,0,2,1:T(8,128)} fusion(f32[16,2,32,36,36]{4,3,0,2,1:T(8,128)} %slice_add_fusion), kind=kLoop, calls=%fused_computation.133 | loop fusion | flops 4718592 | bytes 28311552 | tf_op jit(solution)/shard_map/add | solution.py:111
  593.0 42.8 %fusion.72 = f32[16,2,32,32,32]{4,3,0,2,1:T(8,128)} fusion(f32[16,2,32,32,36]{4,3,0,2,1:T(8,128)} %slice_add_fusion.8), kind=kLoop, calls=%fused_computation.129 | loop fusion | flops 5242880 | bytes 25165824 | tf_op jit(solution)/shard_map/div | solution.py:113
  635.8 13.7 %broadcast_in_dim_reshape.3 = f32[1,1,16,2,32,1024]{5,2,4,3,1,0:T(8,128)} reshape(f32[16,2,32,32,32]{4,3,0,2,1:T(8,128)} %fusion.72) | data formatting | bytes 8388608 | tf_op jit(solution)/shard_map/broadcast_in_dim;reshape | solution.py:159
  649.5 6.6 %copy.19 = f32[1,1,16,2,32,1024]{5,4,3,2,1,0:T(8,128)} copy(f32[1,1,16,2,32,1024]{5,2,4,3,1,0:T(8,128)} %broadcast_in_dim_reshape.3) | data formatting | bytes 8388608
  (204 shorter events, 122.7 us)
Async XLA Ops:
  0.6 24.8 %copy-start = (f32[32,96,128]{2,1,0:T(8,128)S(1)}, f32[32,96,128]{2,1,0:T(8,128)}, u32[]{:S(2)}) copy-start(f32[32,96,128]{2,1,0:T(8,128)} %param.13) | copy-start | bytes 4718596
  0.6 24.8 %copy-start.1 = (f32[32,96,128]{2,1,0:T(8,128)S(1)}, f32[32,96,128]{2,1,0:T(8,128)}, u32[]{:S(2)}) copy-start(f32[32,96,128]{2,1,0:T(8,128)} %param.11) | copy-start | bytes 4718596
  3.4 22.0 %collective-permute-start = (f32[5,3,96,128]{3,2,1,0:T(8,128)}, f32[5,3,96,128]{3,2,1,0:T(8,128)}, u32[]{:S(2)}, u32[]{:S(2)}) collective-permute-start(f32[5,3,96,128]{3,2,1,0:T(8,128)} %get-tuple-element.389), channel_id=1, source_target_pairs={{0,8},{8,16},{16,24},{24,32},{32,40},{40,48},{48,56},{56,64},{64,7... | collective-permute-start | bytes 2211848 | tf_op jit(solution)/shard_map/ppermute | solution.py:23
  4.9 20.5 %collective-permute-start.1 = (f32[5,3,96,128]{3,2,1,0:T(8,128)}, f32[5,3,96,128]{3,2,1,0:T(8,128)}, u32[]{:S(2)}, u32[]{:S(2)}) collective-permute-start(f32[5,3,96,128]{3,2,1,0:T(8,128)} %get-tuple-element.390), channel_id=1, source_target_pairs={{8,0},{16,8},{24,16},{32,24},{40,32},{48,40},{56,48},{64,56},{72,6... | collective-permute-start | bytes 2211848 | tf_op jit(solution)/shard_map/ppermute | solution.py:24
  36.9 86.3 %copy-start.11 = (s32[1,1,12,1]{2,3,1,0:T(1,128)S(1)}, s32[1,1,12,1]{2,3,1,0:T(1,128)}, u32[]{:S(2)}) copy-start(s32[1,1,12,1]{2,3,1,0:T(1,128)} %param.15) | copy-start | bytes 148
  121.5 6.5 collective-permute-start.2
  121.5 6.5 collective-permute-start.3
  224.1 84.9 %copy-start.6 = (f32[32,96,128]{2,1,0:T(8,128)S(1)}, f32[32,96,128]{2,1,0:T(8,128)}, u32[]{:S(2)}) copy-start(f32[32,96,128]{2,1,0:T(8,128)} %param.14) | copy-start | bytes 4718596
  308.9 8.6 %copy-start.12 = (s32[1,1,12,1]{2,3,1,0:T(1,128)S(1)}, s32[1,1,12,1]{2,3,1,0:T(1,128)}, u32[]{:S(2)}) copy-start(s32[1,1,12,1]{2,3,1,0:T(1,128)} %param.15) | copy-start | bytes 148
  311.8 8.0 %collective-permute-start.4 = (f32[2,96,128]{2,1,0:T(8,128)S(1)}, f32[2,96,128]{2,1,0:T(8,128)S(1)}, u32[]{:S(2)}, u32[]{:S(2)}) collective-permute-start(f32[2,96,128]{2,1,0:T(8,128)S(1)} %get-tuple-element.407), channel_id=1, source_target_pairs={{0,8},{8,16},{16,24},{24,32},{32,40},{40,48},{48,56},{56,64},{64,7... | collective-permute-start | bytes 294920 | tf_op jit(solution)/shard_map/ppermute | solution.py:23
  311.8 8.1 %collective-permute-start.5 = (f32[2,96,128]{2,1,0:T(8,128)S(1)}, f32[2,96,128]{2,1,0:T(8,128)S(1)}, u32[]{:S(2)}, u32[]{:S(2)}) collective-permute-start(f32[2,96,128]{2,1,0:T(8,128)S(1)} %get-tuple-element.408), channel_id=1, source_target_pairs={{8,0},{16,8},{24,16},{32,24},{40,32},{48,40},{56,48},{64,56},{72,6... | collective-permute-start | bytes 294920 | tf_op jit(solution)/shard_map/ppermute | solution.py:24
  319.8 6.6 copy-start.2
  319.9 6.4 copy-start.4
  319.9 3.4 collective-permute-start.6
  320.9 5.4 collective-permute-start.7
  326.3 0.6 copy-start.8
  327.1 0.9 copy-start.3
  327.1 0.9 copy-start.5
  327.1 0.9 copy-start.9
  347.7 10.2 %copy-start.7 = (f32[1,36,1296]{2,0,1:T(1,128)S(1)}, f32[1,36,1296]{2,0,1:T(1,128)}, u32[]{:S(2)}) copy-start(f32[1,36,1296]{2,0,1:T(1,128)} %stack_reshape.38) | copy-start | bytes 559876
  355.4 12.1 %copy-start.10 = (pred[16,12]{1,0:T(8,128)(4,1)S(1)}, pred[16,12]{1,0:T(8,128)(4,1)}, u32[]{:S(2)}) copy-start(pred[16,12]{1,0:T(8,128)(4,1)} %iota_compare_fusion.1) | copy-start | bytes 580
  382.7 104.2 %all-to-all-start = ((f32[16,2,36,1296]{3,1,2,0:T(2,128)}), f32[16,2,36,1296]{3,1,2,0:T(2,128)}, u32[]{:S(2)}, u32[]{:S(2)}) async-start(f32[16,2,36,1296]{3,1,2,0:T(2,128)} %copy.17), calls=%async_computation | async-start | bytes 12976128 | tf_op jit(solution)/shard_map/all_to_all | solution.py:154
where the time goes:
time: 669 us; the launch traced here: 657 us
  other arithmetic  390 us (58%)
  local copies, waits for them, and re-layouts  124 us (19%)
  waiting for transfers between devices  114 us (17%)
  starting transfers between devices  22.1 us (3%)
    all_to_all x1, waiting for transfers between devices, body(): lax.all_to_all(send_buffer, 'box', split_axis=0, concat_axis=0, tiled=True)  89.3 us
    min x20, other arithmetic, sweep_line(): jnp.minimum(jnp.maximum(interface, jnp.minimum(cell_here, cell_next)), jn...  87.5 us
    add x2, other arithmetic, box_filter(): summed = summed + cut_along(result, shift_by, extent, filter_axis)  83.3 us
    dynamic_update_slice x20, other arithmetic, one_block(): return lax.dynamic_update_slice_in_dim(result, swept, offset, block_axis)  57.4 us
    add x20, other arithmetic, sweep_line(): centre + jnp.clip(dev_right, -2.0 * jnp.abs(dev_left), 2.0 * jnp.abs(dev_...  44.8 us
    div x1, other arithmetic, box_filter(): return result / float((2 * radius + 1) ** 3)  42.8 us
    another operation x13, local copies, waits for them, and re-layouts, body(): box_cells = jnp.stack(windows)  33.3 us
    ppermute x4, waiting for transfers between devices, with_halo(): before = lax.ppermute(last, axis, up)  24.5 us
  transfers between devices with their start and end apart: 9, of which 6 were waited for; matrix products, arithmetic and copies ran while one was open for 2% of the time, Pallas kernels for 0%

commit v1 on v0

v1 whole, which is shorter than its diff:
```python
import functools
import math

import jax
import jax.numpy as jnp
from jax import lax
from jax.experimental import pallas as pl
from jax.experimental.pallas import tpu as pltpu
from jax.sharding import PartitionSpec as P

BOX = 32
BOX_Y = 3
BOX_Z = 4
NX = 32
NY = 96
NZ = 128
FRAME = 112
GROUP = 16
STEP = 0.03
SCALES = (1.0, STEP, STEP, STEP, 2.0 * STEP * STEP)
UNSCALES = (1.0, 1.0 / STEP, 1.0 / STEP, 1.0 / STEP, 1.0 / (2.0 * STEP * STEP))
SOUND = math.sqrt(5.0 / 3.0)
TINY = 1e-30
VMEM_LIMIT = 56 * 1024 * 1024


def limit(value, other):
    bound = jnp.abs(other + other)
    return jnp.maximum(jnp.minimum(value, bound), -bound)


def deviation(d_prev, d_here, d_next):
    value = 0.5 * d_here + (d_prev - d_next) * (1.0 / 12.0)
    return jnp.minimum(jnp.maximum(value, jnp.minimum(d_here, 0.0)), jnp.maximum(d_here, 0.0))


def invert(x):
    return 1.0 / x


def state_of(u, normal):
    inverse = invert(u[0])
    squares = u[1] * u[1] + u[2] * u[2] + u[3] * u[3]
    pressure = u[4] - squares * inverse
    third = pressure * (1.0 / 3.0)
    velocity = u[normal] * inverse
    ratio = jnp.maximum(third * inverse, TINY)
    reach = jnp.abs(velocity) + SOUND * (ratio * lax.rsqrt(ratio))
    return velocity, third, reach


def flux(left, right, normal):
    v_left, p_left, reach_left = state_of(left, normal)
    v_right, p_right, reach_right = state_of(right, normal)
    reach = jnp.maximum(reach_left, reach_right)
    up = v_left + reach
    down = v_right - reach
    out = [left[f] * up + right[f] * down for f in range(5)]
    out[normal] = out[normal] + (p_left + p_right)
    work = p_left * v_left + p_right * v_right
    out[4] = out[4] + (work + work)
    return out


class Line:
    def __init__(self, normal):
        self.normal = normal
        self.q = []
        self.d = []
        self.dl = None
        self.er = None
        self.flux = None

    def load(self, q, carry):
        self.q = list(q)
        self.d = [carry[0:5], carry[5:10]]
        self.dl = carry[10:15]
        self.er = carry[15:20]
        self.flux = carry[20:25]

    def carry(self):
        return tuple(self.d[0]) + tuple(self.d[1]) + tuple(self.dl) + tuple(self.er) + tuple(self.flux)

    def push(self, new):
        q, d = self.q, self.d
        out = None
        if q:
            d0 = [a - b for a, b in zip(new, q[-1])]
            if len(d) >= 2:
                d2, d1 = d[-2], d[-1]
                dr = [deviation(*t) for t in zip(d2, d1, d0)]
                if self.dl is not None:
                    here = q[-2]
                    right = [c + limit(r, l) for c, r, l in zip(here, dr, self.dl)]
                    if self.er is not None:
                        left = [c + limit(l, r) for c, r, l in zip(here, dr, self.dl)]
                        now = flux(self.er, left, self.normal)
                        if self.flux is not None:
                            out = [c - (a - b) for c, a, b in zip(q[-3], now, self.flux)]
                        self.flux = now
                    self.er = right
                self.dl = [r - s for r, s in zip(dr, d1)]
            d.append(d0)
            self.d = d[-2:]
        q.append(new)
        self.q = q[-3:]
        return out


def turn(x, shift):
    return pltpu.roll(x, shift % NZ, 1)


def sweep_lanes(q):
    d = [turn(x, -1) - x for x in q]
    dr = [deviation(turn(x, 1), x, turn(x, -1)) for x in d]
    dl = [turn(r - x, 1) for r, x in zip(dr, d)]
    right = [c + limit(r, l) for c, r, l in zip(q, dr, dl)]
    left = [turn(c + limit(l, r), -1) for c, r, l in zip(q, dr, dl)]
    now = flux(right, left, 3)
    return [c - (f - turn(f, 1)) for c, f in zip(q, now)]


def lane_sum(t):
    pair = t + turn(t, -1)
    return t + turn(pair, 2) + turn(pair, -1)


def x_sweep(q_ref, s_ref, segments):
    def tile(t, _):
        row = pl.multiple_of(t * 8, 8)
        for base, out_base, count in segments:
            line = Line(1)
            for i in range(count + 6):
                new = [q_ref[f, base + i, pl.ds(row, 8), :] * SCALES[f] if f else q_ref[f, base + i, pl.ds(row, 8), :]
                       for f in range(5)]
                out = line.push(new)
                if out is not None:
                    x = out_base + i - 6
                    for f in range(5):
                        s_ref[pl.ds((f * GROUP + x) * FRAME + row, 8), :] = out[f]
        return 0

    lax.fori_loop(0, FRAME // 8, tile, 0)


ROWS_STEP = 4


def yz_sweep(s_ref, dm_ref, o_ref, t_ref):
    def group(g, _):
        def at(f, row):
            return pl.ds((f * GROUP + g * 8) * FRAME + row, 8, stride=FRAME)

        def rows(row):
            return [s_ref[at(f, row), :] for f in range(5)]

        first = Line(2)
        for row in range(3, 9):
            first.push(rows(row))

        def some(b, carry):
            line = Line(2)
            base = 9 + b * ROWS_STEP
            line.load([rows(base - 3), rows(base - 2), rows(base - 1)], carry)
            ahead = [rows(base + r) for r in range(ROWS_STEP)]
            for r in range(ROWS_STEP):
                swept = line.push(ahead[r])
                final = sweep_lanes(swept)
                row = base + r - 3
                for f in range(5):
                    o_ref[at(f, row), :] = final[f] * UNSCALES[f] if f else final[f]
                total = final[0] + dm_ref[at(0, row), :]
                t_ref[at(0, row), :] = lane_sum(total)
            return line.carry()

        lax.fori_loop(0, 100 // ROWS_STEP, some, first.carry())
        return 0

    lax.fori_loop(0, GROUP // 8, group, 0)


def smooth(planes, dest_ref, x_ref, y_ref, send_ref, send_row):
    def x_tile(t, _):
        row = pl.multiple_of(t * 8, 8)
        values = [planes(p, row) for p in range(12)]
        pairs = [values[p] + values[p + 1] for p in range(11)]
        for p in range(8):
            x_ref[pl.ds(p * FRAME + row, 8), :] = pairs[p] + pairs[p + 2] + values[p + 4]
        return 0

    lax.fori_loop(0, FRAME // 8, x_tile, 0)

    def y_plane(p, _):
        for t in range(NY // 8):
            start = p * FRAME + 8 + 8 * t
            parts = [x_ref[pl.ds(start + k, 8), :] for k in range(-2, 3)]
            total = ((parts[0] + parts[1]) + (parts[3] + parts[4])) + parts[2]
            y_ref[pl.ds(p * NY + 8 * t, 8), :] = total * (1.0 / 125.0)
        return 0

    lax.fori_loop(0, 8, y_plane, 0)

    places = []
    dests = [dest_ref[k] for k in range(12)]
    for k in range(12):
        slot = jnp.int32(0)
        for other in range(k):
            slot = slot + (dests[other] == dests[k]).astype(jnp.int32)
        places.append(dests[k] * 2 + slot)

    quarter = lax.broadcasted_iota(jnp.int32, (8, NZ), 1) // BOX

    def pick(values):
        out = values[3]
        for b in range(3):
            out = jnp.where(quarter == b, values[b], out)
        return out

    for by in range(BOX_Y):
        for m in range(8):
            s = [y_ref[pl.ds(by * BOX + 4 * m + q, 8, stride=NY), :] for q in range(4)]
            moved = []
            for k in range(4):
                mixed = pick([s[(b + k) % 4] for b in range(4)])
                moved.append(turn(mixed, k * BOX) if k else mixed)
            for bz in range(4):
                out = pick([moved[(q - bz) % 4] for q in range(4)])
                send_ref[places[by * 4 + bz], pl.ds(send_row, 8), pl.ds(m * NZ, NZ)] = out


def clear(send_ref):
    def one(i, _):
        send_ref[i] = jnp.zeros(send_ref.shape[1:], jnp.float32)
        return 0

    lax.fori_loop(0, send_ref.shape[0], one, 0)


def fetch(copies):
    for c in copies:
        c.start()
    for c in copies:
        c.wait()


def load_copies(density, momentum, energy, sem, q_ref, own, place, count):
    mid = pl.ds(8, NY)
    src, dst = pl.ds(own, count), pl.ds(place, count)
    return [
        pltpu.make_async_copy(density.at[src], q_ref.at[0, dst, mid], sem),
        pltpu.make_async_copy(momentum.at[:, src], q_ref.at[pl.ds(1, 3), dst, mid], sem),
        pltpu.make_async_copy(energy.at[src], q_ref.at[4, dst, mid], sem),
    ]


def side_copies(before, after, sem, q_ref, own, place, count):
    src, dst = pl.ds(own, count), pl.ds(place, count)
    return [
        pltpu.make_async_copy(before.at[pl.ds(0, 5), src], q_ref.at[:, dst, pl.ds(0, 8)], sem),
        pltpu.make_async_copy(after.at[pl.ds(0, 5), src], q_ref.at[:, dst, pl.ds(104, 8)], sem),
    ]


def flat_rows(ref, count, rows):
    return ref.reshape(count, rows, NZ)


def dm_copies(dm, before, after, sem, dm_ref, own, place, count):
    src, dst = pl.ds(own, count), pl.ds(place, count)
    d3 = flat_rows(dm_ref, GROUP, FRAME)
    return [
        pltpu.make_async_copy(dm.at[src], d3.at[dst, pl.ds(8, NY)], sem),
        pltpu.make_async_copy(before.at[5, src], d3.at[dst, pl.ds(0, 8)], sem),
        pltpu.make_async_copy(after.at[5, src], d3.at[dst, pl.ds(104, 8)], sem),
    ]


def out_copies(o_ref, outs, sem, own, place, count):
    o4 = o_ref.reshape(5, GROUP, FRAME, NZ)
    src, dst, mid = pl.ds(place, count), pl.ds(own, count), pl.ds(8, NY)
    density, momentum, energy = outs
    return [
        pltpu.make_async_copy(o4.at[0, src, mid], density.at[dst], sem),
        pltpu.make_async_copy(o4.at[pl.ds(1, 3), src, mid], momentum.at[:, dst], sem),
        pltpu.make_async_copy(o4.at[4, src, mid], energy.at[dst], sem),
    ]


def inner_kernel(dest, density, momentum, energy, dm, y_before, y_after,
                 out_density, out_momentum, out_energy, out_sums, send,
                 q_ref, s_ref, o_ref, dm_ref, t_ref, x_ref, y_ref, sem, out_sem):
    fetch(load_copies(density, momentum, energy, sem, q_ref, 1, 0, 22)
          + side_copies(y_before, y_after, sem, q_ref, 1, 0, 22)
          + dm_copies(dm, y_before, y_after, sem, dm_ref, 4, 0, 16))
    x_sweep(q_ref, s_ref, ((0, 0, 16),))
    yz_sweep(s_ref, dm_ref, o_ref, t_ref)
    t3 = flat_rows(t_ref, GROUP, FRAME)
    leaving = out_copies(o_ref, (out_density, out_momentum, out_energy), out_sem, 4, 0, 16)
    leaving.append(pltpu.make_async_copy(t3, out_sums, out_sem))
    for c in leaving:
        c.start()
    clear(send)
    smooth(lambda p, row: t_ref[pl.ds((2 + p) * FRAME + row, 8), :], dest, x_ref, y_ref, send, 0)
    for c in leaving:
        c.wait()


def outer_kernel(density, momentum, energy, dm, y_before, y_after, x_before, x_after, c_before, c_after,
                 in_density, in_momentum, in_energy,
                 out_density, out_momentum, out_energy, out_sums, to_next, to_prev,
                 q_ref, s_ref, o_ref, dm_ref, t_ref, sem, out_sem):
    mid = pl.ds(8, NY)
    copies = (load_copies(density, momentum, energy, sem, q_ref, 17, 0, 15)
              + load_copies(density, momentum, energy, sem, q_ref, 0, 21, 7)
              + side_copies(y_before, y_after, sem, q_ref, 17, 0, 15)
              + side_copies(y_before, y_after, sem, q_ref, 0, 21, 7)
              + side_copies(c_before, c_after, sem, q_ref, 0, 15, 6)
              + dm_copies(dm, y_before, y_after, sem, dm_ref, 20, 0, 12)
              + dm_copies(dm, y_before, y_after, sem, dm_ref, 0, 12, 4))
    copies.append(pltpu.make_async_copy(x_after, q_ref.at[:, pl.ds(15, 3), mid], sem))
    copies.append(pltpu.make_async_copy(x_before, q_ref.at[:, pl.ds(18, 3), mid], sem))
    fetch(copies)
    x_sweep(q_ref, s_ref, ((0, 0, 12), (18, 12, 4)))
    yz_sweep(s_ref, dm_ref, o_ref, t_ref)
    t3 = flat_rows(t_ref, GROUP, FRAME)
    outs = (out_density, out_momentum, out_energy)
    leaving = out_copies(o_ref, outs, out_sem, 20, 0, 12) + out_copies(o_ref, outs, out_sem, 0, 12, 4)
    leaving.append(pltpu.make_async_copy(t3, out_sums, out_sem))
    leaving.append(pltpu.make_async_copy(t3.at[pl.ds(10, 2)], to_next, out_sem))
    leaving.append(pltpu.make_async_copy(t3.at[pl.ds(12, 2)], to_prev, out_sem))
    fetch(leaving)


def rest_kernel(dest, sums_inner, sums_outer, from_prev, from_next, send, w_ref, x_ref, y_ref, sem):
    def part(src, own, place, count):
        return pltpu.make_async_copy(src.at[pl.ds(own, count)], w_ref.at[pl.ds(place, count)], sem)

    copies = [
        part(from_prev, 0, 0, 2),
        part(sums_outer, 12, 2, 4),
        part(sums_inner, 0, 6, 6),
        part(sums_inner, 10, 12, 6),
        part(sums_outer, 0, 18, 12),
        part(from_next, 0, 30, 2),
    ]
    for c in copies:
        c.start()
    clear(send)
    for c in copies:
        c.wait()
    for row, base in ((0, 0), (8, 12), (16, 20)):
        smooth(lambda p, r: w_ref[base + p, pl.ds(r, 8), :], dest, x_ref, y_ref, send, row)


ANY = pl.BlockSpec(memory_space=pl.ANY)
SMEM = pl.BlockSpec(memory_space=pltpu.SMEM)
VMEM = pl.BlockSpec(memory_space=pltpu.VMEM)
F32 = jnp.float32


def shape(*dims):
    return jax.ShapeDtypeStruct(dims, F32)


def params():
    return pltpu.CompilerParams(vmem_limit_bytes=VMEM_LIMIT)


def main_scratch(planes):
    rows = GROUP * FRAME
    return [
        pltpu.VMEM((5, planes, FRAME, NZ), F32),
        pltpu.VMEM((5 * rows, NZ), F32),
        pltpu.VMEM((5 * rows, NZ), F32),
        pltpu.VMEM((rows, NZ), F32),
        pltpu.VMEM((rows, NZ), F32),
    ]


def smooth_scratch():
    return [pltpu.VMEM((8 * FRAME, NZ), F32), pltpu.VMEM((8 * NY, NZ), F32)]


FIELD_SHAPES = (shape(NX, NY, NZ), shape(3, NX, NY, NZ), shape(NX, NY, NZ))


def shifted(value, axis, by):
    size = lax.axis_size(axis)
    return lax.ppermute(value, axis, [(i, (i + by) % size) for i in range(size)])


def body(density, momentum, energy, dm_density, box_dest):
    dest = box_dest[0, 0, :, 0]
    fields = (density[None], momentum, energy[None])

    def cut(arrays, planes, rows):
        return jnp.concatenate([a[:, planes[0]:planes[1], rows[0]:rows[1]] for a in arrays], axis=0)

    y_before = shifted(cut(fields + (dm_density[None],), (0, NX), (NY - 8, NY)), "grp", 1)
    y_after = shifted(cut(fields + (dm_density[None],), (0, NX), (0, 8)), "grp", -1)
    x_before = shifted(cut(fields, (NX - 3, NX), (0, NY)), "box", 1)
    x_after = shifted(cut(fields, (0, 3), (0, NY)), "box", -1)

    inner = pl.pallas_call(
        inner_kernel,
        out_shape=FIELD_SHAPES + (shape(GROUP, FRAME, NZ), shape(32, 8, 1024)),
        in_specs=[SMEM] + [ANY] * 6,
        out_specs=[ANY] * 4 + [VMEM],
        scratch_shapes=main_scratch(22) + smooth_scratch() + [pltpu.SemaphoreType.DMA, pltpu.SemaphoreType.DMA],
        compiler_params=params(),
        name="inner",
    )(dest, density, momentum, energy, dm_density, y_before, y_after)
    new_density, new_momentum, new_energy, sums_inner, send_inner = inner
    got_inner = lax.all_to_all(send_inner.reshape(16, 2, 8, 1024), "box", split_axis=0, concat_axis=0, tiled=True)

    x_both = jnp.concatenate([x_after, x_before], axis=1)
    c_before = shifted(x_both[:, :, NY - 8:], "grp", 1)
    c_after = shifted(x_both[:, :, :8], "grp", -1)
    outer = pl.pallas_call(
        outer_kernel,
        out_shape=FIELD_SHAPES + (shape(GROUP, FRAME, NZ), shape(2, FRAME, NZ), shape(2, FRAME, NZ)),
        in_specs=[ANY] * 13,
        out_specs=[ANY] * 6,
        scratch_shapes=main_scratch(28) + [pltpu.SemaphoreType.DMA, pltpu.SemaphoreType.DMA],
        input_output_aliases={10: 0, 11: 1, 12: 2},
        compiler_params=params(),
        name="outer",
    )(density, momentum, energy, dm_density, y_before, y_after, x_before, x_after, c_before, c_after,
      new_density, new_momentum, new_energy)
    new_density, new_momentum, new_energy, sums_outer, to_next, to_prev = outer
    from_prev = shifted(to_next, "box", 1)
    from_next = shifted(to_prev, "box", -1)
    send_rest = pl.pallas_call(
        rest_kernel,
        out_shape=shape(32, 24, 1024),
        in_specs=[SMEM] + [ANY] * 4,
        out_specs=VMEM,
        scratch_shapes=[pltpu.VMEM((32, FRAME, NZ), F32)] + smooth_scratch() + [pltpu.SemaphoreType.DMA],
        compiler_params=params(),
        name="rest",
    )(dest, sums_inner, sums_outer, from_prev, from_next)
    got_rest = lax.all_to_all(send_rest.reshape(16, 2, 24, 1024), "box", split_axis=0, concat_axis=0, tiled=True)
    kd = jnp.concatenate([got_rest[:, :, :8], got_inner, got_rest[:, :, 8:]], axis=2)
    return (new_density, new_momentum, new_energy, kd[None, None])


def solution(mesh):
    in_specs = (
        P("box", "grp", None),
        P(None, "box", "grp", None),
        P("box", "grp", None),
        P("box", "grp", None),
        P("grp", "box", None, None),
    )
    out_specs = (
        P("box", "grp", None),
        P(None, "box", "grp", None),
        P("box", "grp", None),
        P("grp", "box", None, None, None, None),
    )
    return jax.shard_map(body, mesh=mesh, in_specs=in_specs, out_specs=out_specs, check_vma=False)
```

time: 669 us -> 210 us (0.31); the launches traced: 657 us -> 210 us
  other arithmetic: 390 us -> 4.98 us
  local copies, waits for them, and re-layouts: 124 us -> 11 us
  Pallas kernels: 0 us -> 99.1 us
  waiting for transfers between devices: 114 us -> 28.6 us
  blocking collectives: 0 us -> 47.2 us
    add x23 -> x0, other arithmetic: 131 us -> none  [the longest x2 83.3 us: box_filter(): summed = summed + cut_along(result, shift_by, extent, filter_axis)]
    pallas_call x0 -> x3, Pallas kernels: none -> 99.1 us  [the longest x1 47.1 us: body(): pl.pallas_call(inner_kernel, out_shape=FIELD_SHAPES + (shape(GROUP, FRAME...]
    min x20 -> x0, other arithmetic: 87.5 us -> none  [sweep_line(): jnp.minimum(jnp.maximum(interface, jnp.minimum(cell_here, cell_next)), jn...]
    all_to_all x1, waiting for transfers between devices: 89.3 us -> 14.2 us  [body(): lax.all_to_all(send_inner.reshape(16, 2, 8, 1024), 'box', split_axis=0, c...]
    another operation x69 -> x0, local copies, waits for them, and re-layouts: 60.5 us -> none  [the longest x13 33.3 us: body(): box_cells = jnp.stack(windows)]
    dynamic_update_slice x20 -> x0, other arithmetic: 57.4 us -> none  [one_block(): return lax.dynamic_update_slice_in_dim(result, swept, offset, block_axis)]
    all_to_all x0 -> x1, blocking collectives: none -> 47.2 us  [body(): lax.all_to_all(send_rest.reshape(16, 2, 24, 1024), 'box', split_axis=0, c...]
    div x1 -> x0, other arithmetic: 42.8 us -> none  [box_filter(): return result / float((2 * radius + 1) ** 3)]
  transfers between devices with their start and end apart: 9 -> 9, of which waited for: 6 -> 4; matrix products, arithmetic and copies ran while one was open for 2% -> 3% of each run, Pallas kernels for 0% -> 22%
where the time goes in v1:
time: 210 us
  Pallas kernels  99.1 us (47%)
  blocking collectives  47.2 us (22%)
  waiting for transfers between devices  28.6 us (14%)
  starting transfers between devices  18 us (9%)
  local copies, waits for them, and re-layouts  11 us (5%)
  other arithmetic  4.98 us (2%)
    all_to_all x1, blocking collectives, body(): lax.all_to_all(send_rest.reshape(16, 2, 24, 1024), 'box', split_axis=0, c...  47.2 us
    pallas_call x1, Pallas kernels, body(): pl.pallas_call(inner_kernel, out_shape=FIELD_SHAPES + (shape(GROUP, FRAME...  47.1 us
    pallas_call x1, Pallas kernels, body(): pl.pallas_call(outer_kernel, out_shape=FIELD_SHAPES + (shape(GROUP, FRAME...  46.5 us
    ppermute x8, waiting for transfers between devices, shifted(): lax.ppermute(value, axis, [(i, (i + by) % size) for i in range(size)])  14.3 us
    all_to_all x1, waiting for transfers between devices, body(): lax.all_to_all(send_inner.reshape(16, 2, 8, 1024), 'box', split_axis=0, c...  14.2 us
    ppermute x8, starting transfers between devices, shifted(): lax.ppermute(value, axis, [(i, (i + by) % size) for i in range(size)])  13.6 us
    slice x5, local copies, waits for them, and re-layouts, cut(): a[:, planes[0]:planes[1], rows[0]:rows[1]]  5.68 us
    pallas_call x1, Pallas kernels, body(): pl.pallas_call(rest_kernel, out_shape=shape(32, 24, 1024), in_specs=[SMEM...  5.57 us
  transfers between devices with their start and end apart: 9, of which 4 were waited for; matrix products, arithmetic and copies ran while one was open for 3% of the time, Pallas kernels for 22%

profile of v1, /device:TPU:32, one launch (start us, length us, event | category | flops | bytes accessed | tf_op | source)
XLA Modules:
  0.0 209.6 jit_solution(12267994747797018469)
XLA Ops:
  0.6 1.2 fusion
  1.8 1.2 fusion.2
  3.0 0.1 pad_maximum_fusion.2
  3.1 1.6 collective-permute-start.2
  4.7 3.9 %collective-permute-start.3 = (f32[5,3,96,128]{3,2,1,0:T(8,128)S(1)}, f32[5,3,96,128]{3,2,1,0:T(8,128)S(1)}, u32[]{:S(2)}, u32[]{:S(2)}) collective-permute-start(f32[5,3,96,128]{3,2,1,0:T(8,128)S(1)} %pad_maximum_fusion.3), channel_id=1, source_target_pairs={{0,120},{8,0},{16,8},{24,16},{32,24},{40,32},{48,40},{56,48},{64,5... | collective-permute-start | bytes 2211848 | tf_op jit(solution)/shard_map/ppermute | solution.py:390
  8.6 1.2 fusion.1
  9.8 1.1 fusion.4
  10.9 1.0 fusion.6
  11.9 0.1 pad_maximum_fusion
  12.0 0.0 collective-permute-start
  12.0 0.1 pad_maximum_fusion.1
  12.1 1.7 collective-permute-start.1
  13.8 10.4 %collective-permute-done.3.x_after = f32[5,3,96,128]{3,2,1,0:T(8,128)S(1)} collective-permute-done((f32[5,3,96,128]{3,2,1,0:T(8,128)S(1)}, f32[5,3,96,128]{3,2,1,0:T(8,128)S(1)}, u32[]{:S(2)}, u32[]{:S(2)}) %collective-permute-start.3) | collective-permute-done | bytes 737312 | tf_op jit(solution)/shard_map/ppermute | solution.py:390
  24.2 0.0 copy-start.3
  24.3 0.5 collective-permute-done.2.x_before
  24.8 0.0 copy-start.2
  24.8 0.1 constant_dynamic-update-slice_fusion
  24.9 0.2 copy-done.3
  25.1 0.0 collective-permute-start.5
  25.1 0.5 collective-permute-start.4
  25.6 0.0 collective-permute-done.y_before
  25.6 0.0 copy-start
  25.6 0.0 collective-permute-done.1.y_after
  25.6 0.0 copy-start.1
  25.7 0.9 copy-done
  26.5 0.3 copy-done.1
  26.8 47.1 %inner.1 = (f32[32,96,128]{2,1,0:T(8,128)}, f32[3,32,96,128]{3,2,1,0:T(8,128)}, f32[32,96,128]{2,1,0:T(8,128)}, f32[16,112,128]{2,1,0:T(8,128)}, f32[32,8,1024]{2,1,0:T(8,128)}) custom-call(s32[12]{0:T(128)} %bitcast.15, f32[32,96,128]{2,1,0:T(8,128)} %density.3, f32[3,32,96,128]{3,2,1,0:T(8,128)} %momentum.3, f32[32,96,128]{2,1,0:T(8,128)} %energy.3, ...), custom_call_target="tpu_custom_call" | custom-call | tf_op jit(solution)/shard_map/inner/pallas_call | solution.py:405
  73.9 0.0 copy-done.2
  73.9 0.0 collective-permute-done.5.c_after
  74.0 0.0 copy-start.4
  74.0 0.0 collective-permute-done.4.c_before
  74.0 0.0 copy-start.5
  74.0 0.6 copy-done.4
  74.6 0.0 copy-done.5
  74.6 46.5 %outer.1 = (f32[32,96,128]{2,1,0:T(8,128)}, f32[3,32,96,128]{3,2,1,0:T(8,128)}, f32[32,96,128]{2,1,0:T(8,128)}, f32[16,112,128]{2,1,0:T(8,128)}, f32[2,112,128]{2,1,0:T(8,128)}, /*index=5*/f32[2,112,128]{2,1,0:T(8,128)}) custom-call(f32[32,96,128]{2,1,0:T(8,128)} %density.3, ...), custom_call_target="tpu_custom_call", output_to_operand_aliasing={{0}: (10, {}), {1}: (11, {}), {2}: (12, {})} | custom-call | tf_op jit(solution)/shard_map/outer/pallas_call | solution.py:420
  121.1 0.1 collective-permute-start.6
  121.2 5.8 %collective-permute-start.7 = (f32[2,112,128]{2,1,0:T(8,128)}, f32[2,112,128]{2,1,0:T(8,128)S(1)}, u32[]{:S(2)}, u32[]{:S(2)}) collective-permute-start(f32[2,112,128]{2,1,0:T(8,128)} %get-tuple-element.24), channel_id=1, source_target_pairs={{0,120},{8,0},{16,8},{24,16},{32,24},{40,32},{48,40},{56,48},{64,5... | collective-permute-start | bytes 344072 | tf_op jit(solution)/shard_map/ppermute | solution.py:390
  127.0 3.3 %collective-permute-done.6.from_prev = f32[2,112,128]{2,1,0:T(8,128)S(1)} collective-permute-done((f32[2,112,128]{2,1,0:T(8,128)}, f32[2,112,128]{2,1,0:T(8,128)S(1)}, u32[]{:S(2)}, u32[]{:S(2)}) %collective-permute-start.6) | collective-permute-done | bytes 114720 | tf_op jit(solution)/shard_map/ppermute | solution.py:390
  130.3 0.0 copy-start.6
  130.3 0.0 collective-permute-done.7.from_next
  130.4 0.0 copy-start.7
  130.4 0.6 copy-done.6
  131.0 0.0 copy-done.7
  131.0 5.6 %rest.1 = f32[32,24,1024]{2,1,0:T(8,128)} custom-call(s32[12]{0:T(128)} %bitcast.16, f32[16,112,128]{2,1,0:T(8,128)} %get-tuple-element.21.sums_inner, f32[16,112,128]{2,1,0:T(8,128)} %get-tuple-element.22.sums_outer, f32[2,112,128]{2,1,0:T(8,128)} %copy-done.6, f32[2,112,128]{2,1,0:T(8,128)} %copy-done.7), custom_call_target="tpu_custom_call" | custom-call | tf_op jit(solution)/shard_map/rest/pallas_call | solution.py:434
  136.6 47.2 %all_to_all.10 = f32[16,2,24,1024]{3,2,1,0:T(8,128)S(1)} all-to-all(f32[16,2,24,1024]{3,2,1,0:T(8,128)} %bitcast.8), channel_id=1, replica_groups=mesh['box'=16,'grp'=8] {'box'}, dimensions={0} | all-to-all | bytes 6291456 | tf_op jit(solution)/shard_map/all_to_all | solution.py:443
  183.8 4.3 %all-to-all-start.1 = ((f32[16,2,8,1024]{3,2,1,0:T(8,128)}), f32[16,2,8,1024]{3,2,1,0:T(8,128)}, u32[]{:S(2)}, u32[]{:S(2)}) async-start(f32[16,2,8,1024]{3,2,1,0:T(8,128)} %bitcast.14), calls=%async_computation.1 | async-start | bytes 2097152 | tf_op jit(solution)/shard_map/all_to_all | solution.py:415
  188.1 1.1 slice.84
  189.2 1.5 slice.85
  190.7 14.2 %all-to-all-done.1 = f32[16,2,8,1024]{3,2,1,0:T(8,128)} async-done(((f32[16,2,8,1024]{3,2,1,0:T(8,128)}), f32[16,2,8,1024]{3,2,1,0:T(8,128)}, u32[]{:S(2)}, u32[]{:S(2)}) %all-to-all-start.1) | async-done | bytes 1048608 | tf_op jit(solution)/shard_map/all_to_all | solution.py:415
  204.9 4.8 %maximum_bitcast_fusion = f32[1,1,16,2,32,1024]{5,4,3,2,1,0:T(8,128)} fusion(f32[16,2,16,1024]{3,2,1,0:T(8,128)} %slice.85, f32[16,2,8,1024]{3,2,1,0:T(8,128)} %all-to-all-done.1, f32[16,2,8,1024]{3,2,1,0:T(8,128)} %slice.84), kind=kLoop, calls=%fused_computation | loop fusion | flops 2097152 | bytes 8388608 | tf_op jit(solution)/shard_map/broadcast_in_dim | solution.py:445
  (3 shorter events, 0.1 us)
Async XLA Ops:
  3.1 21.8 %collective-permute-start.2 = (f32[5,3,96,128]{3,2,1,0:T(8,128)S(1)}, f32[5,3,96,128]{3,2,1,0:T(8,128)S(1)}, u32[]{:S(2)}, u32[]{:S(2)}) collective-permute-start(f32[5,3,96,128]{3,2,1,0:T(8,128)S(1)} %pad_maximum_fusion.2), channel_id=1, source_target_pairs={{0,8},{8,16},{16,24},{24,32},{32,40},{40,48},{48,56},{56,64},{64,7... | collective-permute-start | bytes 2211848 | tf_op jit(solution)/shard_map/ppermute | solution.py:390
  4.7 19.6 %collective-permute-start.3 = (f32[5,3,96,128]{3,2,1,0:T(8,128)S(1)}, f32[5,3,96,128]{3,2,1,0:T(8,128)S(1)}, u32[]{:S(2)}, u32[]{:S(2)}) collective-permute-start(f32[5,3,96,128]{3,2,1,0:T(8,128)S(1)} %pad_maximum_fusion.3), channel_id=1, source_target_pairs={{0,120},{8,0},{16,8},{24,16},{32,24},{40,32},{48,40},{56,48},{64,5... | collective-permute-start | bytes 2211848 | tf_op jit(solution)/shard_map/ppermute | solution.py:390
  12.0 13.7 %collective-permute-start = (f32[6,32,8,128]{3,2,1,0:T(8,128)S(1)}, f32[6,32,8,128]{3,2,1,0:T(8,128)S(1)}, u32[]{:S(2)}, u32[]{:S(2)}) collective-permute-start(f32[6,32,8,128]{3,2,1,0:T(8,128)S(1)} %pad_maximum_fusion), channel_id=1, source_target_pairs={{0,1},{1,2},{2,3},{3,4},{4,5},{5,6},{6,7},{7,0},{8,9},{9,10},{10,1... | collective-permute-start | bytes 2359304 | tf_op jit(solution)/shard_map/ppermute | solution.py:390
  12.1 13.6 %collective-permute-start.1 = (f32[6,32,8,128]{3,2,1,0:T(8,128)S(1)}, f32[6,32,8,128]{3,2,1,0:T(8,128)S(1)}, u32[]{:S(2)}, u32[]{:S(2)}) collective-permute-start(f32[6,32,8,128]{3,2,1,0:T(8,128)S(1)} %pad_maximum_fusion.1), channel_id=1, source_target_pairs={{0,7},{1,0},{2,1},{3,2},{4,3},{5,4},{6,5},{7,6},{8,15},{9,8},{10,9... | collective-permute-start | bytes 2359304 | tf_op jit(solution)/shard_map/ppermute | solution.py:390
  24.2 0.9 copy-start.3
  24.8 49.1 %copy-start.2 = (f32[5,3,96,128]{3,2,1,0:T(8,128)}, f32[5,3,96,128]{3,2,1,0:T(8,128)S(1)}, u32[]{:S(2)}) copy-start(f32[5,3,96,128]{3,2,1,0:T(8,128)S(1)} %collective-permute-done.2.x_before) | copy-start | bytes 2211844
  25.1 48.8 %collective-permute-start.5 = (f32[5,6,8,128]{3,2,1,0:T(8,128)S(1)}, f32[5,6,8,128]{3,2,1,0:T(8,128)S(1)}, u32[]{:S(2)}, u32[]{:S(2)}) collective-permute-start(f32[5,6,8,128]{3,2,1,0:T(8,128)S(1)} %get-tuple-element.40), channel_id=1, source_target_pairs={{0,7},{1,0},{2,1},{3,2},{4,3},{5,4},{6,5},{7,6},{8,15},{9,8},{10,9... | collective-permute-start | bytes 368648 | tf_op jit(solution)/shard_map/ppermute | solution.py:390
  25.1 48.8 %collective-permute-start.4 = (f32[5,6,8,128]{3,2,1,0:T(8,128)S(1)}, f32[5,6,8,128]{3,2,1,0:T(8,128)S(1)}, u32[]{:S(2)}, u32[]{:S(2)}) collective-permute-start(f32[5,6,8,128]{3,2,1,0:T(8,128)S(1)} %get-tuple-element.41), channel_id=1, source_target_pairs={{0,1},{1,2},{2,3},{3,4},{4,5},{5,6},{6,7},{7,0},{8,9},{9,10},{10,1... | collective-permute-start | bytes 368648 | tf_op jit(solution)/shard_map/ppermute | solution.py:390
  25.6 0.9 copy-start
  25.6 1.2 copy-start.1
  74.0 0.7 copy-start.4
  74.0 0.7 copy-start.5
  121.1 9.2 %collective-permute-start.6 = (f32[2,112,128]{2,1,0:T(8,128)}, f32[2,112,128]{2,1,0:T(8,128)S(1)}, u32[]{:S(2)}, u32[]{:S(2)}) collective-permute-start(f32[2,112,128]{2,1,0:T(8,128)} %get-tuple-element.23), channel_id=1, source_target_pairs={{0,8},{8,16},{16,24},{24,32},{32,40},{40,48},{48,56},{56,64},{64,7... | collective-permute-start | bytes 344072 | tf_op jit(solution)/shard_map/ppermute | solution.py:390
  121.2 9.2 %collective-permute-start.7 = (f32[2,112,128]{2,1,0:T(8,128)}, f32[2,112,128]{2,1,0:T(8,128)S(1)}, u32[]{:S(2)}, u32[]{:S(2)}) collective-permute-start(f32[2,112,128]{2,1,0:T(8,128)} %get-tuple-element.24), channel_id=1, source_target_pairs={{0,120},{8,0},{16,8},{24,16},{32,24},{40,32},{48,40},{56,48},{64,5... | collective-permute-start | bytes 344072 | tf_op jit(solution)/shard_map/ppermute | solution.py:390
  130.3 0.7 copy-start.6
  130.4 0.6 copy-start.7
  183.8 21.1 %all-to-all-start.1 = ((f32[16,2,8,1024]{3,2,1,0:T(8,128)}), f32[16,2,8,1024]{3,2,1,0:T(8,128)}, u32[]{:S(2)}, u32[]{:S(2)}) async-start(f32[16,2,8,1024]{3,2,1,0:T(8,128)} %bitcast.14), calls=%async_computation.1 | async-start | bytes 2097152 | tf_op jit(solution)/shard_map/all_to_all | solution.py:415

commit v2 on v1

--- a/solution.py
+++ b/solution.py
@@ -15,7 +15,8 @@
 NY = 96
 NZ = 128
 FRAME = 112
-GROUP = 16
+TILES = FRAME // 8
+STRIDE = 120
 STEP = 0.03
 SCALES = (1.0, STEP, STEP, STEP, 2.0 * STEP * STEP)
 UNSCALES = (1.0, 1.0 / STEP, 1.0 / STEP, 1.0 / STEP, 1.0 / (2.0 * STEP * STEP))
@@ -126,8 +127,9 @@
     return t + turn(pair, 2) + turn(pair, -1)
 
 
-def x_sweep(q_ref, s_ref, segments):
+def x_sweep(q_ref, s_ref, planes, segments, ready):
     def tile(t, _):
+        ready(t)
         row = pl.multiple_of(t * 8, 8)
         for base, out_base, count in segments:
             line = Line(1)
@@ -138,19 +140,19 @@
                 if out is not None:
                     x = out_base + i - 6
                     for f in range(5):
-                        s_ref[pl.ds((f * GROUP + x) * FRAME + row, 8), :] = out[f]
+                        s_ref[pl.ds((f * planes + x) * STRIDE + row, 8), :] = out[f]
         return 0
 
-    lax.fori_loop(0, FRAME // 8, tile, 0)
-
-
-ROWS_STEP = 4
-
-
-def yz_sweep(s_ref, dm_ref, o_ref, t_ref):
+    lax.fori_loop(0, TILES, tile, 0)
+
+
+ROWS_STEP = 10
+
+
+def yz_sweep(s_ref, dm_ref, o_ref, t_ref, planes, t_base):
     def group(g, _):
-        def at(f, row):
-            return pl.ds((f * GROUP + g * 8) * FRAME + row, 8, stride=FRAME)
+        def at(f, row, base=0):
+            return pl.ds((f * planes + g * 8 + base) * STRIDE + row, 8, stride=STRIDE)
 
         def rows(row):
             return [s_ref[at(f, row), :] for f in range(5)]
@@ -171,13 +173,13 @@
                 for f in range(5):
                     o_ref[at(f, row), :] = final[f] * UNSCALES[f] if f else final[f]
                 total = final[0] + dm_ref[at(0, row), :]
-                t_ref[at(0, row), :] = lane_sum(total)
+                t_ref[at(0, row, t_base), :] = lane_sum(total)
             return line.carry()
 
         lax.fori_loop(0, 100 // ROWS_STEP, some, first.carry())
         return 0
 
-    lax.fori_loop(0, GROUP // 8, group, 0)
+    lax.fori_loop(0, planes // 8, group, 0)
 
 
 def smooth(planes, dest_ref, x_ref, y_ref, send_ref, send_row):
@@ -189,7 +191,7 @@
             x_ref[pl.ds(p * FRAME + row, 8), :] = pairs[p] + pairs[p + 2] + values[p + 4]
         return 0
 
-    lax.fori_loop(0, FRAME // 8, x_tile, 0)
+    lax.fori_loop(0, TILES, x_tile, 0)
 
     def y_plane(p, _):
         for t in range(NY // 8):
@@ -237,38 +239,68 @@
     lax.fori_loop(0, send_ref.shape[0], one, 0)
 
 
-def fetch(copies):
-    for c in copies:
-        c.start()
-    for c in copies:
-        c.wait()
-
-
-def load_copies(density, momentum, energy, sem, q_ref, own, place, count):
-    mid = pl.ds(8, NY)
-    src, dst = pl.ds(own, count), pl.ds(place, count)
-    return [
-        pltpu.make_async_copy(density.at[src], q_ref.at[0, dst, mid], sem),
-        pltpu.make_async_copy(momentum.at[:, src], q_ref.at[pl.ds(1, 3), dst, mid], sem),
-        pltpu.make_async_copy(energy.at[src], q_ref.at[4, dst, mid], sem),
-    ]
-
-
-def side_copies(before, after, sem, q_ref, own, place, count):
-    src, dst = pl.ds(own, count), pl.ds(place, count)
-    return [
-        pltpu.make_async_copy(before.at[pl.ds(0, 5), src], q_ref.at[:, dst, pl.ds(0, 8)], sem),
-        pltpu.make_async_copy(after.at[pl.ds(0, 5), src], q_ref.at[:, dst, pl.ds(104, 8)], sem),
-    ]
-
-
-def flat_rows(ref, count, rows):
-    return ref.reshape(count, rows, NZ)
+def rows_of(t):
+    return pl.ds(pl.multiple_of(t * 8, 8), 8)
+
+
+class Tiles:
+    def __init__(self, q_ref, sems, parts):
+        self.q_ref, self.sems, self.parts = q_ref, sems, parts
+
+    def copies(self, t, kind):
+        out = []
+        for own, before, after, src, dst in self.parts:
+            q = self.q_ref.at[:, dst, rows_of(t)]
+            sem = self.sems.at[t]
+            if kind == "before":
+                out.append(pltpu.make_async_copy(before.at[pl.ds(0, 5), src], q, sem))
+            elif kind == "after":
+                out.append(pltpu.make_async_copy(after.at[pl.ds(0, 5), src], q, sem))
+            elif len(own) == 1:
+                out.append(pltpu.make_async_copy(own[0].at[:, src, rows_of(t - 1)], q, sem))
+            else:
+                density, momentum, energy = own
+                rows = rows_of(t - 1)
+                place = self.q_ref.at
+                out.append(pltpu.make_async_copy(density.at[src, rows], place[0, dst, rows_of(t)], sem))
+                out.append(pltpu.make_async_copy(momentum.at[:, src, rows], place[pl.ds(1, 3), dst, rows_of(t)], sem))
+                out.append(pltpu.make_async_copy(energy.at[src, rows], place[4, dst, rows_of(t)], sem))
+        return out
+
+    def each(self, t, act):
+        @pl.when(t == 0)
+        def _():
+            for c in self.copies(t, "before"):
+                act(c)
+
+        @pl.when(t == TILES - 1)
+        def _():
+            for c in self.copies(t, "after"):
+                act(c)
+
+        @pl.when((t > 0) & (t < TILES - 1))
+        def _():
+            for c in self.copies(t, "own"):
+                act(c)
+
+    def start(self):
+        def one(t, _):
+            self.each(t, lambda c: c.start())
+            return 0
+
+        lax.fori_loop(0, TILES, one, 0)
+
+    def wait(self, t):
+        self.each(t, lambda c: c.wait())
+
+
+def framed(ref):
+    return ref.reshape(ref.shape[0] // STRIDE, STRIDE, NZ)
 
 
 def dm_copies(dm, before, after, sem, dm_ref, own, place, count):
     src, dst = pl.ds(own, count), pl.ds(place, count)
-    d3 = flat_rows(dm_ref, GROUP, FRAME)
+    d3 = framed(dm_ref)
     return [
         pltpu.make_async_copy(dm.at[src], d3.at[dst, pl.ds(8, NY)], sem),
         pltpu.make_async_copy(before.at[5, src], d3.at[dst, pl.ds(0, 8)], sem),
@@ -276,8 +308,8 @@
     ]
 
 
-def out_copies(o_ref, outs, sem, own, place, count):
-    o4 = o_ref.reshape(5, GROUP, FRAME, NZ)
+def out_copies(o_ref, planes, outs, sem, own, place, count):
+    o4 = o_ref.reshape(5, planes, STRIDE, NZ)
     src, dst, mid = pl.ds(place, count), pl.ds(own, count), pl.ds(8, NY)
     density, momentum, energy = outs
     return [
@@ -287,69 +319,102 @@
     ]
 
 
+def start_all(copies):
+    for c in copies:
+        c.start()
+
+
+def wait_all(copies):
+    for c in copies:
+        c.wait()
+
+
+def sums_copy(t_ref, base, count, out, sem):
+    return pltpu.make_async_copy(framed(t_ref).at[pl.ds(base, count), pl.ds(0, FRAME)], out, sem)
+
+
 def inner_kernel(dest, density, momentum, energy, dm, y_before, y_after,
                  out_density, out_momentum, out_energy, out_sums, send,
-                 q_ref, s_ref, o_ref, dm_ref, t_ref, x_ref, y_ref, sem, out_sem):
-    fetch(load_copies(density, momentum, energy, sem, q_ref, 1, 0, 22)
-          + side_copies(y_before, y_after, sem, q_ref, 1, 0, 22)
-          + dm_copies(dm, y_before, y_after, sem, dm_ref, 4, 0, 16))
-    x_sweep(q_ref, s_ref, ((0, 0, 16),))
-    yz_sweep(s_ref, dm_ref, o_ref, t_ref)
-    t3 = flat_rows(t_ref, GROUP, FRAME)
-    leaving = out_copies(o_ref, (out_density, out_momentum, out_energy), out_sem, 4, 0, 16)
-    leaving.append(pltpu.make_async_copy(t3, out_sums, out_sem))
-    for c in leaving:
-        c.start()
+                 q_ref, s_ref, o_ref, dm_ref, t_ref, x_ref, y_ref, sems, sem, out_sem):
+    tiles = Tiles(q_ref, sems, [((density, momentum, energy), y_before, y_after, pl.ds(1, 22), pl.ds(0, 22))])
+    tiles.start()
+    copies = dm_copies(dm, y_before, y_after, sem, dm_ref, 4, 0, 16)
+    start_all(copies)
     clear(send)
-    smooth(lambda p, row: t_ref[pl.ds((2 + p) * FRAME + row, 8), :], dest, x_ref, y_ref, send, 0)
-    for c in leaving:
-        c.wait()
+    x_sweep(q_ref, s_ref, 16, ((0, 0, 16),), tiles.wait)
+    wait_all(copies)
+    yz_sweep(s_ref, dm_ref, o_ref, t_ref, 16, 0)
+    leaving = out_copies(o_ref, 16, (out_density, out_momentum, out_energy), out_sem, 4, 0, 16)
+    leaving.append(sums_copy(t_ref, 0, 16, out_sums, out_sem))
+    start_all(leaving)
+    smooth(lambda p, row: t_ref[pl.ds((2 + p) * STRIDE + row, 8), :], dest, x_ref, y_ref, send, 0)
+    wait_all(leaving)
+
+
+def middle_kernel(dest, density, momentum, energy, dm, y_before, y_after, sums_inner,
+                  in_density, in_momentum, in_energy,
+                  out_density, out_momentum, out_energy, out_sums, send,
+                  q_ref, s_ref, o_ref, dm_ref, t_ref, x_ref, y_ref, sems, sem, out_sem):
+    tiles = Tiles(q_ref, sems, [((density, momentum, energy), y_before, y_after, pl.ds(17, 14), pl.ds(0, 14))])
+    tiles.start()
+    copies = dm_copies(dm, y_before, y_after, sem, dm_ref, 20, 0, 8)
+    copies.append(pltpu.make_async_copy(
+        sums_inner.at[pl.ds(10, 6)], framed(t_ref).at[pl.ds(0, 6), pl.ds(0, FRAME)], sem))
+    start_all(copies)
+    clear(send)
+    x_sweep(q_ref, s_ref, 8, ((0, 0, 8),), tiles.wait)
+    wait_all(copies)
+    yz_sweep(s_ref, dm_ref, o_ref, t_ref, 8, 6)
+    leaving = out_copies(o_ref, 8, (out_density, out_momentum, out_energy), out_sem, 20, 0, 8)
+    leaving.append(sums_copy(t_ref, 6, 8, out_sums, out_sem))
+    start_all(leaving)
+    smooth(lambda p, row: t_ref[pl.ds(p * STRIDE + row, 8), :], dest, x_ref, y_ref, send, 0)
+    wait_all(leaving)
 
 
 def outer_kernel(density, momentum, energy, dm, y_before, y_after, x_before, x_after, c_before, c_after,
                  in_density, in_momentum, in_energy,
                  out_density, out_momentum, out_energy, out_sums, to_next, to_prev,
-                 q_ref, s_ref, o_ref, dm_ref, t_ref, sem, out_sem):
-    mid = pl.ds(8, NY)
-    copies = (load_copies(density, momentum, energy, sem, q_ref, 17, 0, 15)
-              + load_copies(density, momentum, energy, sem, q_ref, 0, 21, 7)
-              + side_copies(y_before, y_after, sem, q_ref, 17, 0, 15)
-              + side_copies(y_before, y_after, sem, q_ref, 0, 21, 7)
-              + side_copies(c_before, c_after, sem, q_ref, 0, 15, 6)
-              + dm_copies(dm, y_before, y_after, sem, dm_ref, 20, 0, 12)
-              + dm_copies(dm, y_before, y_after, sem, dm_ref, 0, 12, 4))
-    copies.append(pltpu.make_async_copy(x_after, q_ref.at[:, pl.ds(15, 3), mid], sem))
-    copies.append(pltpu.make_async_copy(x_before, q_ref.at[:, pl.ds(18, 3), mid], sem))
-    fetch(copies)
-    x_sweep(q_ref, s_ref, ((0, 0, 12), (18, 12, 4)))
-    yz_sweep(s_ref, dm_ref, o_ref, t_ref)
-    t3 = flat_rows(t_ref, GROUP, FRAME)
+                 q_ref, s_ref, o_ref, dm_ref, t_ref, sems, sem, out_sem):
+    fields = (density, momentum, energy)
+    tiles = Tiles(q_ref, sems, [
+        (fields, y_before, y_after, pl.ds(25, 7), pl.ds(0, 7)),
+        ((x_after,), c_before, c_after, pl.ds(0, 3), pl.ds(7, 3)),
+        ((x_before,), c_before.at[:, pl.ds(3, 3)], c_after.at[:, pl.ds(3, 3)], pl.ds(0, 3), pl.ds(10, 3)),
+        (fields, y_before, y_after, pl.ds(0, 7), pl.ds(13, 7)),
+    ])
+    tiles.start()
+    copies = (dm_copies(dm, y_before, y_after, sem, dm_ref, 28, 0, 4)
+              + dm_copies(dm, y_before, y_after, sem, dm_ref, 0, 4, 4))
+    start_all(copies)
+    x_sweep(q_ref, s_ref, 8, ((0, 0, 4), (10, 4, 4)), tiles.wait)
+    wait_all(copies)
+    yz_sweep(s_ref, dm_ref, o_ref, t_ref, 8, 0)
     outs = (out_density, out_momentum, out_energy)
-    leaving = out_copies(o_ref, outs, out_sem, 20, 0, 12) + out_copies(o_ref, outs, out_sem, 0, 12, 4)
-    leaving.append(pltpu.make_async_copy(t3, out_sums, out_sem))
-    leaving.append(pltpu.make_async_copy(t3.at[pl.ds(10, 2)], to_next, out_sem))
-    leaving.append(pltpu.make_async_copy(t3.at[pl.ds(12, 2)], to_prev, out_sem))
-    fetch(leaving)
-
-
-def rest_kernel(dest, sums_inner, sums_outer, from_prev, from_next, send, w_ref, x_ref, y_ref, sem):
+    leaving = out_copies(o_ref, 8, outs, out_sem, 28, 0, 4) + out_copies(o_ref, 8, outs, out_sem, 0, 4, 4)
+    leaving.append(sums_copy(t_ref, 0, 8, out_sums, out_sem))
+    leaving.append(sums_copy(t_ref, 2, 2, to_next, out_sem))
+    leaving.append(sums_copy(t_ref, 4, 2, to_prev, out_sem))
+    start_all(leaving)
+    wait_all(leaving)
+
+
+def rest_kernel(dest, sums_inner, sums_middle, sums_outer, from_prev, from_next, send, w_ref, x_ref, y_ref, sem):
     def part(src, own, place, count):
         return pltpu.make_async_copy(src.at[pl.ds(own, count)], w_ref.at[pl.ds(place, count)], sem)
 
     copies = [
         part(from_prev, 0, 0, 2),
-        part(sums_outer, 12, 2, 4),
+        part(sums_outer, 4, 2, 4),
         part(sums_inner, 0, 6, 6),
-        part(sums_inner, 10, 12, 6),
-        part(sums_outer, 0, 18, 12),
-        part(from_next, 0, 30, 2),
+        part(sums_middle, 2, 12, 6),
+        part(sums_outer, 0, 18, 4),
+        part(from_next, 0, 22, 2),
     ]
-    for c in copies:
-        c.start()
+    start_all(copies)
     clear(send)
-    for c in copies:
-        c.wait()
-    for row, base in ((0, 0), (8, 12), (16, 20)):
+    wait_all(copies)
+    for row, base in ((0, 0), (8, 12)):
         smooth(lambda p, r: w_ref[base + p, pl.ds(r, 8), :], dest, x_ref, y_ref, send, row)
 
 
@@ -367,15 +432,22 @@
     return pltpu.CompilerParams(vmem_limit_bytes=VMEM_LIMIT)
 
 
-def main_scratch(planes):
-    rows = GROUP * FRAME
+def cost(planes):
+    return pl.CostEstimate(flops=planes * 40_000_000_000, bytes_accessed=planes * 600_000, transcendentals=0)
+
+
+def main_scratch(planes, held, sums):
     return [
-        pltpu.VMEM((5, planes, FRAME, NZ), F32),
-        pltpu.VMEM((5 * rows, NZ), F32),
-        pltpu.VMEM((5 * rows, NZ), F32),
-        pltpu.VMEM((rows, NZ), F32),
-        pltpu.VMEM((rows, NZ), F32),
+        pltpu.VMEM((5, held, FRAME, NZ), F32),
+        pltpu.VMEM((5 * planes * STRIDE, NZ), F32),
+        pltpu.VMEM((5 * planes * STRIDE, NZ), F32),
+        pltpu.VMEM((planes * STRIDE, NZ), F32),
+        pltpu.VMEM((sums * STRIDE, NZ), F32),
     ]
+
+
+def semaphores():
+    return [pltpu.SemaphoreType.DMA((TILES,)), pltpu.SemaphoreType.DMA, pltpu.SemaphoreType.DMA]
 
 
 def smooth_scratch():
@@ -402,46 +474,68 @@
     x_before = shifted(cut(fields, (NX - 3, NX), (0, NY)), "box", 1)
     x_after = shifted(cut(fields, (0, 3), (0, NY)), "box", -1)
 
+    def exchange(send, planes):
+        return lax.all_to_all(send.reshape(16, 2, planes, 1024), "box", split_axis=0, concat_axis=0, tiled=True)
+
     inner = pl.pallas_call(
         inner_kernel,
-        out_shape=FIELD_SHAPES + (shape(GROUP, FRAME, NZ), shape(32, 8, 1024)),
+        out_shape=FIELD_SHAPES + (shape(16, FRAME, NZ), shape(32, 8, 1024)),
         in_specs=[SMEM] + [ANY] * 6,
         out_specs=[ANY] * 4 + [VMEM],
-        scratch_shapes=main_scratch(22) + smooth_scratch() + [pltpu.SemaphoreType.DMA, pltpu.SemaphoreType.DMA],
+        scratch_shapes=main_scratch(16, 22, 16) + smooth_scratch() + semaphores(),
         compiler_params=params(),
+        cost_estimate=cost(16),
         name="inner",
     )(dest, density, momentum, energy, dm_density, y_before, y_after)
-    new_density, new_momentum, new_energy, sums_inner, send_inner = inner
-    got_inner = lax.all_to_all(send_inner.reshape(16, 2, 8, 1024), "box", split_axis=0, concat_axis=0, tiled=True)
-
+    *made, sums_inner, send_inner = inner
+    got_inner = exchange(send_inner, 8)
+
+    x_before, x_after, sums_inner = lax.optimization_barrier((x_before, x_after, sums_inner))
     x_both = jnp.concatenate([x_after, x_before], axis=1)
     c_before = shifted(x_both[:, :, NY - 8:], "grp", 1)
     c_after = shifted(x_both[:, :, :8], "grp", -1)
+    middle = pl.pallas_call(
+        middle_kernel,
+        out_shape=FIELD_SHAPES + (shape(8, FRAME, NZ), shape(32, 8, 1024)),
+        in_specs=[SMEM] + [ANY] * 10,
+        out_specs=[ANY] * 4 + [VMEM],
+        scratch_shapes=main_scratch(8, 14, 14) + smooth_scratch() + semaphores(),
+        input_output_aliases={8: 0, 9: 1, 10: 2},
+        compiler_params=params(),
+        cost_estimate=cost(8),
+        name="middle",
+    )(dest, density, momentum, energy, dm_density, y_before, y_after, sums_inner, *made)
+    *made, sums_middle, send_middle = middle
+    send_middle, got_inner = lax.optimization_barrier((send_middle, got_inner))
+    got_middle = exchange(send_middle, 8)
+
     outer = pl.pallas_call(
         outer_kernel,
-        out_shape=FIELD_SHAPES + (shape(GROUP, FRAME, NZ), shape(2, FRAME, NZ), shape(2, FRAME, NZ)),
+        out_shape=FIELD_SHAPES + (shape(8, FRAME, NZ), shape(2, FRAME, NZ), shape(2, FRAME, NZ)),
         in_specs=[ANY] * 13,
         out_specs=[ANY] * 6,
-        scratch_shapes=main_scratch(28) + [pltpu.SemaphoreType.DMA, pltpu.SemaphoreType.DMA],
+        scratch_shapes=main_scratch(8, 20, 8) + semaphores(),
         input_output_aliases={10: 0, 11: 1, 12: 2},
         compiler_params=params(),
+        cost_estimate=cost(8),
         name="outer",
-    )(density, momentum, energy, dm_density, y_before, y_after, x_before, x_after, c_before, c_after,
-      new_density, new_momentum, new_energy)
+    )(density, momentum, energy, dm_density, y_before, y_after, x_before, x_after, c_before, c_after, *made)
     new_density, new_momentum, new_energy, sums_outer, to_next, to_prev = outer
     from_prev = shifted(to_next, "box", 1)
     from_next = shifted(to_prev, "box", -1)
     send_rest = pl.pallas_call(
         rest_kernel,
-        out_shape=shape(32, 24, 1024),
-        in_specs=[SMEM] + [ANY] * 4,
+        out_shape=shape(32, 16, 1024),
+        in_specs=[SMEM] + [ANY] * 5,
         out_specs=VMEM,
-        scratch_shapes=[pltpu.VMEM((32, FRAME, NZ), F32)] + smooth_scratch() + [pltpu.SemaphoreType.DMA],
+        scratch_shapes=[pltpu.VMEM((24, FRAME, NZ), F32)] + smooth_scratch() + [pltpu.SemaphoreType.DMA],
         compiler_params=params(),
+        cost_estimate=cost(2),
         name="rest",
-    )(dest, sums_inner, sums_outer, from_prev, from_next)
-    got_rest = lax.all_to_all(send_rest.reshape(16, 2, 24, 1024), "box", split_axis=0, concat_axis=0, tiled=True)
-    kd = jnp.concatenate([got_rest[:, :, :8], got_inner, got_rest[:, :, 8:]], axis=2)
+    )(dest, sums_inner, sums_middle, sums_outer, from_prev, from_next)
+    send_rest, got_middle = lax.optimization_barrier((send_rest, got_middle))
+    got_rest = exchange(send_rest, 16)
+    kd = jnp.concatenate([got_rest[:, :, :8], got_inner, got_middle, got_rest[:, :, 8:]], axis=2)
     return (new_density, new_momentum, new_energy, kd[None, None])
 
 

time: 210 us -> 156 us (0.74)
  Pallas kernels: 99.1 us -> 64.4 us
  blocking collectives: 47.2 us -> 32.7 us
  waiting for transfers between devices: 28.6 us -> 15.5 us
  starting transfers between devices: 18 us -> 25.2 us
    pallas_call x3 -> x4, Pallas kernels: 99.1 us -> 64.4 us  [the longest x1 28.4 us: body(): pl.pallas_call(inner_kernel, out_shape=FIELD_SHAPES + (shape(16, FRAME, N...]
    all_to_all x1, blocking collectives: 47.2 us -> 32.7 us  [exchange(): lax.all_to_all(send.reshape(16, 2, planes, 1024), 'box', split_axis=0, co...]
    ppermute x8, waiting for transfers between devices: 14.3 us -> 0.02 us  [shifted(): lax.ppermute(value, axis, [(i, (i + by) % size) for i in range(size)])]
    all_to_all x1 -> x2, starting transfers between devices: 4.34 us -> 10.8 us  [exchange(): lax.all_to_all(send.reshape(16, 2, planes, 1024), 'box', split_axis=0, co...]
    all_to_all x1 -> x2, waiting for transfers between devices: 14.2 us -> 15.5 us  [exchange(): lax.all_to_all(send.reshape(16, 2, planes, 1024), 'box', split_axis=0, co...]
  transfers between devices with their start and end apart: 9 -> 10, of which waited for: 4 -> 1; matrix products, arithmetic and copies ran while one was open for 3% -> 5% of each run, Pallas kernels for 22% -> 42%
where the time goes in v2:
time: 156 us; the launch traced here: 155 us
  Pallas kernels  64.4 us (41%)
  blocking collectives  32.7 us (21%)
  starting transfers between devices  25.2 us (16%)
  waiting for transfers between devices  15.5 us (10%)
  local copies, waits for them, and re-layouts  10.8 us (7%)
  other arithmetic  5.59 us (4%)
    all_to_all x1, blocking collectives, exchange(): lax.all_to_all(send.reshape(16, 2, planes, 1024), 'box', split_axis=0, co...  32.7 us
    pallas_call x1, Pallas kernels, body(): pl.pallas_call(inner_kernel, out_shape=FIELD_SHAPES + (shape(16, FRAME, N...  28.4 us
    pallas_call x1, Pallas kernels, body(): pl.pallas_call(middle_kernel, out_shape=FIELD_SHAPES + (shape(8, FRAME, N...  16.3 us
    all_to_all x2, waiting for transfers between devices, exchange(): lax.all_to_all(send.reshape(16, 2, planes, 1024), 'box', split_axis=0, co...  15.5 us
    pallas_call x1, Pallas kernels, body(): pl.pallas_call(outer_kernel, out_shape=FIELD_SHAPES + (shape(8, FRAME, NZ...  15.2 us
    ppermute x8, starting transfers between devices, shifted(): lax.ppermute(value, axis, [(i, (i + by) % size) for i in range(size)])  14.5 us
    all_to_all x2, starting transfers between devices, exchange(): lax.all_to_all(send.reshape(16, 2, planes, 1024), 'box', split_axis=0, co...  10.8 us
    slice x5, local copies, waits for them, and re-layouts, cut(): a[:, planes[0]:planes[1], rows[0]:rows[1]]  5.68 us
  transfers between devices with their start and end apart: 10, of which 1 were waited for; matrix products, arithmetic and copies ran while one was open for 5% of the time, Pallas kernels for 42%

profile of v2, /device:TPU:32, one launch (start us, length us, event | category | flops | bytes accessed | tf_op | source)
XLA Modules:
  0.0 155.1 jit_solution(7623667424917692414)
XLA Ops:
  0.6 1.0 fusion.7
  1.6 1.2 fusion.1
  2.8 1.1 fusion.5
  3.9 0.1 pad_maximum_fusion
  4.0 0.0 collective-permute-start
  4.0 0.1 pad_maximum_fusion.1
  4.1 1.7 %collective-permute-start.1 = (f32[6,32,8,128]{3,2,1,0:T(8,128)S(1)}, f32[6,32,8,128]{3,2,1,0:T(8,128)S(1)}, u32[]{:S(2)}, u32[]{:S(2)}) collective-permute-start(f32[6,32,8,128]{3,2,1,0:T(8,128)S(1)} %pad_maximum_fusion.1), channel_id=1, source_target_pairs={{0,7},{1,0},{2,1},{3,2},{4,3},{5,4},{6,5},{7,6},{8,15},{9,8},{10,9... | collective-permute-start | bytes 2359304 | tf_op jit(solution)/shard_map/ppermute | solution.py:462
  5.8 1.2 fusion.3
  7.0 1.2 fusion
  8.2 0.9 pad_maximum_fusion.2
  9.1 1.5 collective-permute-start.2
  10.6 0.9 pad_maximum_fusion.3
  11.6 3.9 %collective-permute-start.3 = (f32[5,3,96,128]{3,2,1,0:T(8,128)}, f32[5,3,96,128]{3,2,1,0:T(8,128)}, u32[]{:S(2)}, u32[]{:S(2)}) collective-permute-start(f32[5,3,96,128]{3,2,1,0:T(8,128)} %pad_maximum_fusion.3), channel_id=1, source_target_pairs={{0,120},{8,0},{16,8},{24,16},{32,24},{40,32},{48,40},{56,48},{64,5... | collective-permute-start | bytes 2211848 | tf_op jit(solution)/shard_map/ppermute | solution.py:462
  15.4 0.0 collective-permute-done.y_before
  15.4 0.0 copy-start
  15.4 0.0 collective-permute-done.1.y_after
  15.4 0.0 copy-start.1
  15.5 0.9 copy-done
  16.3 0.3 copy-done.1
  16.6 28.4 %inner.1 = (f32[32,96,128]{2,1,0:T(8,128)}, f32[3,32,96,128]{3,2,1,0:T(8,128)}, f32[32,96,128]{2,1,0:T(8,128)}, f32[16,112,128]{2,1,0:T(8,128)}, f32[32,8,1024]{2,1,0:T(8,128)}) custom-call(s32[12]{0:T(128)} %bitcast.16, f32[32,96,128]{2,1,0:T(8,128)} %density.5, f32[3,32,96,128]{3,2,1,0:T(8,128)} %momentum.5, f32[32,96,128]{2,1,0:T(8,128)} %energy.5, ...), custom_call_target="tpu_custom_call" | custom-call | flops 640000000000 | bytes 9600000 | tf_op jit(solution)/shard_map/inner/pallas_call | solution.py:480
  45.0 0.0 collective-permute-done.2.x_before
  45.0 0.0 collective-permute-done.3.x_after
  45.0 7.1 %all-to-all-start = ((f32[16,2,8,1024]{3,2,1,0:T(8,128)}), f32[16,2,8,1024]{3,2,1,0:T(8,128)}, u32[]{:S(2)}, u32[]{:S(2)}) async-start(f32[16,2,8,1024]{3,2,1,0:T(8,128)} %bitcast.10), calls=%async_computation | async-start | bytes 2097152 | tf_op jit(solution)/shard_map/all_to_all | solution.py:478
  52.1 1.2 constant_dynamic-update-slice_fusion.1
  53.3 1.2 constant_dynamic-update-slice_fusion
  54.5 0.7 fusion.8
  55.2 1.7 %collective-permute-start.5 = (f32[5,6,8,128]{3,2,1,0:T(8,128)}, f32[5,6,8,128]{3,2,1,0:T(8,128)}, u32[]{:S(2)}, u32[]{:S(2)}) collective-permute-start(f32[5,6,8,128]{3,2,1,0:T(8,128)} %get-tuple-element.66), channel_id=1, source_target_pairs={{0,7},{1,0},{2,1},{3,2},{4,3},{5,4},{6,5},{7,6},{8,15},{9,8},{10,9... | collective-permute-start | bytes 368648 | tf_op jit(solution)/shard_map/ppermute | solution.py:462
  56.8 0.3 collective-permute-start.4
  57.1 16.3 %middle.1 = (f32[32,96,128]{2,1,0:T(8,128)}, f32[3,32,96,128]{3,2,1,0:T(8,128)}, f32[32,96,128]{2,1,0:T(8,128)}, f32[8,112,128]{2,1,0:T(8,128)}, f32[32,8,1024]{2,1,0:T(8,128)}) custom-call(s32[12]{0:T(128)} %bitcast.17, f32[32,96,128]{2,1,0:T(8,128)} %density.5, ...), custom_call_target="tpu_custom_call", output_to_operand_aliasing={{0}: (8, {}), {1}: (9, {}), {2}: (10, {})} | custom-call | flops 320000000000 | bytes 4800000 | tf_op jit(solution)/shard_map/middle/pallas_call | solution.py:497
  73.4 0.0 collective-permute-done.5.c_after
  73.4 0.0 collective-permute-done.4.c_before
  73.4 15.2 %outer.1 = (f32[32,96,128]{2,1,0:T(8,128)}, f32[3,32,96,128]{3,2,1,0:T(8,128)}, f32[32,96,128]{2,1,0:T(8,128)}, f32[8,112,128]{2,1,0:T(8,128)}, f32[2,112,128]{2,1,0:T(8,128)}, /*index=5*/f32[2,112,128]{2,1,0:T(8,128)}) custom-call(f32[32,96,128]{2,1,0:T(8,128)} %density.5, ...), custom_call_target="tpu_custom_call", output_to_operand_aliasing={{0}: (10, {}), {1}: (11, {}), {2}: (12, {})} | custom-call | flops 320000000000 | bytes 4800000 | tf_op jit(solution)/shard_map/outer/pallas_call | solution.py:512
  88.7 1.7 %collective-permute-start.6 = (f32[2,112,128]{2,1,0:T(8,128)}, f32[2,112,128]{2,1,0:T(8,128)S(1)}, u32[]{:S(2)}, u32[]{:S(2)}) collective-permute-start(f32[2,112,128]{2,1,0:T(8,128)} %get-tuple-element.42), channel_id=1, source_target_pairs={{0,8},{8,16},{16,24},{24,32},{32,40},{40,48},{48,56},{56,64},{64,7... | collective-permute-start | bytes 344072 | tf_op jit(solution)/shard_map/ppermute | solution.py:462
  90.3 3.8 %collective-permute-start.7 = (f32[2,112,128]{2,1,0:T(8,128)}, f32[2,112,128]{2,1,0:T(8,128)S(1)}, u32[]{:S(2)}, u32[]{:S(2)}) collective-permute-start(f32[2,112,128]{2,1,0:T(8,128)} %get-tuple-element.43), channel_id=1, source_target_pairs={{0,120},{8,0},{16,8},{24,16},{32,24},{40,32},{48,40},{56,48},{64,5... | collective-permute-start | bytes 344072 | tf_op jit(solution)/shard_map/ppermute | solution.py:462
  94.1 0.0 all-to-all-done
  94.1 3.7 %all-to-all-start.1 = ((f32[16,2,8,1024]{3,2,1,0:T(8,128)}), f32[16,2,8,1024]{3,2,1,0:T(8,128)S(1)}, u32[]{:S(2)}, u32[]{:S(2)}) async-start(f32[16,2,8,1024]{3,2,1,0:T(8,128)} %bitcast.5), calls=%async_computation.1 | async-start | bytes 2097152 | tf_op jit(solution)/shard_map/all_to_all | solution.py:478
  97.8 0.0 collective-permute-done.6.from_prev
  97.8 0.0 copy-start.2
  97.8 0.0 collective-permute-done.7.from_next
  97.8 0.0 copy-start.3
  97.8 0.6 copy-done.2
  98.4 0.1 copy-done.3
  98.5 4.5 %rest.1 = f32[32,16,1024]{2,1,0:T(8,128)} custom-call(s32[12]{0:T(128)} %bitcast.18, f32[16,112,128]{2,1,0:T(8,128)} %get-tuple-element.30.sums_inner, f32[8,112,128]{2,1,0:T(8,128)} %get-tuple-element.40.sums_middle, f32[8,112,128]{2,1,0:T(8,128)} %get-tuple-element.41.sums_outer, f32[2,112,128]{2,1,0:T(8,128)} %copy-done.2, f32[2,112,128]{2,1,0:T(8,128)} %copy-done.3), custom_call_target="tpu_custom_call" | custom-call | flops 80000000000 | bytes 1200000 | tf_op jit(solution)/shard_map/rest/pallas_call | solution.py:526
  103.0 15.5 %all-to-all-done.1 = f32[16,2,8,1024]{3,2,1,0:T(8,128)S(1)} async-done(((f32[16,2,8,1024]{3,2,1,0:T(8,128)}), f32[16,2,8,1024]{3,2,1,0:T(8,128)S(1)}, u32[]{:S(2)}, u32[]{:S(2)}) %all-to-all-start.1) | async-done | bytes 1048608 | tf_op jit(solution)/shard_map/all_to_all | solution.py:478
  118.5 32.7 %all_to_all.15 = f32[16,2,16,1024]{3,2,1,0:T(8,128)S(1)} all-to-all(f32[16,2,16,1024]{3,2,1,0:T(8,128)} %bitcast.9), channel_id=1, replica_groups=mesh['box'=16,'grp'=8] {'box'}, dimensions={0} | all-to-all | bytes 4194304 | tf_op jit(solution)/shard_map/all_to_all | solution.py:478
  151.2 0.2 fusion.2
  151.5 3.6 %maximum_bitcast_fusion = f32[1,1,16,2,32,1024]{5,4,3,2,1,0:T(8,128)} fusion(f32[16,2,8,1024]{3,2,1,0:T(8,128)S(1)} %get-tuple-element.55, f32[16,2,8,1024]{3,2,1,0:T(8,128)S(1)} %all-to-all-done.1, f32[16,2,8,1024]{3,2,1,0:T(8,128)} %all-to-all-done, f32[16,2,8,1024]{3,2,1,0:T(8,128)S(1)} %get-tuple-element.54), kind=kLoop, calls=%fused_computation | loop fusion | flops 3145728 | bytes 8388608 | tf_op jit(solution)/shard_map/broadcast_in_dim | solution.py:539
Async XLA Ops:
  4.0 11.4 %collective-permute-start = (f32[6,32,8,128]{3,2,1,0:T(8,128)S(1)}, f32[6,32,8,128]{3,2,1,0:T(8,128)S(1)}, u32[]{:S(2)}, u32[]{:S(2)}) collective-permute-start(f32[6,32,8,128]{3,2,1,0:T(8,128)S(1)} %pad_maximum_fusion), channel_id=1, source_target_pairs={{0,1},{1,2},{2,3},{3,4},{4,5},{5,6},{6,7},{7,0},{8,9},{9,10},{10,1... | collective-permute-start | bytes 2359304 | tf_op jit(solution)/shard_map/ppermute | solution.py:462
  4.1 11.3 %collective-permute-start.1 = (f32[6,32,8,128]{3,2,1,0:T(8,128)S(1)}, f32[6,32,8,128]{3,2,1,0:T(8,128)S(1)}, u32[]{:S(2)}, u32[]{:S(2)}) collective-permute-start(f32[6,32,8,128]{3,2,1,0:T(8,128)S(1)} %pad_maximum_fusion.1), channel_id=1, source_target_pairs={{0,7},{1,0},{2,1},{3,2},{4,3},{5,4},{6,5},{7,6},{8,15},{9,8},{10,9... | collective-permute-start | bytes 2359304 | tf_op jit(solution)/shard_map/ppermute | solution.py:462
  9.1 35.9 %collective-permute-start.2 = (f32[5,3,96,128]{3,2,1,0:T(8,128)}, f32[5,3,96,128]{3,2,1,0:T(8,128)}, u32[]{:S(2)}, u32[]{:S(2)}) collective-permute-start(f32[5,3,96,128]{3,2,1,0:T(8,128)} %pad_maximum_fusion.2), channel_id=1, source_target_pairs={{0,8},{8,16},{16,24},{24,32},{32,40},{40,48},{48,56},{56,64},{64,7... | collective-permute-start | bytes 2211848 | tf_op jit(solution)/shard_map/ppermute | solution.py:462
  11.6 33.4 %collective-permute-start.3 = (f32[5,3,96,128]{3,2,1,0:T(8,128)}, f32[5,3,96,128]{3,2,1,0:T(8,128)}, u32[]{:S(2)}, u32[]{:S(2)}) collective-permute-start(f32[5,3,96,128]{3,2,1,0:T(8,128)} %pad_maximum_fusion.3), channel_id=1, source_target_pairs={{0,120},{8,0},{16,8},{24,16},{32,24},{40,32},{48,40},{56,48},{64,5... | collective-permute-start | bytes 2211848 | tf_op jit(solution)/shard_map/ppermute | solution.py:462
  15.4 0.9 copy-start
  15.4 1.1 copy-start.1
  45.0 49.1 %all-to-all-start = ((f32[16,2,8,1024]{3,2,1,0:T(8,128)}), f32[16,2,8,1024]{3,2,1,0:T(8,128)}, u32[]{:S(2)}, u32[]{:S(2)}) async-start(f32[16,2,8,1024]{3,2,1,0:T(8,128)} %bitcast.10), calls=%async_computation | async-start | bytes 2097152 | tf_op jit(solution)/shard_map/all_to_all | solution.py:478
  55.2 18.2 %collective-permute-start.5 = (f32[5,6,8,128]{3,2,1,0:T(8,128)}, f32[5,6,8,128]{3,2,1,0:T(8,128)}, u32[]{:S(2)}, u32[]{:S(2)}) collective-permute-start(f32[5,6,8,128]{3,2,1,0:T(8,128)} %get-tuple-element.66), channel_id=1, source_target_pairs={{0,7},{1,0},{2,1},{3,2},{4,3},{5,4},{6,5},{7,6},{8,15},{9,8},{10,9... | collective-permute-start | bytes 368648 | tf_op jit(solution)/shard_map/ppermute | solution.py:462
  56.8 16.6 %collective-permute-start.4 = (f32[5,6,8,128]{3,2,1,0:T(8,128)}, f32[5,6,8,128]{3,2,1,0:T(8,128)}, u32[]{:S(2)}, u32[]{:S(2)}) collective-permute-start(f32[5,6,8,128]{3,2,1,0:T(8,128)} %get-tuple-element.67), channel_id=1, source_target_pairs={{0,1},{1,2},{2,3},{3,4},{4,5},{5,6},{6,7},{7,0},{8,9},{9,10},{10,1... | collective-permute-start | bytes 368648 | tf_op jit(solution)/shard_map/ppermute | solution.py:462
  88.7 9.1 %collective-permute-start.6 = (f32[2,112,128]{2,1,0:T(8,128)}, f32[2,112,128]{2,1,0:T(8,128)S(1)}, u32[]{:S(2)}, u32[]{:S(2)}) collective-permute-start(f32[2,112,128]{2,1,0:T(8,128)} %get-tuple-element.42), channel_id=1, source_target_pairs={{0,8},{8,16},{16,24},{24,32},{32,40},{40,48},{48,56},{56,64},{64,7... | collective-permute-start | bytes 344072 | tf_op jit(solution)/shard_map/ppermute | solution.py:462
  90.3 7.4 %collective-permute-start.7 = (f32[2,112,128]{2,1,0:T(8,128)}, f32[2,112,128]{2,1,0:T(8,128)S(1)}, u32[]{:S(2)}, u32[]{:S(2)}) collective-permute-start(f32[2,112,128]{2,1,0:T(8,128)} %get-tuple-element.43), channel_id=1, source_target_pairs={{0,120},{8,0},{16,8},{24,16},{32,24},{40,32},{48,40},{56,48},{64,5... | collective-permute-start | bytes 344072 | tf_op jit(solution)/shard_map/ppermute | solution.py:462
  94.1 24.4 %all-to-all-start.1 = ((f32[16,2,8,1024]{3,2,1,0:T(8,128)}), f32[16,2,8,1024]{3,2,1,0:T(8,128)S(1)}, u32[]{:S(2)}, u32[]{:S(2)}) async-start(f32[16,2,8,1024]{3,2,1,0:T(8,128)} %bitcast.5), calls=%async_computation.1 | async-start | bytes 2097152 | tf_op jit(solution)/shard_map/all_to_all | solution.py:478
  97.8 0.6 copy-start.2
  97.8 0.7 copy-start.3

commit v3 on v2

--- a/solution.py
+++ b/solution.py
@@ -22,6 +22,7 @@
 UNSCALES = (1.0, 1.0 / STEP, 1.0 / STEP, 1.0 / STEP, 1.0 / (2.0 * STEP * STEP))
 SOUND = math.sqrt(5.0 / 3.0)
 TINY = 1e-30
+COST = 1_100_000_000
 VMEM_LIMIT = 56 * 1024 * 1024
 
 
@@ -127,32 +128,41 @@
     return t + turn(pair, 2) + turn(pair, -1)
 
 
-def x_sweep(q_ref, s_ref, planes, segments, ready):
+def x_lines(segments, read, write):
+    for base, out_base, count in segments:
+        line = Line(1)
+        for i in range(count + 6):
+            new = [read(f, base + i) * SCALES[f] if f else read(f, base + i) for f in range(5)]
+            out = line.push(new)
+            if out is not None:
+                for f in range(5):
+                    write(f, out_base + i - 6, out[f])
+
+
+def x_sweep(q_ref, s_ref, planes, segments, tiles, ready, place):
     def tile(t, _):
         ready(t)
         row = pl.multiple_of(t * 8, 8)
-        for base, out_base, count in segments:
-            line = Line(1)
-            for i in range(count + 6):
-                new = [q_ref[f, base + i, pl.ds(row, 8), :] * SCALES[f] if f else q_ref[f, base + i, pl.ds(row, 8), :]
-                       for f in range(5)]
-                out = line.push(new)
-                if out is not None:
-                    x = out_base + i - 6
-                    for f in range(5):
-                        s_ref[pl.ds((f * planes + x) * STRIDE + row, 8), :] = out[f]
-        return 0
-
-    lax.fori_loop(0, TILES, tile, 0)
+        to = pl.multiple_of(place(t), 8)
+
+        def write(f, x, value):
+            s_ref[pl.ds((f * planes + x) * STRIDE + to, 8), :] = value
+
+        x_lines(segments, lambda f, i: q_ref[f, i, pl.ds(row, 8), :], write)
+        return 0
+
+    lax.fori_loop(0, tiles, tile, 0)
 
 
 ROWS_STEP = 10
 
 
-def yz_sweep(s_ref, dm_ref, o_ref, t_ref, planes, t_base):
+def yz_sweep(s_ref, dm_ref, o_ref, t_ref, planes, ready, done):
     def group(g, _):
-        def at(f, row, base=0):
-            return pl.ds((f * planes + g * 8 + base) * STRIDE + row, 8, stride=STRIDE)
+        ready(g)
+
+        def at(f, row):
+            return pl.ds((f * planes + g * 8) * STRIDE + row, 8, stride=STRIDE)
 
         def rows(row):
             return [s_ref[at(f, row), :] for f in range(5)]
@@ -173,10 +183,11 @@
                 for f in range(5):
                     o_ref[at(f, row), :] = final[f] * UNSCALES[f] if f else final[f]
                 total = final[0] + dm_ref[at(0, row), :]
-                t_ref[at(0, row, t_base), :] = lane_sum(total)
+                t_ref[at(0, row), :] = lane_sum(total)
             return line.carry()
 
         lax.fori_loop(0, 100 // ROWS_STEP, some, first.carry())
+        done(g)
         return 0
 
     lax.fori_loop(0, planes // 8, group, 0)
@@ -333,63 +344,119 @@
     return pltpu.make_async_copy(framed(t_ref).at[pl.ds(base, count), pl.ds(0, FRAME)], out, sem)
 
 
-def inner_kernel(dest, density, momentum, energy, dm, y_before, y_after,
+def pack_kernel(density, momentum, energy, dm, y_last, y_first, x_last, x_first, c_ll, c_lf, c_fl, c_ff, sem):
+    copies = []
+
+    def fields(out, planes, rows):
+        copies.append(pltpu.make_async_copy(density.at[planes, rows], out.at[0], sem))
+        copies.append(pltpu.make_async_copy(momentum.at[:, planes, rows], out.at[pl.ds(1, 3)], sem))
+        copies.append(pltpu.make_async_copy(energy.at[planes, rows], out.at[4], sem))
+
+    ends = (pl.ds(NY - 8, 8), pl.ds(0, 8))
+    for out, rows in zip((y_last, y_first), ends):
+        fields(out, pl.ds(0, NX), rows)
+        copies.append(pltpu.make_async_copy(dm.at[:, rows], out.at[5], sem))
+    for x_out, c_out, planes in ((x_last, (c_ll, c_lf), pl.ds(NX - 3, 3)), (x_first, (c_fl, c_ff), pl.ds(0, 3))):
+        fields(x_out, planes, pl.ds(0, NY))
+        for n, rows in enumerate(ends):
+            fields(c_out[n], planes, rows)
+    start_all(copies)
+    wait_all(copies)
+
+
+WIDE = 24
+
+
+def x_kernel(density, momentum, energy, out, q_ref, s_ref, sems, out_sem):
+    held = pl.ds(1, WIDE + 6)
+
+    def copies(t):
+        rows = rows_of(t)
+        return [
+            pltpu.make_async_copy(density.at[held, rows], q_ref.at[0, :, rows], sems.at[t]),
+            pltpu.make_async_copy(momentum.at[:, held, rows], q_ref.at[pl.ds(1, 3), :, rows], sems.at[t]),
+            pltpu.make_async_copy(energy.at[held, rows], q_ref.at[4, :, rows], sems.at[t]),
+        ]
+
+    def leaving(t):
+        return pltpu.make_async_copy(s_ref.at[:, :, rows_of(t)], out.at[:, :, rows_of(t)], out_sem)
+
+    def begin(t, _):
+        start_all(copies(t))
+        return 0
+
+    def tile(t, _):
+        wait_all(copies(t))
+        rows = rows_of(t)
+
+        def write(f, x, value):
+            s_ref[f, x, rows, :] = value
+
+        x_lines(((0, 0, WIDE),), lambda f, i: q_ref[f, i, rows, :], write)
+        leaving(t).start()
+        return 0
+
+    def end(t, _):
+        leaving(t).wait()
+        return 0
+
+    lax.fori_loop(0, NY // 8, begin, 0)
+    lax.fori_loop(0, NY // 8, tile, 0)
+    lax.fori_loop(0, NY // 8, end, 0)
+
+
+def inner_kernel(dest, swept, dm, y_before, y_after,
                  out_density, out_momentum, out_energy, out_sums, send,
                  q_ref, s_ref, o_ref, dm_ref, t_ref, x_ref, y_ref, sems, sem, out_sem):
-    tiles = Tiles(q_ref, sems, [((density, momentum, energy), y_before, y_after, pl.ds(1, 22), pl.ds(0, 22))])
-    tiles.start()
-    copies = dm_copies(dm, y_before, y_after, sem, dm_ref, 4, 0, 16)
-    start_all(copies)
+    held = pl.ds(1, WIDE + 6)
+    s4 = s_ref.reshape(5, WIDE, STRIDE, NZ)
+    outs = (out_density, out_momentum, out_energy)
+
+    def swept_copy(g):
+        planes = pl.ds(g * 8, 8)
+        return pltpu.make_async_copy(swept.at[:, planes], s4.at[:, planes, pl.ds(8, NY)], sems.at[g])
+
+    def leaving(g):
+        return out_copies(o_ref, WIDE, outs, out_sem, 4 + g * 8, g * 8, 8)
+
+    halo = [
+        pltpu.make_async_copy(y_before.at[pl.ds(0, 5), held], q_ref.at[:, :, pl.ds(0, 8)], sem),
+        pltpu.make_async_copy(y_after.at[pl.ds(0, 5), held], q_ref.at[:, :, pl.ds(8, 8)], sem),
+    ] + dm_copies(dm, y_before, y_after, sem, dm_ref, 4, 0, WIDE)
+    start_all(halo)
+    for g in range(WIDE // 8):
+        swept_copy(g).start()
     clear(send)
-    x_sweep(q_ref, s_ref, 16, ((0, 0, 16),), tiles.wait)
-    wait_all(copies)
-    yz_sweep(s_ref, dm_ref, o_ref, t_ref, 16, 0)
-    leaving = out_copies(o_ref, 16, (out_density, out_momentum, out_energy), out_sem, 4, 0, 16)
-    leaving.append(sums_copy(t_ref, 0, 16, out_sums, out_sem))
-    start_all(leaving)
-    smooth(lambda p, row: t_ref[pl.ds((2 + p) * STRIDE + row, 8), :], dest, x_ref, y_ref, send, 0)
-    wait_all(leaving)
-
-
-def middle_kernel(dest, density, momentum, energy, dm, y_before, y_after, sums_inner,
-                  in_density, in_momentum, in_energy,
-                  out_density, out_momentum, out_energy, out_sums, send,
-                  q_ref, s_ref, o_ref, dm_ref, t_ref, x_ref, y_ref, sems, sem, out_sem):
-    tiles = Tiles(q_ref, sems, [((density, momentum, energy), y_before, y_after, pl.ds(17, 14), pl.ds(0, 14))])
-    tiles.start()
-    copies = dm_copies(dm, y_before, y_after, sem, dm_ref, 20, 0, 8)
-    copies.append(pltpu.make_async_copy(
-        sums_inner.at[pl.ds(10, 6)], framed(t_ref).at[pl.ds(0, 6), pl.ds(0, FRAME)], sem))
-    start_all(copies)
-    clear(send)
-    x_sweep(q_ref, s_ref, 8, ((0, 0, 8),), tiles.wait)
-    wait_all(copies)
-    yz_sweep(s_ref, dm_ref, o_ref, t_ref, 8, 6)
-    leaving = out_copies(o_ref, 8, (out_density, out_momentum, out_energy), out_sem, 20, 0, 8)
-    leaving.append(sums_copy(t_ref, 6, 8, out_sums, out_sem))
-    start_all(leaving)
-    smooth(lambda p, row: t_ref[pl.ds(p * STRIDE + row, 8), :], dest, x_ref, y_ref, send, 0)
-    wait_all(leaving)
-
-
-def outer_kernel(density, momentum, energy, dm, y_before, y_after, x_before, x_after, c_before, c_after,
+    wait_all(halo)
+    x_sweep(q_ref, s_ref, WIDE, ((0, 0, WIDE),), 2, lambda t: None, lambda t: t * 104)
+    yz_sweep(s_ref, dm_ref, o_ref, t_ref, WIDE, lambda g: swept_copy(g).wait(), lambda g: start_all(leaving(g)))
+    sums = sums_copy(t_ref, 0, WIDE, out_sums, sem)
+    sums.start()
+    for row, base in ((0, 2), (8, 10)):
+        smooth(lambda p, r: t_ref[pl.ds((base + p) * STRIDE + r, 8), :], dest, x_ref, y_ref, send, row)
+    sums.wait()
+    for g in range(WIDE // 8):
+        wait_all(leaving(g))
+
+
+def outer_kernel(density, momentum, energy, dm, y_before, y_after, x_before, x_after, c_bb, c_ba, c_ab, c_aa,
                  in_density, in_momentum, in_energy,
                  out_density, out_momentum, out_energy, out_sums, to_next, to_prev,
                  q_ref, s_ref, o_ref, dm_ref, t_ref, sems, sem, out_sem):
     fields = (density, momentum, energy)
     tiles = Tiles(q_ref, sems, [
         (fields, y_before, y_after, pl.ds(25, 7), pl.ds(0, 7)),
-        ((x_after,), c_before, c_after, pl.ds(0, 3), pl.ds(7, 3)),
-        ((x_before,), c_before.at[:, pl.ds(3, 3)], c_after.at[:, pl.ds(3, 3)], pl.ds(0, 3), pl.ds(10, 3)),
+        ((x_after,), c_ab, c_aa, pl.ds(0, 3), pl.ds(7, 3)),
+        ((x_before,), c_bb, c_ba, pl.ds(0, 3), pl.ds(10, 3)),
         (fields, y_before, y_after, pl.ds(0, 7), pl.ds(13, 7)),
     ])
     tiles.start()
     copies = (dm_copies(dm, y_before, y_after, sem, dm_ref, 28, 0, 4)
               + dm_copies(dm, y_before, y_after, sem, dm_ref, 0, 4, 4))
     start_all(copies)
-    x_sweep(q_ref, s_ref, 8, ((0, 0, 4), (10, 4, 4)), tiles.wait)
+    x_sweep(q_ref, s_ref, 8, ((0, 0, 4), (10, 4, 4)), TILES, tiles.wait, lambda t: t * 8)
     wait_all(copies)
-    yz_sweep(s_ref, dm_ref, o_ref, t_ref, 8, 0)
+    yz_sweep(s_ref, dm_ref, o_ref, t_ref, 8, lambda g: None, lambda g: None)
     outs = (out_density, out_momentum, out_energy)
     leaving = out_copies(o_ref, 8, outs, out_sem, 28, 0, 4) + out_copies(o_ref, 8, outs, out_sem, 0, 4, 4)
     leaving.append(sums_copy(t_ref, 0, 8, out_sums, out_sem))
@@ -399,7 +466,7 @@
     wait_all(leaving)
 
 
-def rest_kernel(dest, sums_inner, sums_middle, sums_outer, from_prev, from_next, send, w_ref, x_ref, y_ref, sem):
+def rest_kernel(dest, sums_inner, sums_outer, from_prev, from_next, send, w_ref, x_ref, y_ref, sem):
     def part(src, own, place, count):
         return pltpu.make_async_copy(src.at[pl.ds(own, count)], w_ref.at[pl.ds(place, count)], sem)
 
@@ -407,7 +474,7 @@
         part(from_prev, 0, 0, 2),
         part(sums_outer, 4, 2, 4),
         part(sums_inner, 0, 6, 6),
-        part(sums_middle, 2, 12, 6),
+        part(sums_inner, 18, 12, 6),
         part(sums_outer, 0, 18, 4),
         part(from_next, 0, 22, 2),
     ]
@@ -432,17 +499,17 @@
     return pltpu.CompilerParams(vmem_limit_bytes=VMEM_LIMIT)
 
 
-def cost(planes):
-    return pl.CostEstimate(flops=planes * 40_000_000_000, bytes_accessed=planes * 600_000, transcendentals=0)
-
-
-def main_scratch(planes, held, sums):
+def cost(micros):
+    return pl.CostEstimate(flops=int(micros * COST), bytes_accessed=0, transcendentals=0)
+
+
+def main_scratch(planes, held, rows):
     return [
-        pltpu.VMEM((5, held, FRAME, NZ), F32),
+        pltpu.VMEM((5, held, rows, NZ), F32),
         pltpu.VMEM((5 * planes * STRIDE, NZ), F32),
         pltpu.VMEM((5 * planes * STRIDE, NZ), F32),
         pltpu.VMEM((planes * STRIDE, NZ), F32),
-        pltpu.VMEM((sums * STRIDE, NZ), F32),
+        pltpu.VMEM((planes * STRIDE, NZ), F32),
     ]
 
 
@@ -462,80 +529,93 @@
     return lax.ppermute(value, axis, [(i, (i + by) % size) for i in range(size)])
 
 
+def diagonal(value, by_box, by_grp):
+    boxes, grps = lax.axis_size("box"), lax.axis_size("grp")
+    pairs = []
+    for i in range(boxes):
+        for j in range(grps):
+            pairs.append((i * grps + j, (i + by_box) % boxes * grps + (j + by_grp) % grps))
+    return lax.ppermute(value, ("box", "grp"), pairs)
+
+
 def body(density, momentum, energy, dm_density, box_dest):
     dest = box_dest[0, 0, :, 0]
-    fields = (density[None], momentum, energy[None])
-
-    def cut(arrays, planes, rows):
-        return jnp.concatenate([a[:, planes[0]:planes[1], rows[0]:rows[1]] for a in arrays], axis=0)
-
-    y_before = shifted(cut(fields + (dm_density[None],), (0, NX), (NY - 8, NY)), "grp", 1)
-    y_after = shifted(cut(fields + (dm_density[None],), (0, NX), (0, 8)), "grp", -1)
-    x_before = shifted(cut(fields, (NX - 3, NX), (0, NY)), "box", 1)
-    x_after = shifted(cut(fields, (0, 3), (0, NY)), "box", -1)
+    fields = (density, momentum, energy)
+    halo_shapes = (shape(6, NX, 8, NZ),) * 2 + (shape(5, 3, NY, NZ),) * 2 + (shape(5, 3, 8, NZ),) * 4
+    y_last, y_first, x_last, x_first, c_ll, c_lf, c_fl, c_ff = pl.pallas_call(
+        pack_kernel,
+        out_shape=halo_shapes,
+        in_specs=[ANY] * 4,
+        out_specs=[ANY] * 8,
+        scratch_shapes=[pltpu.SemaphoreType.DMA],
+        cost_estimate=cost(2),
+        name="pack",
+    )(density, momentum, energy, dm_density)
+    y_before = shifted(y_last, "grp", 1)
+    y_after = shifted(y_first, "grp", -1)
+    x_before = shifted(x_last, "box", 1)
+    x_after = shifted(x_first, "box", -1)
+    c_bb = diagonal(c_ll, 1, 1)
+    c_ba = diagonal(c_lf, 1, -1)
+    c_ab = diagonal(c_fl, -1, 1)
+    c_aa = diagonal(c_ff, -1, -1)
+
+    swept = pl.pallas_call(
+        x_kernel,
+        out_shape=shape(5, WIDE, NY, NZ),
+        in_specs=[ANY] * 3,
+        out_specs=ANY,
+        scratch_shapes=[
+            pltpu.VMEM((5, WIDE + 6, NY, NZ), F32), pltpu.VMEM((5, WIDE, NY, NZ), F32),
+            pltpu.SemaphoreType.DMA((NY // 8,)), pltpu.SemaphoreType.DMA],
+        compiler_params=params(),
+        cost_estimate=cost(9),
+        name="x_own",
+    )(*fields)
 
     def exchange(send, planes):
         return lax.all_to_all(send.reshape(16, 2, planes, 1024), "box", split_axis=0, concat_axis=0, tiled=True)
 
     inner = pl.pallas_call(
         inner_kernel,
-        out_shape=FIELD_SHAPES + (shape(16, FRAME, NZ), shape(32, 8, 1024)),
-        in_specs=[SMEM] + [ANY] * 6,
+        out_shape=FIELD_SHAPES + (shape(WIDE, FRAME, NZ), shape(32, 16, 1024)),
+        in_specs=[SMEM] + [ANY] * 4,
         out_specs=[ANY] * 4 + [VMEM],
-        scratch_shapes=main_scratch(16, 22, 16) + smooth_scratch() + semaphores(),
+        scratch_shapes=main_scratch(WIDE, WIDE + 6, 16) + smooth_scratch() + semaphores(),
         compiler_params=params(),
-        cost_estimate=cost(16),
+        cost_estimate=cost(33),
         name="inner",
-    )(dest, density, momentum, energy, dm_density, y_before, y_after)
+    )(dest, swept, dm_density, y_before, y_after)
     *made, sums_inner, send_inner = inner
-    got_inner = exchange(send_inner, 8)
-
-    x_before, x_after, sums_inner = lax.optimization_barrier((x_before, x_after, sums_inner))
-    x_both = jnp.concatenate([x_after, x_before], axis=1)
-    c_before = shifted(x_both[:, :, NY - 8:], "grp", 1)
-    c_after = shifted(x_both[:, :, :8], "grp", -1)
-    middle = pl.pallas_call(
-        middle_kernel,
-        out_shape=FIELD_SHAPES + (shape(8, FRAME, NZ), shape(32, 8, 1024)),
-        in_specs=[SMEM] + [ANY] * 10,
-        out_specs=[ANY] * 4 + [VMEM],
-        scratch_shapes=main_scratch(8, 14, 14) + smooth_scratch() + semaphores(),
-        input_output_aliases={8: 0, 9: 1, 10: 2},
-        compiler_params=params(),
-        cost_estimate=cost(8),
-        name="middle",
-    )(dest, density, momentum, energy, dm_density, y_before, y_after, sums_inner, *made)
-    *made, sums_middle, send_middle = middle
-    send_middle, got_inner = lax.optimization_barrier((send_middle, got_inner))
-    got_middle = exchange(send_middle, 8)
+    got_inner = exchange(send_inner, 16)
 
     outer = pl.pallas_call(
         outer_kernel,
         out_shape=FIELD_SHAPES + (shape(8, FRAME, NZ), shape(2, FRAME, NZ), shape(2, FRAME, NZ)),
-        in_specs=[ANY] * 13,
+        in_specs=[ANY] * 15,
         out_specs=[ANY] * 6,
-        scratch_shapes=main_scratch(8, 20, 8) + semaphores(),
-        input_output_aliases={10: 0, 11: 1, 12: 2},
+        scratch_shapes=main_scratch(8, 20, FRAME) + semaphores(),
+        input_output_aliases={12: 0, 13: 1, 14: 2},
         compiler_params=params(),
-        cost_estimate=cost(8),
+        cost_estimate=cost(14),
         name="outer",
-    )(density, momentum, energy, dm_density, y_before, y_after, x_before, x_after, c_before, c_after, *made)
+    )(*fields, dm_density, y_before, y_after, x_before, x_after, c_bb, c_ba, c_ab, c_aa, *made)
     new_density, new_momentum, new_energy, sums_outer, to_next, to_prev = outer
     from_prev = shifted(to_next, "box", 1)
     from_next = shifted(to_prev, "box", -1)
     send_rest = pl.pallas_call(
         rest_kernel,
         out_shape=shape(32, 16, 1024),
-        in_specs=[SMEM] + [ANY] * 5,
+        in_specs=[SMEM] + [ANY] * 4,
         out_specs=VMEM,
         scratch_shapes=[pltpu.VMEM((24, FRAME, NZ), F32)] + smooth_scratch() + [pltpu.SemaphoreType.DMA],
         compiler_params=params(),
-        cost_estimate=cost(2),
+        cost_estimate=cost(5),
         name="rest",
-    )(dest, sums_inner, sums_middle, sums_outer, from_prev, from_next)
-    send_rest, got_middle = lax.optimization_barrier((send_rest, got_middle))
+    )(dest, sums_inner, sums_outer, from_prev, from_next)
+    send_rest, got_inner = lax.optimization_barrier((send_rest, got_inner))
     got_rest = exchange(send_rest, 16)
-    kd = jnp.concatenate([got_rest[:, :, :8], got_inner, got_middle, got_rest[:, :, 8:]], axis=2)
+    kd = jnp.concatenate([got_rest[:, :, :8], got_inner, got_rest[:, :, 8:]], axis=2)
     return (new_density, new_momentum, new_energy, kd[None, None])
 
 

time: 156 us -> 240 us (1.54)
  Pallas kernels: 64.4 us -> 163 us
  local copies, waits for them, and re-layouts: 10.8 us -> 1.4 us
  waiting for transfers between devices: 15.5 us -> 12.3 us
  other arithmetic: 5.59 us -> 2.55 us
    pallas_call x2 -> x3, Pallas kernels: 44.7 us -> 143 us  [the longest x1 101 us: body(): pl.pallas_call(pack_kernel, out_shape=halo_shapes, in_specs=[ANY] * 4, ou...]
    all_to_all x2 -> x1, waiting for transfers between devices: 15.5 us -> 0.01 us  [exchange(): lax.all_to_all(send.reshape(16, 2, planes, 1024), 'box', split_axis=0, co...]
    ppermute x8 -> x6, waiting for transfers between devices: 0.02 us -> 12.2 us  [shifted(): lax.ppermute(value, axis, [(i, (i + by) % size) for i in range(size)])]
    ppermute x0 -> x4, starting transfers between devices: none -> 7.13 us  [diagonal(): return lax.ppermute(value, ('box', 'grp'), pairs)]
    all_to_all x2 -> x1, starting transfers between devices: 10.8 us -> 3.73 us  [exchange(): lax.all_to_all(send.reshape(16, 2, planes, 1024), 'box', split_axis=0, co...]
    slice x6 -> x0, local copies, waits for them, and re-layouts: 6.39 us -> none  [the longest x5 5.68 us: cut(): a[:, planes[0]:planes[1], rows[0]:rows[1]]]
    ppermute x8 -> x6, starting transfers between devices: 14.5 us -> 13.3 us  [shifted(): lax.ppermute(value, axis, [(i, (i + by) % size) for i in range(size)])]
  transfers between devices with their start and end apart: 10 -> 11, of which waited for: 1 -> 2; matrix products, arithmetic and copies ran while one was open for 5% -> 0% of each run, Pallas kernels for 42% -> 26%
where the time goes in v3:
time: 240 us; the launch traced here: 239 us
  Pallas kernels  163 us (68%)
  blocking collectives  35.1 us (15%)
  starting transfers between devices  24.1 us (10%)
  waiting for transfers between devices  12.3 us (5%)
  other arithmetic  2.55 us (1%)
    pallas_call x1, Pallas kernels, body(): pl.pallas_call(pack_kernel, out_shape=halo_shapes, in_specs=[ANY] * 4, ou...  101 us
    all_to_all x1, blocking collectives, exchange(): lax.all_to_all(send.reshape(16, 2, planes, 1024), 'box', split_axis=0, co...  35.1 us
    pallas_call x1, Pallas kernels, body(): pl.pallas_call(inner_kernel, out_shape=FIELD_SHAPES + (shape(WIDE, FRAME,...  32.2 us
    pallas_call x1, Pallas kernels, body(): pl.pallas_call(outer_kernel, out_shape=FIELD_SHAPES + (shape(8, FRAME, NZ...  15.2 us
    ppermute x6, starting transfers between devices, shifted(): lax.ppermute(value, axis, [(i, (i + by) % size) for i in range(size)])  13.3 us
    ppermute x6, waiting for transfers between devices, shifted(): lax.ppermute(value, axis, [(i, (i + by) % size) for i in range(size)])  12.2 us
    pallas_call x1, Pallas kernels, body(): pl.pallas_call(x_kernel, out_shape=shape(5, WIDE, NY, NZ), in_specs=[ANY]...  9.99 us
    ppermute x4, starting transfers between devices, diagonal(): return lax.ppermute(value, ('box', 'grp'), pairs)  7.13 us
  transfers between devices with their start and end apart: 11, of which 2 were waited for; matrix products, arithmetic and copies ran while one was open for 0% of the time, Pallas kernels for 26%

profile of v3, /device:TPU:32, one launch (start us, length us, event | category | flops | bytes accessed | tf_op | source)
XLA Modules:
  0.0 239.1 jit_solution(11891069630070280210)
XLA Ops:
  0.6 100.9 %pack.1 = (f32[6,32,8,128]{3,2,1,0:T(8,128)}, f32[6,32,8,128]{3,2,1,0:T(8,128)}, f32[5,3,96,128]{3,2,1,0:T(8,128)}, f32[5,3,96,128]{3,2,1,0:T(8,128)}, f32[5,3,8...) custom-call(f32[32,96,128]{2,1,0:T(8,128)} %density.5, ...), custom_call_target="tpu_custom_call" | custom-call | flops 2200000000 | tf_op jit(solution)/shard_map/pack/pallas_call | solution.py:545
  101.5 1.0 collective-permute-start.4
  102.5 2.7 %collective-permute-start.5 = (f32[5,3,8,128]{3,2,1,0:T(8,128)}, f32[5,3,8,128]{3,2,1,0:T(8,128)S(1)}, u32[]{:S(2)}, u32[]{:S(2)}) collective-permute-start(f32[5,3,8,128]{3,2,1,0:T(8,128)} %get-tuple-element.30), channel_id=1, source_target_pairs={{0,15},{1,8},{2,9},{3,10},{4,11},{5,12},{6,13},{7,14},{8,23},{9,16... | collective-permute-start | bytes 184328 | tf_op jit(solution)/shard_map/ppermute | solution.py:538
  105.2 2.8 %collective-permute-start.6 = (f32[5,3,8,128]{3,2,1,0:T(8,128)}, f32[5,3,8,128]{3,2,1,0:T(8,128)S(1)}, u32[]{:S(2)}, u32[]{:S(2)}) collective-permute-start(f32[5,3,8,128]{3,2,1,0:T(8,128)} %get-tuple-element.31), channel_id=1, source_target_pairs={{0,121},{1,122},{2,123},{3,124},{4,125},{5,126},{6,127},{7,120},{8... | collective-permute-start | bytes 184328 | tf_op jit(solution)/shard_map/ppermute | solution.py:538
  108.0 2.5 %collective-permute-start = (f32[6,32,8,128]{3,2,1,0:T(8,128)}, f32[6,32,8,128]{3,2,1,0:T(8,128)S(1)}, u32[]{:S(2)}, u32[]{:S(2)}) collective-permute-start(f32[6,32,8,128]{3,2,1,0:T(8,128)} %get-tuple-element.25), channel_id=1, source_target_pairs={{0,1},{1,2},{2,3},{3,4},{4,5},{5,6},{6,7},{7,0},{8,9},{9,10},{10,1... | collective-permute-start | bytes 2359304 | tf_op jit(solution)/shard_map/ppermute | solution.py:529
  110.5 0.0 copy-start.7
  110.5 0.0 collective-permute-start.1
  110.5 10.0 %x_own.1.swept = f32[5,24,96,128]{3,2,1,0:T(8,128)} custom-call(f32[32,96,128]{2,1,0:T(8,128)} %density.5, f32[3,32,96,128]{3,2,1,0:T(8,128)} %momentum.5, f32[32,96,128]{2,1,0:T(8,128)} %energy.5), custom_call_target="tpu_custom_call" | custom-call | flops 9900000256 | tf_op jit(solution)/shard_map/x_own/pallas_call | solution.py:563
  120.5 0.0 collective-permute-done.4.c_bb
  120.5 0.0 copy-start.4
  120.5 0.0 copy-done.7
  120.5 0.6 collective-permute-start.7
  121.2 0.0 collective-permute-done.y_before
  121.2 0.0 copy-start
  121.2 1.1 collective-permute-start.2
  122.3 0.0 collective-permute-done.1.y_after
  122.3 0.0 copy-start.1
  122.3 4.3 %collective-permute-start.3 = (f32[5,3,96,128]{3,2,1,0:T(8,128)}, f32[5,3,96,128]{3,2,1,0:T(8,128)}, u32[]{:S(2)}, u32[]{:S(2)}) collective-permute-start(f32[5,3,96,128]{3,2,1,0:T(8,128)} %get-tuple-element.28), channel_id=1, source_target_pairs={{0,120},{8,0},{16,8},{24,16},{32,24},{40,32},{48,40},{56,48},{64,5... | collective-permute-start | bytes 2211848 | tf_op jit(solution)/shard_map/ppermute | solution.py:529
  126.6 0.0 copy-done
  126.6 0.0 copy-done.1
  126.6 32.2 %inner.1 = (f32[32,96,128]{2,1,0:T(8,128)}, f32[3,32,96,128]{3,2,1,0:T(8,128)}, f32[32,96,128]{2,1,0:T(8,128)}, f32[24,112,128]{2,1,0:T(8,128)}, f32[32,16,1024]{2,1,0:T(8,128)}) custom-call(s32[12]{0:T(128)} %bitcast.7, f32[5,24,96,128]{3,2,1,0:T(8,128)} %x_own.1.swept, f32[32,96,128]{2,1,0:T(8,128)} %dm.5, f32[6,32,8,128]{3,2,1,0:T(8,128)} %copy-done, ...), custom_call_target="tpu_custom_call" | custom-call | flops 36300001280 | tf_op jit(solution)/shard_map/inner/pallas_call | solution.py:579
  158.8 0.0 copy-done.4
  158.8 3.7 %all-to-all-start = ((f32[16,2,16,1024]{3,2,1,0:T(8,128)}), f32[16,2,16,1024]{3,2,1,0:T(8,128)S(1)}, u32[]{:S(2)}, u32[]{:S(2)}) async-start(f32[16,2,16,1024]{3,2,1,0:T(8,128)} %bitcast.5), calls=%async_computation | async-start | bytes 4194304 | tf_op jit(solution)/shard_map/all_to_all | solution.py:577
  162.6 0.0 collective-permute-done.5.c_ba
  162.6 0.0 copy-start.5
  162.6 0.0 collective-permute-done.6.c_ab
  162.6 0.0 copy-start.6
  162.6 0.0 collective-permute-done.7.c_aa
  162.6 0.0 copy-start.8
  162.6 0.0 collective-permute-done.2.x_before
  162.6 0.0 collective-permute-done.3.x_after
  162.6 0.6 copy-done.5
  163.2 0.0 copy-done.6
  163.2 0.0 copy-done.8
  163.2 15.2 %outer.1 = (f32[32,96,128]{2,1,0:T(8,128)}, f32[3,32,96,128]{3,2,1,0:T(8,128)}, f32[32,96,128]{2,1,0:T(8,128)}, f32[8,112,128]{2,1,0:T(8,128)}, f32[2,112,128]{2,1,0:T(8,128)}, /*index=5*/f32[2,112,128]{2,1,0:T(8,128)}) custom-call(f32[32,96,128]{2,1,0:T(8,128)} %density.5, ...), custom_call_target="tpu_custom_call", output_to_operand_aliasing={{0}: (12, {}), {1}: (13, {}), {2}: (14, {})} | custom-call | flops 15399999488 | tf_op jit(solution)/shard_map/outer/pallas_call | solution.py:592
  178.5 1.9 collective-permute-start.8
  180.3 3.5 %collective-permute-start.9 = (f32[2,112,128]{2,1,0:T(8,128)}, f32[2,112,128]{2,1,0:T(8,128)S(1)}, u32[]{:S(2)}, u32[]{:S(2)}) collective-permute-start(f32[2,112,128]{2,1,0:T(8,128)} %get-tuple-element.42), channel_id=1, source_target_pairs={{0,120},{8,0},{16,8},{24,16},{32,24},{40,32},{48,40},{56,48},{64,5... | collective-permute-start | bytes 344072 | tf_op jit(solution)/shard_map/ppermute | solution.py:529
  183.9 9.2 %collective-permute-done.8.from_prev = f32[2,112,128]{2,1,0:T(8,128)S(1)} collective-permute-done((f32[2,112,128]{2,1,0:T(8,128)}, f32[2,112,128]{2,1,0:T(8,128)S(1)}, u32[]{:S(2)}, u32[]{:S(2)}) %collective-permute-start.8) | collective-permute-done | bytes 114720 | tf_op jit(solution)/shard_map/ppermute | solution.py:529
  193.1 0.0 copy-start.2
  193.1 3.0 %collective-permute-done.9.from_next = f32[2,112,128]{2,1,0:T(8,128)S(1)} collective-permute-done((f32[2,112,128]{2,1,0:T(8,128)}, f32[2,112,128]{2,1,0:T(8,128)S(1)}, u32[]{:S(2)}, u32[]{:S(2)}) %collective-permute-start.9) | collective-permute-done | bytes 114720 | tf_op jit(solution)/shard_map/ppermute | solution.py:529
  196.1 0.0 copy-start.3
  196.1 0.0 copy-done.2
  196.1 0.6 copy-done.3
  196.8 4.5 %rest.1 = f32[32,16,1024]{2,1,0:T(8,128)} custom-call(s32[12]{0:T(128)} %bitcast.8, f32[24,112,128]{2,1,0:T(8,128)} %get-tuple-element.39.sums_inner, f32[8,112,128]{2,1,0:T(8,128)} %get-tuple-element.40.sums_outer, f32[2,112,128]{2,1,0:T(8,128)} %copy-done.2, f32[2,112,128]{2,1,0:T(8,128)} %copy-done.3), custom_call_target="tpu_custom_call" | custom-call | flops 5500000256 | tf_op jit(solution)/shard_map/rest/pallas_call | solution.py:606
  201.3 0.0 all-to-all-done
  201.3 35.1 %all_to_all.10 = f32[16,2,16,1024]{3,2,1,0:T(8,128)S(1)} all-to-all(f32[16,2,16,1024]{3,2,1,0:T(8,128)} %bitcast.6), channel_id=1, replica_groups=mesh['box'=16,'grp'=8] {'box'}, dimensions={0} | all-to-all | bytes 4194304 | tf_op jit(solution)/shard_map/all_to_all | solution.py:577
  236.4 0.1 fusion
  236.5 2.5 %maximum_bitcast_fusion = f32[1,1,16,2,32,1024]{5,4,3,2,1,0:T(8,128)} fusion(f32[16,2,8,1024]{3,2,1,0:T(8,128)S(1)} %get-tuple-element.47, f32[16,2,16,1024]{3,2,1,0:T(8,128)S(1)} %all-to-all-done, f32[16,2,8,1024]{3,2,1,0:T(8,128)S(1)} %get-tuple-element.46), kind=kLoop, calls=%fused_computation | loop fusion | flops 2097152 | bytes 8388608 | tf_op jit(solution)/shard_map/broadcast_in_dim | solution.py:619
Async XLA Ops:
  101.5 19.0 %collective-permute-start.4 = (f32[5,3,8,128]{3,2,1,0:T(8,128)}, f32[5,3,8,128]{3,2,1,0:T(8,128)S(1)}, u32[]{:S(2)}, u32[]{:S(2)}) collective-permute-start(f32[5,3,8,128]{3,2,1,0:T(8,128)} %get-tuple-element.29), channel_id=1, source_target_pairs={{0,9},{1,10},{2,11},{3,12},{4,13},{5,14},{6,15},{7,8},{8,17},{9,18... | collective-permute-start | bytes 184328 | tf_op jit(solution)/shard_map/ppermute | solution.py:538
  102.5 60.0 %collective-permute-start.5 = (f32[5,3,8,128]{3,2,1,0:T(8,128)}, f32[5,3,8,128]{3,2,1,0:T(8,128)S(1)}, u32[]{:S(2)}, u32[]{:S(2)}) collective-permute-start(f32[5,3,8,128]{3,2,1,0:T(8,128)} %get-tuple-element.30), channel_id=1, source_target_pairs={{0,15},{1,8},{2,9},{3,10},{4,11},{5,12},{6,13},{7,14},{8,23},{9,16... | collective-permute-start | bytes 184328 | tf_op jit(solution)/shard_map/ppermute | solution.py:538
  105.2 57.4 %collective-permute-start.6 = (f32[5,3,8,128]{3,2,1,0:T(8,128)}, f32[5,3,8,128]{3,2,1,0:T(8,128)S(1)}, u32[]{:S(2)}, u32[]{:S(2)}) collective-permute-start(f32[5,3,8,128]{3,2,1,0:T(8,128)} %get-tuple-element.31), channel_id=1, source_target_pairs={{0,121},{1,122},{2,123},{3,124},{4,125},{5,126},{6,127},{7,120},{8... | collective-permute-start | bytes 184328 | tf_op jit(solution)/shard_map/ppermute | solution.py:538
  108.0 13.2 %collective-permute-start = (f32[6,32,8,128]{3,2,1,0:T(8,128)}, f32[6,32,8,128]{3,2,1,0:T(8,128)S(1)}, u32[]{:S(2)}, u32[]{:S(2)}) collective-permute-start(f32[6,32,8,128]{3,2,1,0:T(8,128)} %get-tuple-element.25), channel_id=1, source_target_pairs={{0,1},{1,2},{2,3},{3,4},{4,5},{5,6},{6,7},{7,0},{8,9},{9,10},{10,1... | collective-permute-start | bytes 2359304 | tf_op jit(solution)/shard_map/ppermute | solution.py:529
  110.5 10.0 %copy-start.7 = (f32[5,3,8,128]{3,2,1,0:T(8,128)S(1)}, f32[5,3,8,128]{3,2,1,0:T(8,128)}, u32[]{:S(2)}) copy-start(f32[5,3,8,128]{3,2,1,0:T(8,128)} %get-tuple-element.32) | copy-start | bytes 184324
  110.5 11.8 %collective-permute-start.1 = (f32[6,32,8,128]{3,2,1,0:T(8,128)}, f32[6,32,8,128]{3,2,1,0:T(8,128)S(1)}, u32[]{:S(2)}, u32[]{:S(2)}) collective-permute-start(f32[6,32,8,128]{3,2,1,0:T(8,128)} %get-tuple-element.26), channel_id=1, source_target_pairs={{0,7},{1,0},{2,1},{3,2},{4,3},{5,4},{6,5},{7,6},{8,15},{9,8},{10,9... | collective-permute-start | bytes 2359304 | tf_op jit(solution)/shard_map/ppermute | solution.py:529
  120.5 38.3 %copy-start.4 = (f32[5,3,8,128]{3,2,1,0:T(8,128)}, f32[5,3,8,128]{3,2,1,0:T(8,128)S(1)}, u32[]{:S(2)}) copy-start(f32[5,3,8,128]{3,2,1,0:T(8,128)S(1)} %collective-permute-done.4.c_bb) | copy-start | bytes 184324
  120.5 42.1 %collective-permute-start.7 = (f32[5,3,8,128]{3,2,1,0:T(8,128)S(1)}, f32[5,3,8,128]{3,2,1,0:T(8,128)S(1)}, u32[]{:S(2)}, u32[]{:S(2)}) collective-permute-start(f32[5,3,8,128]{3,2,1,0:T(8,128)S(1)} %copy-done.7), channel_id=1, source_target_pairs={{0,127},{1,120},{2,121},{3,122},{4,123},{5,124},{6,125},{7,126},{8... | collective-permute-start | bytes 184328 | tf_op jit(solution)/shard_map/ppermute | solution.py:538
  121.2 5.4 %copy-start = (f32[6,32,8,128]{3,2,1,0:T(8,128)}, f32[6,32,8,128]{3,2,1,0:T(8,128)S(1)}, u32[]{:S(2)}) copy-start(f32[6,32,8,128]{3,2,1,0:T(8,128)S(1)} %collective-permute-done.y_before) | copy-start | bytes 2359300
  121.2 41.4 %collective-permute-start.2 = (f32[5,3,96,128]{3,2,1,0:T(8,128)}, f32[5,3,96,128]{3,2,1,0:T(8,128)}, u32[]{:S(2)}, u32[]{:S(2)}) collective-permute-start(f32[5,3,96,128]{3,2,1,0:T(8,128)} %get-tuple-element.27), channel_id=1, source_target_pairs={{0,8},{8,16},{16,24},{24,32},{32,40},{40,48},{48,56},{56,64},{64,7... | collective-permute-start | bytes 2211848 | tf_op jit(solution)/shard_map/ppermute | solution.py:529
  122.3 4.3 %copy-start.1 = (f32[6,32,8,128]{3,2,1,0:T(8,128)}, f32[6,32,8,128]{3,2,1,0:T(8,128)S(1)}, u32[]{:S(2)}) copy-start(f32[6,32,8,128]{3,2,1,0:T(8,128)S(1)} %collective-permute-done.1.y_after) | copy-start | bytes 2359300
  122.3 40.3 %collective-permute-start.3 = (f32[5,3,96,128]{3,2,1,0:T(8,128)}, f32[5,3,96,128]{3,2,1,0:T(8,128)}, u32[]{:S(2)}, u32[]{:S(2)}) collective-permute-start(f32[5,3,96,128]{3,2,1,0:T(8,128)} %get-tuple-element.28), channel_id=1, source_target_pairs={{0,120},{8,0},{16,8},{24,16},{32,24},{40,32},{48,40},{56,48},{64,5... | collective-permute-start | bytes 2211848 | tf_op jit(solution)/shard_map/ppermute | solution.py:529
  158.8 42.5 %all-to-all-start = ((f32[16,2,16,1024]{3,2,1,0:T(8,128)}), f32[16,2,16,1024]{3,2,1,0:T(8,128)S(1)}, u32[]{:S(2)}, u32[]{:S(2)}) async-start(f32[16,2,16,1024]{3,2,1,0:T(8,128)} %bitcast.5), calls=%async_computation | async-start | bytes 4194304 | tf_op jit(solution)/shard_map/all_to_all | solution.py:577
  162.6 0.6 copy-start.5
  162.6 0.6 copy-start.6
  162.6 0.6 copy-start.8
  178.5 14.7 %collective-permute-start.8 = (f32[2,112,128]{2,1,0:T(8,128)}, f32[2,112,128]{2,1,0:T(8,128)S(1)}, u32[]{:S(2)}, u32[]{:S(2)}) collective-permute-start(f32[2,112,128]{2,1,0:T(8,128)} %get-tuple-element.41), channel_id=1, source_target_pairs={{0,8},{8,16},{16,24},{24,32},{32,40},{40,48},{48,56},{56,64},{64,7... | collective-permute-start | bytes 344072 | tf_op jit(solution)/shard_map/ppermute | solution.py:529
  180.3 15.8 %collective-permute-start.9 = (f32[2,112,128]{2,1,0:T(8,128)}, f32[2,112,128]{2,1,0:T(8,128)S(1)}, u32[]{:S(2)}, u32[]{:S(2)}) collective-permute-start(f32[2,112,128]{2,1,0:T(8,128)} %get-tuple-element.42), channel_id=1, source_target_pairs={{0,120},{8,0},{16,8},{24,16},{32,24},{40,32},{48,40},{56,48},{64,5... | collective-permute-start | bytes 344072 | tf_op jit(solution)/shard_map/ppermute | solution.py:529
  193.1 3.0 %copy-start.2 = (f32[2,112,128]{2,1,0:T(8,128)}, f32[2,112,128]{2,1,0:T(8,128)S(1)}, u32[]{:S(2)}) copy-start(f32[2,112,128]{2,1,0:T(8,128)S(1)} %collective-permute-done.8.from_prev) | copy-start | bytes 344068
  196.1 0.6 copy-start.3

commit v4 on v3

--- a/solution.py
+++ b/solution.py
@@ -546,8 +546,9 @@
         pack_kernel,
         out_shape=halo_shapes,
         in_specs=[ANY] * 4,
-        out_specs=[ANY] * 8,
+        out_specs=[VMEM] * 8,
         scratch_shapes=[pltpu.SemaphoreType.DMA],
+        compiler_params=params(),
         cost_estimate=cost(2),
         name="pack",
     )(density, momentum, energy, dm_density)

time: 240 us -> 143 us (0.60)
  Pallas kernels: 163 us -> 65.7 us
    pallas_call x1, Pallas kernels: 101 us -> 3.73 us  [body(): pl.pallas_call(pack_kernel, out_shape=halo_shapes, in_specs=[ANY] * 4, ou...]
  transfers between devices with their start and end apart: 11 -> 11, of which waited for: 2 -> 2; matrix products, arithmetic and copies ran while one was open for 0% -> 0% of each run, Pallas kernels for 26% -> 44%
where the time goes in v4:
time: 143 us; the launch traced here: 142 us
  Pallas kernels  65.7 us (46%)
  blocking collectives  35.1 us (25%)
  starting transfers between devices  24.1 us (17%)
  waiting for transfers between devices  12.3 us (9%)
  other arithmetic  2.55 us (2%)
    all_to_all x1, blocking collectives, exchange(): lax.all_to_all(send.reshape(16, 2, planes, 1024), 'box', split_axis=0, co...  35.1 us
    pallas_call x1, Pallas kernels, body(): pl.pallas_call(inner_kernel, out_shape=FIELD_SHAPES + (shape(WIDE, FRAME,...  32.2 us
    pallas_call x1, Pallas kernels, body(): pl.pallas_call(outer_kernel, out_shape=FIELD_SHAPES + (shape(8, FRAME, NZ...  15.2 us
    ppermute x6, starting transfers between devices, shifted(): lax.ppermute(value, axis, [(i, (i + by) % size) for i in range(size)])  13.3 us
    ppermute x6, waiting for transfers between devices, shifted(): lax.ppermute(value, axis, [(i, (i + by) % size) for i in range(size)])  12.2 us
    pallas_call x1, Pallas kernels, body(): pl.pallas_call(x_kernel, out_shape=shape(5, WIDE, NY, NZ), in_specs=[ANY]...  9.99 us
    ppermute x4, starting transfers between devices, diagonal(): return lax.ppermute(value, ('box', 'grp'), pairs)  7.13 us
    pallas_call x1, Pallas kernels, body(): pl.pallas_call(rest_kernel, out_shape=shape(32, 16, 1024), in_specs=[SMEM...  4.51 us
  transfers between devices with their start and end apart: 11, of which 2 were waited for; matrix products, arithmetic and copies ran while one was open for 0% of the time, Pallas kernels for 44%

profile of v4, /device:TPU:32, one launch (start us, length us, event | category | flops | bytes accessed | tf_op | source)
XLA Modules:
  0.0 141.9 jit_solution(3139448684595329185)
XLA Ops:
  0.6 3.7 %pack.1 = (f32[6,32,8,128]{3,2,1,0:T(8,128)}, f32[6,32,8,128]{3,2,1,0:T(8,128)}, f32[5,3,96,128]{3,2,1,0:T(8,128)}, f32[5,3,96,128]{3,2,1,0:T(8,128)}, f32[5,3,8...) custom-call(f32[32,96,128]{2,1,0:T(8,128)} %density.5, ...), custom_call_target="tpu_custom_call" | custom-call | flops 2200000000 | tf_op jit(solution)/shard_map/pack/pallas_call | solution.py:545
  4.4 1.0 collective-permute-start.4
  5.4 2.7 %collective-permute-start.5 = (f32[5,3,8,128]{3,2,1,0:T(8,128)}, f32[5,3,8,128]{3,2,1,0:T(8,128)S(1)}, u32[]{:S(2)}, u32[]{:S(2)}) collective-permute-start(f32[5,3,8,128]{3,2,1,0:T(8,128)} %get-tuple-element.30), channel_id=1, source_target_pairs={{0,15},{1,8},{2,9},{3,10},{4,11},{5,12},{6,13},{7,14},{8,23},{9,16... | collective-permute-start | bytes 184328 | tf_op jit(solution)/shard_map/ppermute | solution.py:538
  8.0 2.8 %collective-permute-start.6 = (f32[5,3,8,128]{3,2,1,0:T(8,128)}, f32[5,3,8,128]{3,2,1,0:T(8,128)S(1)}, u32[]{:S(2)}, u32[]{:S(2)}) collective-permute-start(f32[5,3,8,128]{3,2,1,0:T(8,128)} %get-tuple-element.31), channel_id=1, source_target_pairs={{0,121},{1,122},{2,123},{3,124},{4,125},{5,126},{6,127},{7,120},{8... | collective-permute-start | bytes 184328 | tf_op jit(solution)/shard_map/ppermute | solution.py:538
  10.9 2.5 %collective-permute-start = (f32[6,32,8,128]{3,2,1,0:T(8,128)}, f32[6,32,8,128]{3,2,1,0:T(8,128)S(1)}, u32[]{:S(2)}, u32[]{:S(2)}) collective-permute-start(f32[6,32,8,128]{3,2,1,0:T(8,128)} %get-tuple-element.25), channel_id=1, source_target_pairs={{0,1},{1,2},{2,3},{3,4},{4,5},{5,6},{6,7},{7,0},{8,9},{9,10},{10,1... | collective-permute-start | bytes 2359304 | tf_op jit(solution)/shard_map/ppermute | solution.py:529
  13.4 0.0 copy-start.7
  13.4 0.0 collective-permute-start.1
  13.4 10.0 %x_own.1.swept = f32[5,24,96,128]{3,2,1,0:T(8,128)} custom-call(f32[32,96,128]{2,1,0:T(8,128)} %density.5, f32[3,32,96,128]{3,2,1,0:T(8,128)} %momentum.5, f32[32,96,128]{2,1,0:T(8,128)} %energy.5), custom_call_target="tpu_custom_call" | custom-call | flops 9900000256 | tf_op jit(solution)/shard_map/x_own/pallas_call | solution.py:564
  23.4 0.0 collective-permute-done.4.c_bb
  23.4 0.0 copy-start.4
  23.4 0.0 copy-done.7
  23.4 0.6 collective-permute-start.7
  24.0 0.0 collective-permute-done.y_before
  24.0 0.0 copy-start
  24.0 1.1 collective-permute-start.2
  25.1 0.0 collective-permute-done.1.y_after
  25.1 0.0 copy-start.1
  25.1 4.3 %collective-permute-start.3 = (f32[5,3,96,128]{3,2,1,0:T(8,128)}, f32[5,3,96,128]{3,2,1,0:T(8,128)}, u32[]{:S(2)}, u32[]{:S(2)}) collective-permute-start(f32[5,3,96,128]{3,2,1,0:T(8,128)} %get-tuple-element.28), channel_id=1, source_target_pairs={{0,120},{8,0},{16,8},{24,16},{32,24},{40,32},{48,40},{56,48},{64,5... | collective-permute-start | bytes 2211848 | tf_op jit(solution)/shard_map/ppermute | solution.py:529
  29.4 0.0 copy-done
  29.4 0.0 copy-done.1
  29.4 32.2 %inner.1 = (f32[32,96,128]{2,1,0:T(8,128)}, f32[3,32,96,128]{3,2,1,0:T(8,128)}, f32[32,96,128]{2,1,0:T(8,128)}, f32[24,112,128]{2,1,0:T(8,128)}, f32[32,16,1024]{2,1,0:T(8,128)}) custom-call(s32[12]{0:T(128)} %bitcast.7, f32[5,24,96,128]{3,2,1,0:T(8,128)} %x_own.1.swept, f32[32,96,128]{2,1,0:T(8,128)} %dm.5, f32[6,32,8,128]{3,2,1,0:T(8,128)} %copy-done, ...), custom_call_target="tpu_custom_call" | custom-call | flops 36300001280 | tf_op jit(solution)/shard_map/inner/pallas_call | solution.py:580
  61.7 0.0 copy-done.4
  61.7 3.7 %all-to-all-start = ((f32[16,2,16,1024]{3,2,1,0:T(8,128)}), f32[16,2,16,1024]{3,2,1,0:T(8,128)S(1)}, u32[]{:S(2)}, u32[]{:S(2)}) async-start(f32[16,2,16,1024]{3,2,1,0:T(8,128)} %bitcast.5), calls=%async_computation | async-start | bytes 4194304 | tf_op jit(solution)/shard_map/all_to_all | solution.py:578
  65.4 0.0 collective-permute-done.5.c_ba
  65.4 0.0 copy-start.5
  65.4 0.0 collective-permute-done.6.c_ab
  65.4 0.0 copy-start.6
  65.4 0.0 collective-permute-done.7.c_aa
  65.5 0.0 copy-start.8
  65.5 0.0 collective-permute-done.2.x_before
  65.5 0.0 collective-permute-done.3.x_after
  65.5 0.6 copy-done.5
  66.0 0.0 copy-done.6
  66.1 0.0 copy-done.8
  66.1 15.2 %outer.1 = (f32[32,96,128]{2,1,0:T(8,128)}, f32[3,32,96,128]{3,2,1,0:T(8,128)}, f32[32,96,128]{2,1,0:T(8,128)}, f32[8,112,128]{2,1,0:T(8,128)}, f32[2,112,128]{2,1,0:T(8,128)}, /*index=5*/f32[2,112,128]{2,1,0:T(8,128)}) custom-call(f32[32,96,128]{2,1,0:T(8,128)} %density.5, ...), custom_call_target="tpu_custom_call", output_to_operand_aliasing={{0}: (12, {}), {1}: (13, {}), {2}: (14, {})} | custom-call | flops 15399999488 | tf_op jit(solution)/shard_map/outer/pallas_call | solution.py:593
  81.3 1.9 %collective-permute-start.8 = (f32[2,112,128]{2,1,0:T(8,128)}, f32[2,112,128]{2,1,0:T(8,128)S(1)}, u32[]{:S(2)}, u32[]{:S(2)}) collective-permute-start(f32[2,112,128]{2,1,0:T(8,128)} %get-tuple-element.41), channel_id=1, source_target_pairs={{0,8},{8,16},{16,24},{24,32},{32,40},{40,48},{48,56},{56,64},{64,7... | collective-permute-start | bytes 344072 | tf_op jit(solution)/shard_map/ppermute | solution.py:529
  83.2 3.5 %collective-permute-start.9 = (f32[2,112,128]{2,1,0:T(8,128)}, f32[2,112,128]{2,1,0:T(8,128)S(1)}, u32[]{:S(2)}, u32[]{:S(2)}) collective-permute-start(f32[2,112,128]{2,1,0:T(8,128)} %get-tuple-element.42), channel_id=1, source_target_pairs={{0,120},{8,0},{16,8},{24,16},{32,24},{40,32},{48,40},{56,48},{64,5... | collective-permute-start | bytes 344072 | tf_op jit(solution)/shard_map/ppermute | solution.py:529
  86.7 9.2 %collective-permute-done.8.from_prev = f32[2,112,128]{2,1,0:T(8,128)S(1)} collective-permute-done((f32[2,112,128]{2,1,0:T(8,128)}, f32[2,112,128]{2,1,0:T(8,128)S(1)}, u32[]{:S(2)}, u32[]{:S(2)}) %collective-permute-start.8) | collective-permute-done | bytes 114720 | tf_op jit(solution)/shard_map/ppermute | solution.py:529
  96.0 0.0 copy-start.2
  96.0 3.0 %collective-permute-done.9.from_next = f32[2,112,128]{2,1,0:T(8,128)S(1)} collective-permute-done((f32[2,112,128]{2,1,0:T(8,128)}, f32[2,112,128]{2,1,0:T(8,128)S(1)}, u32[]{:S(2)}, u32[]{:S(2)}) %collective-permute-start.9) | collective-permute-done | bytes 114720 | tf_op jit(solution)/shard_map/ppermute | solution.py:529
  99.0 0.0 copy-start.3
  99.0 0.0 copy-done.2
  99.0 0.6 copy-done.3
  99.6 4.5 %rest.1 = f32[32,16,1024]{2,1,0:T(8,128)} custom-call(s32[12]{0:T(128)} %bitcast.8, f32[24,112,128]{2,1,0:T(8,128)} %get-tuple-element.39.sums_inner, f32[8,112,128]{2,1,0:T(8,128)} %get-tuple-element.40.sums_outer, f32[2,112,128]{2,1,0:T(8,128)} %copy-done.2, f32[2,112,128]{2,1,0:T(8,128)} %copy-done.3), custom_call_target="tpu_custom_call" | custom-call | flops 5500000256 | tf_op jit(solution)/shard_map/rest/pallas_call | solution.py:607
  104.1 0.0 all-to-all-done
  104.2 35.1 %all_to_all.10 = f32[16,2,16,1024]{3,2,1,0:T(8,128)S(1)} all-to-all(f32[16,2,16,1024]{3,2,1,0:T(8,128)} %bitcast.6), channel_id=1, replica_groups=mesh['box'=16,'grp'=8] {'box'}, dimensions={0} | all-to-all | bytes 4194304 | tf_op jit(solution)/shard_map/all_to_all | solution.py:578
  139.2 0.1 fusion
  139.4 2.5 %maximum_bitcast_fusion = f32[1,1,16,2,32,1024]{5,4,3,2,1,0:T(8,128)} fusion(f32[16,2,8,1024]{3,2,1,0:T(8,128)S(1)} %get-tuple-element.47, f32[16,2,16,1024]{3,2,1,0:T(8,128)S(1)} %all-to-all-done, f32[16,2,8,1024]{3,2,1,0:T(8,128)S(1)} %get-tuple-element.46), kind=kLoop, calls=%fused_computation | loop fusion | flops 2097152 | bytes 8388608 | tf_op jit(solution)/shard_map/broadcast_in_dim | solution.py:620
Async XLA Ops:
  4.4 19.0 %collective-permute-start.4 = (f32[5,3,8,128]{3,2,1,0:T(8,128)}, f32[5,3,8,128]{3,2,1,0:T(8,128)S(1)}, u32[]{:S(2)}, u32[]{:S(2)}) collective-permute-start(f32[5,3,8,128]{3,2,1,0:T(8,128)} %get-tuple-element.29), channel_id=1, source_target_pairs={{0,9},{1,10},{2,11},{3,12},{4,13},{5,14},{6,15},{7,8},{8,17},{9,18... | collective-permute-start | bytes 184328 | tf_op jit(solution)/shard_map/ppermute | solution.py:538
  5.4 60.0 %collective-permute-start.5 = (f32[5,3,8,128]{3,2,1,0:T(8,128)}, f32[5,3,8,128]{3,2,1,0:T(8,128)S(1)}, u32[]{:S(2)}, u32[]{:S(2)}) collective-permute-start(f32[5,3,8,128]{3,2,1,0:T(8,128)} %get-tuple-element.30), channel_id=1, source_target_pairs={{0,15},{1,8},{2,9},{3,10},{4,11},{5,12},{6,13},{7,14},{8,23},{9,16... | collective-permute-start | bytes 184328 | tf_op jit(solution)/shard_map/ppermute | solution.py:538
  8.0 57.4 %collective-permute-start.6 = (f32[5,3,8,128]{3,2,1,0:T(8,128)}, f32[5,3,8,128]{3,2,1,0:T(8,128)S(1)}, u32[]{:S(2)}, u32[]{:S(2)}) collective-permute-start(f32[5,3,8,128]{3,2,1,0:T(8,128)} %get-tuple-element.31), channel_id=1, source_target_pairs={{0,121},{1,122},{2,123},{3,124},{4,125},{5,126},{6,127},{7,120},{8... | collective-permute-start | bytes 184328 | tf_op jit(solution)/shard_map/ppermute | solution.py:538
  10.9 13.2 %collective-permute-start = (f32[6,32,8,128]{3,2,1,0:T(8,128)}, f32[6,32,8,128]{3,2,1,0:T(8,128)S(1)}, u32[]{:S(2)}, u32[]{:S(2)}) collective-permute-start(f32[6,32,8,128]{3,2,1,0:T(8,128)} %get-tuple-element.25), channel_id=1, source_target_pairs={{0,1},{1,2},{2,3},{3,4},{4,5},{5,6},{6,7},{7,0},{8,9},{9,10},{10,1... | collective-permute-start | bytes 2359304 | tf_op jit(solution)/shard_map/ppermute | solution.py:529
  13.4 10.0 %copy-start.7 = (f32[5,3,8,128]{3,2,1,0:T(8,128)S(1)}, f32[5,3,8,128]{3,2,1,0:T(8,128)}, u32[]{:S(2)}) copy-start(f32[5,3,8,128]{3,2,1,0:T(8,128)} %get-tuple-element.32) | copy-start | bytes 184324
  13.4 11.8 %collective-permute-start.1 = (f32[6,32,8,128]{3,2,1,0:T(8,128)}, f32[6,32,8,128]{3,2,1,0:T(8,128)S(1)}, u32[]{:S(2)}, u32[]{:S(2)}) collective-permute-start(f32[6,32,8,128]{3,2,1,0:T(8,128)} %get-tuple-element.26), channel_id=1, source_target_pairs={{0,7},{1,0},{2,1},{3,2},{4,3},{5,4},{6,5},{7,6},{8,15},{9,8},{10,9... | collective-permute-start | bytes 2359304 | tf_op jit(solution)/shard_map/ppermute | solution.py:529
  23.4 38.3 %copy-start.4 = (f32[5,3,8,128]{3,2,1,0:T(8,128)}, f32[5,3,8,128]{3,2,1,0:T(8,128)S(1)}, u32[]{:S(2)}) copy-start(f32[5,3,8,128]{3,2,1,0:T(8,128)S(1)} %collective-permute-done.4.c_bb) | copy-start | bytes 184324
  23.4 42.1 %collective-permute-start.7 = (f32[5,3,8,128]{3,2,1,0:T(8,128)S(1)}, f32[5,3,8,128]{3,2,1,0:T(8,128)S(1)}, u32[]{:S(2)}, u32[]{:S(2)}) collective-permute-start(f32[5,3,8,128]{3,2,1,0:T(8,128)S(1)} %copy-done.7), channel_id=1, source_target_pairs={{0,127},{1,120},{2,121},{3,122},{4,123},{5,124},{6,125},{7,126},{8... | collective-permute-start | bytes 184328 | tf_op jit(solution)/shard_map/ppermute | solution.py:538
  24.0 5.4 %copy-start = (f32[6,32,8,128]{3,2,1,0:T(8,128)}, f32[6,32,8,128]{3,2,1,0:T(8,128)S(1)}, u32[]{:S(2)}) copy-start(f32[6,32,8,128]{3,2,1,0:T(8,128)S(1)} %collective-permute-done.y_before) | copy-start | bytes 2359300
  24.0 41.4 %collective-permute-start.2 = (f32[5,3,96,128]{3,2,1,0:T(8,128)}, f32[5,3,96,128]{3,2,1,0:T(8,128)}, u32[]{:S(2)}, u32[]{:S(2)}) collective-permute-start(f32[5,3,96,128]{3,2,1,0:T(8,128)} %get-tuple-element.27), channel_id=1, source_target_pairs={{0,8},{8,16},{16,24},{24,32},{32,40},{40,48},{48,56},{56,64},{64,7... | collective-permute-start | bytes 2211848 | tf_op jit(solution)/shard_map/ppermute | solution.py:529
  25.1 4.3 %copy-start.1 = (f32[6,32,8,128]{3,2,1,0:T(8,128)}, f32[6,32,8,128]{3,2,1,0:T(8,128)S(1)}, u32[]{:S(2)}) copy-start(f32[6,32,8,128]{3,2,1,0:T(8,128)S(1)} %collective-permute-done.1.y_after) | copy-start | bytes 2359300
  25.1 40.3 %collective-permute-start.3 = (f32[5,3,96,128]{3,2,1,0:T(8,128)}, f32[5,3,96,128]{3,2,1,0:T(8,128)}, u32[]{:S(2)}, u32[]{:S(2)}) collective-permute-start(f32[5,3,96,128]{3,2,1,0:T(8,128)} %get-tuple-element.28), channel_id=1, source_target_pairs={{0,120},{8,0},{16,8},{24,16},{32,24},{40,32},{48,40},{56,48},{64,5... | collective-permute-start | bytes 2211848 | tf_op jit(solution)/shard_map/ppermute | solution.py:529
  61.7 42.5 %all-to-all-start = ((f32[16,2,16,1024]{3,2,1,0:T(8,128)}), f32[16,2,16,1024]{3,2,1,0:T(8,128)S(1)}, u32[]{:S(2)}, u32[]{:S(2)}) async-start(f32[16,2,16,1024]{3,2,1,0:T(8,128)} %bitcast.5), calls=%async_computation | async-start | bytes 4194304 | tf_op jit(solution)/shard_map/all_to_all | solution.py:578
  65.4 0.6 copy-start.5
  65.4 0.6 copy-start.6
  65.5 0.6 copy-start.8
  81.3 14.7 %collective-permute-start.8 = (f32[2,112,128]{2,1,0:T(8,128)}, f32[2,112,128]{2,1,0:T(8,128)S(1)}, u32[]{:S(2)}, u32[]{:S(2)}) collective-permute-start(f32[2,112,128]{2,1,0:T(8,128)} %get-tuple-element.41), channel_id=1, source_target_pairs={{0,8},{8,16},{16,24},{24,32},{32,40},{40,48},{48,56},{56,64},{64,7... | collective-permute-start | bytes 344072 | tf_op jit(solution)/shard_map/ppermute | solution.py:529
  83.2 15.8 %collective-permute-start.9 = (f32[2,112,128]{2,1,0:T(8,128)}, f32[2,112,128]{2,1,0:T(8,128)S(1)}, u32[]{:S(2)}, u32[]{:S(2)}) collective-permute-start(f32[2,112,128]{2,1,0:T(8,128)} %get-tuple-element.42), channel_id=1, source_target_pairs={{0,120},{8,0},{16,8},{24,16},{32,24},{40,32},{48,40},{56,48},{64,5... | collective-permute-start | bytes 344072 | tf_op jit(solution)/shard_map/ppermute | solution.py:529
  96.0 3.0 %copy-start.2 = (f32[2,112,128]{2,1,0:T(8,128)}, f32[2,112,128]{2,1,0:T(8,128)S(1)}, u32[]{:S(2)}) copy-start(f32[2,112,128]{2,1,0:T(8,128)S(1)} %collective-permute-done.8.from_prev) | copy-start | bytes 344068
  99.0 0.6 copy-start.3

commit v5 on v4

--- a/solution.py
+++ b/solution.py
@@ -3,11 +3,13 @@
 
 import jax
 import jax.numpy as jnp
+import numpy as np
 from jax import lax
 from jax.experimental import pallas as pl
 from jax.experimental.pallas import tpu as pltpu
 from jax.sharding import PartitionSpec as P
 
+F32 = jnp.float32
 BOX = 32
 BOX_Y = 3
 BOX_Z = 4
@@ -23,7 +25,7 @@
 SOUND = math.sqrt(5.0 / 3.0)
 TINY = 1e-30
 COST = 1_100_000_000
-VMEM_LIMIT = 56 * 1024 * 1024
+VMEM_LIMIT = 54 * 1024 * 1024
 
 
 def limit(value, other):
@@ -31,9 +33,12 @@
     return jnp.maximum(jnp.minimum(value, bound), -bound)
 
 
+def between(value, end):
+    return jnp.minimum(jnp.maximum(value, jnp.minimum(end, 0.0)), jnp.maximum(end, 0.0))
+
+
 def deviation(d_prev, d_here, d_next):
-    value = 0.5 * d_here + (d_prev - d_next) * (1.0 / 12.0)
-    return jnp.minimum(jnp.maximum(value, jnp.minimum(d_here, 0.0)), jnp.maximum(d_here, 0.0))
+    return between(0.5 * d_here + (d_prev - d_next) * (1.0 / 12.0), d_here)
 
 
 def invert(x):
@@ -113,19 +118,22 @@
     return pltpu.roll(x, shift % NZ, 1)
 
 
-def sweep_lanes(q):
-    d = [turn(x, -1) - x for x in q]
-    dr = [deviation(turn(x, 1), x, turn(x, -1)) for x in d]
-    dl = [turn(r - x, 1) for r, x in zip(dr, d)]
-    right = [c + limit(r, l) for c, r, l in zip(q, dr, dl)]
-    left = [turn(c + limit(l, r), -1) for c, r, l in zip(q, dr, dl)]
-    now = flux(right, left, 3)
-    return [c - (f - turn(f, 1)) for c, f in zip(q, now)]
-
-
-def lane_sum(t):
-    pair = t + turn(t, -1)
-    return t + turn(pair, 2) + turn(pair, -1)
+def lane_weights():
+    parts = []
+    for taps in (((1, 1), (0, -1)), ((0, -5), (1, 7), (-1, -1), (2, -1)), tuple((k, 1) for k in range(-2, 3))):
+        w = np.zeros((NZ, NZ), np.float32)
+        for offset, value in taps:
+            for j in range(NZ):
+                w[(j + offset) % NZ, j] = value
+        parts.append(w)
+    w = np.concatenate(parts, axis=1)
+    return jnp.asarray(np.concatenate([w, w], axis=0), jnp.bfloat16)
+
+
+def mixed(x, weights):
+    high = x.astype(jnp.bfloat16)
+    low = (x - high.astype(F32)).astype(jnp.bfloat16)
+    return jnp.dot(jnp.concatenate([high, low], axis=1), weights, preferred_element_type=F32)
 
 
 def x_lines(segments, read, write):
@@ -154,10 +162,11 @@
     lax.fori_loop(0, tiles, tile, 0)
 
 
-ROWS_STEP = 10
-
-
-def yz_sweep(s_ref, dm_ref, o_ref, t_ref, planes, ready, done):
+U = 20
+PAIR = 2
+
+
+def yz_sweep(s_ref, dm_ref, o_ref, t_ref, w_ref, swept_ref, edge_ref, planes, ready, done):
     def group(g, _):
         ready(g)
 
@@ -166,27 +175,51 @@
 
         def rows(row):
             return [s_ref[at(f, row), :] for f in range(5)]
+
+        def block(k, row, count):
+            return pl.ds((k * U + row) * 8, count * 8)
 
         first = Line(2)
         for row in range(3, 9):
             first.push(rows(row))
 
         def some(b, carry):
+            base = b * U + 6
             line = Line(2)
-            base = 9 + b * ROWS_STEP
-            line.load([rows(base - 3), rows(base - 2), rows(base - 1)], carry)
-            ahead = [rows(base + r) for r in range(ROWS_STEP)]
-            for r in range(ROWS_STEP):
-                swept = line.push(ahead[r])
-                final = sweep_lanes(swept)
-                row = base + r - 3
+            line.load([rows(base), rows(base + 1), rows(base + 2)], carry)
+            for r in range(U):
+                swept = line.push(rows(base + 3 + r))
                 for f in range(5):
-                    o_ref[at(f, row), :] = final[f] * UNSCALES[f] if f else final[f]
-                total = final[0] + dm_ref[at(0, row), :]
-                t_ref[at(0, row), :] = lane_sum(total)
+                    swept_ref[block(f, r, 1), :] = swept[f]
+            for f in range(5):
+                q = swept_ref[block(f, 0, U), :]
+                both = mixed(q, w_ref[:, :2 * NZ])
+                d = both[:, :NZ]
+                dr = between(both[:, NZ:] * (1.0 / 12.0), d)
+                dl = turn(dr - d, 1)
+                edge_ref[block(f, 0, U), :] = q + limit(dr, dl)
+                edge_ref[block(5 + f, 0, U), :] = turn(q + limit(dl, dr), -1)
+            for r in range(0, U, PAIR):
+                left = [edge_ref[block(f, r, PAIR), :] for f in range(5)]
+                right = [edge_ref[block(5 + f, r, PAIR), :] for f in range(5)]
+                now = flux(left, right, 3)
+                for f in range(5):
+                    final = swept_ref[block(f, r, PAIR), :] - (now[f] - turn(now[f], 1))
+                    if f == 0:
+                        density = final
+                    else:
+                        final = final * UNSCALES[f]
+                    for i in range(PAIR):
+                        o_ref[at(f, base + r + i), :] = final[8 * i:8 * i + 8]
+                for i in range(PAIR):
+                    total = density[8 * i:8 * i + 8] + dm_ref[at(0, base + r + i), :]
+                    edge_ref[block(0, r + i, 1), :] = total
+            sums = mixed(edge_ref[block(0, 0, U), :], w_ref[:, 2 * NZ:])
+            for r in range(U):
+                t_ref[at(0, base + r), :] = sums[8 * r:8 * r + 8]
             return line.carry()
 
-        lax.fori_loop(0, 100 // ROWS_STEP, some, first.carry())
+        lax.fori_loop(0, 100 // U, some, first.carry())
         done(g)
         return 0
 
@@ -405,9 +438,9 @@
     lax.fori_loop(0, NY // 8, end, 0)
 
 
-def inner_kernel(dest, swept, dm, y_before, y_after,
+def inner_kernel(dest, weights, swept, dm, y_before, y_after,
                  out_density, out_momentum, out_energy, out_sums, send,
-                 q_ref, s_ref, o_ref, dm_ref, t_ref, x_ref, y_ref, sems, sem, out_sem):
+                 q_ref, s_ref, o_ref, dm_ref, t_ref, w_ref, swept_ref, edge_ref, x_ref, y_ref, sems, sem, out_sem):
     held = pl.ds(1, WIDE + 6)
     s4 = s_ref.reshape(5, WIDE, STRIDE, NZ)
     outs = (out_density, out_momentum, out_energy)
@@ -423,13 +456,14 @@
         pltpu.make_async_copy(y_before.at[pl.ds(0, 5), held], q_ref.at[:, :, pl.ds(0, 8)], sem),
         pltpu.make_async_copy(y_after.at[pl.ds(0, 5), held], q_ref.at[:, :, pl.ds(8, 8)], sem),
     ] + dm_copies(dm, y_before, y_after, sem, dm_ref, 4, 0, WIDE)
+    halo.append(pltpu.make_async_copy(weights, w_ref, sem))
     start_all(halo)
     for g in range(WIDE // 8):
         swept_copy(g).start()
     clear(send)
     wait_all(halo)
     x_sweep(q_ref, s_ref, WIDE, ((0, 0, WIDE),), 2, lambda t: None, lambda t: t * 104)
-    yz_sweep(s_ref, dm_ref, o_ref, t_ref, WIDE, lambda g: swept_copy(g).wait(), lambda g: start_all(leaving(g)))
+    yz_sweep(s_ref, dm_ref, o_ref, t_ref, w_ref, swept_ref, edge_ref, WIDE, lambda g: swept_copy(g).wait(), lambda g: start_all(leaving(g)))
     sums = sums_copy(t_ref, 0, WIDE, out_sums, sem)
     sums.start()
     for row, base in ((0, 2), (8, 10)):
@@ -439,10 +473,10 @@
         wait_all(leaving(g))
 
 
-def outer_kernel(density, momentum, energy, dm, y_before, y_after, x_before, x_after, c_bb, c_ba, c_ab, c_aa,
+def outer_kernel(weights, density, momentum, energy, dm, y_before, y_after, x_before, x_after, c_bb, c_ba, c_ab, c_aa,
                  in_density, in_momentum, in_energy,
                  out_density, out_momentum, out_energy, out_sums, to_next, to_prev,
-                 q_ref, s_ref, o_ref, dm_ref, t_ref, sems, sem, out_sem):
+                 q_ref, s_ref, o_ref, dm_ref, t_ref, w_ref, swept_ref, edge_ref, sems, sem, out_sem):
     fields = (density, momentum, energy)
     tiles = Tiles(q_ref, sems, [
         (fields, y_before, y_after, pl.ds(25, 7), pl.ds(0, 7)),
@@ -453,10 +487,11 @@
     tiles.start()
     copies = (dm_copies(dm, y_before, y_after, sem, dm_ref, 28, 0, 4)
               + dm_copies(dm, y_before, y_after, sem, dm_ref, 0, 4, 4))
+    copies.append(pltpu.make_async_copy(weights, w_ref, sem))
     start_all(copies)
     x_sweep(q_ref, s_ref, 8, ((0, 0, 4), (10, 4, 4)), TILES, tiles.wait, lambda t: t * 8)
     wait_all(copies)
-    yz_sweep(s_ref, dm_ref, o_ref, t_ref, 8, lambda g: None, lambda g: None)
+    yz_sweep(s_ref, dm_ref, o_ref, t_ref, w_ref, swept_ref, edge_ref, 8, lambda g: None, lambda g: None)
     outs = (out_density, out_momentum, out_energy)
     leaving = out_copies(o_ref, 8, outs, out_sem, 28, 0, 4) + out_copies(o_ref, 8, outs, out_sem, 0, 4, 4)
     leaving.append(sums_copy(t_ref, 0, 8, out_sums, out_sem))
@@ -488,7 +523,6 @@
 ANY = pl.BlockSpec(memory_space=pl.ANY)
 SMEM = pl.BlockSpec(memory_space=pltpu.SMEM)
 VMEM = pl.BlockSpec(memory_space=pltpu.VMEM)
-F32 = jnp.float32
 
 
 def shape(*dims):
@@ -510,6 +544,9 @@
         pltpu.VMEM((5 * planes * STRIDE, NZ), F32),
         pltpu.VMEM((planes * STRIDE, NZ), F32),
         pltpu.VMEM((planes * STRIDE, NZ), F32),
+        pltpu.VMEM((2 * NZ, 3 * NZ), jnp.bfloat16),
+        pltpu.VMEM((5 * U * 8, NZ), F32),
+        pltpu.VMEM((10 * U * 8, NZ), F32),
     ]
 
 
@@ -541,6 +578,7 @@
 def body(density, momentum, energy, dm_density, box_dest):
     dest = box_dest[0, 0, :, 0]
     fields = (density, momentum, energy)
+    weights = lane_weights()
     halo_shapes = (shape(6, NX, 8, NZ),) * 2 + (shape(5, 3, NY, NZ),) * 2 + (shape(5, 3, 8, NZ),) * 4
     y_last, y_first, x_last, x_first, c_ll, c_lf, c_fl, c_ff = pl.pallas_call(
         pack_kernel,
@@ -580,27 +618,27 @@
     inner = pl.pallas_call(
         inner_kernel,
         out_shape=FIELD_SHAPES + (shape(WIDE, FRAME, NZ), shape(32, 16, 1024)),
-        in_specs=[SMEM] + [ANY] * 4,
+        in_specs=[SMEM] + [ANY] * 5,
         out_specs=[ANY] * 4 + [VMEM],
         scratch_shapes=main_scratch(WIDE, WIDE + 6, 16) + smooth_scratch() + semaphores(),
         compiler_params=params(),
-        cost_estimate=cost(33),
+        cost_estimate=cost(26),
         name="inner",
-    )(dest, swept, dm_density, y_before, y_after)
+    )(dest, weights, swept, dm_density, y_before, y_after)
     *made, sums_inner, send_inner = inner
     got_inner = exchange(send_inner, 16)
 
     outer = pl.pallas_call(
         outer_kernel,
         out_shape=FIELD_SHAPES + (shape(8, FRAME, NZ), shape(2, FRAME, NZ), shape(2, FRAME, NZ)),
-        in_specs=[ANY] * 15,
+        in_specs=[ANY] * 16,
         out_specs=[ANY] * 6,
         scratch_shapes=main_scratch(8, 20, FRAME) + semaphores(),
-        input_output_aliases={12: 0, 13: 1, 14: 2},
+        input_output_aliases={13: 0, 14: 1, 15: 2},
         compiler_params=params(),
-        cost_estimate=cost(14),
+        cost_estimate=cost(13),
         name="outer",
-    )(*fields, dm_density, y_before, y_after, x_before, x_after, c_bb, c_ba, c_ab, c_aa, *made)
+    )(weights, *fields, dm_density, y_before, y_after, x_before, x_after, c_bb, c_ba, c_ab, c_aa, *made)
     new_density, new_momentum, new_energy, sums_outer, to_next, to_prev = outer
     from_prev = shifted(to_next, "box", 1)
     from_next = shifted(to_prev, "box", -1)

time: 143 us -> 136 us (0.951)
  Pallas kernels: 65.7 us -> 55.5 us
  waiting for transfers between devices: 12.3 us -> 14.8 us
    pallas_call x1, Pallas kernels: 32.2 us -> 24.6 us  [body(): pl.pallas_call(inner_kernel, out_shape=FIELD_SHAPES + (shape(WIDE, FRAME,...]
    pallas_call x1, Pallas kernels: 15.2 us -> 12.7 us  [body(): pl.pallas_call(outer_kernel, out_shape=FIELD_SHAPES + (shape(8, FRAME, NZ...]
    ppermute x6, waiting for transfers between devices: 12.2 us -> 14.8 us  [shifted(): lax.ppermute(value, axis, [(i, (i + by) % size) for i in range(size)])]
  transfers between devices with their start and end apart: 11 -> 11, of which waited for: 2 -> 2; matrix products, arithmetic and copies ran while one was open for 0% -> 0% of each run, Pallas kernels for 44% -> 39%
where the time goes in v5:
time: 136 us; the launch traced here: 134 us
  Pallas kernels  55.5 us (41%)
  blocking collectives  35.1 us (26%)
  starting transfers between devices  24.1 us (18%)
  waiting for transfers between devices  14.8 us (11%)
  other arithmetic  2.55 us (2%)
  local copies, waits for them, and re-layouts  1.4 us (1%)
    all_to_all x1, blocking collectives, exchange(): lax.all_to_all(send.reshape(16, 2, planes, 1024), 'box', split_axis=0, co...  35.1 us
    pallas_call x1, Pallas kernels, body(): pl.pallas_call(inner_kernel, out_shape=FIELD_SHAPES + (shape(WIDE, FRAME,...  24.6 us
    ppermute x6, waiting for transfers between devices, shifted(): lax.ppermute(value, axis, [(i, (i + by) % size) for i in range(size)])  14.8 us
    ppermute x6, starting transfers between devices, shifted(): lax.ppermute(value, axis, [(i, (i + by) % size) for i in range(size)])  13.3 us
    pallas_call x1, Pallas kernels, body(): pl.pallas_call(outer_kernel, out_shape=FIELD_SHAPES + (shape(8, FRAME, NZ...  12.7 us
    pallas_call x1, Pallas kernels, body(): pl.pallas_call(x_kernel, out_shape=shape(5, WIDE, NY, NZ), in_specs=[ANY]...  9.99 us
    ppermute x4, starting transfers between devices, diagonal(): return lax.ppermute(value, ('box', 'grp'), pairs)  7.13 us
    pallas_call x1, Pallas kernels, body(): pl.pallas_call(rest_kernel, out_shape=shape(32, 16, 1024), in_specs=[SMEM...  4.51 us
  transfers between devices with their start and end apart: 11, of which 2 were waited for; matrix products, arithmetic and copies ran while one was open for 0% of the time, Pallas kernels for 39%

profile of v5, /device:TPU:32, one launch (start us, length us, event | category | flops | bytes accessed | tf_op | source)
XLA Modules:
  0.0 134.3 jit_solution(6194753459843040802)
XLA Ops:
  0.6 3.7 %pack.1 = (f32[6,32,8,128]{3,2,1,0:T(8,128)}, f32[6,32,8,128]{3,2,1,0:T(8,128)}, f32[5,3,96,128]{3,2,1,0:T(8,128)}, f32[5,3,96,128]{3,2,1,0:T(8,128)}, f32[5,3,8...) custom-call(f32[32,96,128]{2,1,0:T(8,128)} %density.5, ...), custom_call_target="tpu_custom_call" | custom-call | flops 2200000000 | tf_op jit(solution)/shard_map/pack/pallas_call | solution.py:583
  4.4 1.0 collective-permute-start.4
  5.4 2.7 %collective-permute-start.5 = (f32[5,3,8,128]{3,2,1,0:T(8,128)}, f32[5,3,8,128]{3,2,1,0:T(8,128)S(1)}, u32[]{:S(2)}, u32[]{:S(2)}) collective-permute-start(f32[5,3,8,128]{3,2,1,0:T(8,128)} %get-tuple-element.30), channel_id=1, source_target_pairs={{0,15},{1,8},{2,9},{3,10},{4,11},{5,12},{6,13},{7,14},{8,23},{9,16... | collective-permute-start | bytes 184328 | tf_op jit(solution)/shard_map/ppermute | solution.py:575
  8.0 2.8 %collective-permute-start.6 = (f32[5,3,8,128]{3,2,1,0:T(8,128)}, f32[5,3,8,128]{3,2,1,0:T(8,128)S(1)}, u32[]{:S(2)}, u32[]{:S(2)}) collective-permute-start(f32[5,3,8,128]{3,2,1,0:T(8,128)} %get-tuple-element.31), channel_id=1, source_target_pairs={{0,121},{1,122},{2,123},{3,124},{4,125},{5,126},{6,127},{7,120},{8... | collective-permute-start | bytes 184328 | tf_op jit(solution)/shard_map/ppermute | solution.py:575
  10.9 2.5 %collective-permute-start = (f32[6,32,8,128]{3,2,1,0:T(8,128)}, f32[6,32,8,128]{3,2,1,0:T(8,128)S(1)}, u32[]{:S(2)}, u32[]{:S(2)}) collective-permute-start(f32[6,32,8,128]{3,2,1,0:T(8,128)} %get-tuple-element.25), channel_id=1, source_target_pairs={{0,1},{1,2},{2,3},{3,4},{4,5},{5,6},{6,7},{7,0},{8,9},{9,10},{10,1... | collective-permute-start | bytes 2359304 | tf_op jit(solution)/shard_map/ppermute | solution.py:566
  13.4 0.0 copy-start.7
  13.4 0.0 collective-permute-start.1
  13.4 10.0 %x_own.1.swept = f32[5,24,96,128]{3,2,1,0:T(8,128)} custom-call(f32[32,96,128]{2,1,0:T(8,128)} %density.5, f32[3,32,96,128]{3,2,1,0:T(8,128)} %momentum.5, f32[32,96,128]{2,1,0:T(8,128)} %energy.5), custom_call_target="tpu_custom_call" | custom-call | flops 9900000256 | tf_op jit(solution)/shard_map/x_own/pallas_call | solution.py:602
  23.4 0.0 collective-permute-done.4.c_bb
  23.4 0.0 copy-start.4
  23.4 0.0 copy-done.7
  23.4 0.6 collective-permute-start.7
  24.0 0.0 collective-permute-done.y_before
  24.0 0.0 copy-start
  24.0 1.1 collective-permute-start.2
  25.1 0.0 collective-permute-done.1.y_after
  25.1 0.0 copy-start.1
  25.1 4.3 %collective-permute-start.3 = (f32[5,3,96,128]{3,2,1,0:T(8,128)}, f32[5,3,96,128]{3,2,1,0:T(8,128)}, u32[]{:S(2)}, u32[]{:S(2)}) collective-permute-start(f32[5,3,96,128]{3,2,1,0:T(8,128)} %get-tuple-element.28), channel_id=1, source_target_pairs={{0,120},{8,0},{16,8},{24,16},{32,24},{40,32},{48,40},{56,48},{64,5... | collective-permute-start | bytes 2211848 | tf_op jit(solution)/shard_map/ppermute | solution.py:566
  29.4 0.0 copy-done
  29.4 0.0 copy-done.1
  29.4 24.6 %inner.1 = (f32[32,96,128]{2,1,0:T(8,128)}, f32[3,32,96,128]{3,2,1,0:T(8,128)}, f32[32,96,128]{2,1,0:T(8,128)}, f32[24,112,128]{2,1,0:T(8,128)}, f32[32,16,1024]{2,1,0:T(8,128)}) custom-call(s32[12]{0:T(128)} %bitcast.7, bf16[256,384]{1,0:T(8,128)(2,1)} %constant.2.clone.weights, f32[5,24,96,128]{3,2,1,0:T(8,128)} %x_own.1.swept, f32[32,96,128]{2,1,0:T(8,128)} %dm.5, ...), custom_call_target="tpu_custom_call" | custom-call | flops 28600000512 | tf_op jit(solution)/shard_map/inner/pallas_call | solution.py:618
  54.0 0.0 copy-done.4
  54.1 3.7 %all-to-all-start = ((f32[16,2,16,1024]{3,2,1,0:T(8,128)}), f32[16,2,16,1024]{3,2,1,0:T(8,128)S(1)}, u32[]{:S(2)}, u32[]{:S(2)}) async-start(f32[16,2,16,1024]{3,2,1,0:T(8,128)} %bitcast.5), calls=%async_computation | async-start | bytes 4194304 | tf_op jit(solution)/shard_map/all_to_all | solution.py:616
  57.8 0.0 collective-permute-done.5.c_ba
  57.8 0.0 copy-start.5
  57.8 0.0 collective-permute-done.6.c_ab
  57.8 0.0 copy-start.6
  57.8 0.0 collective-permute-done.7.c_aa
  57.8 0.0 copy-start.8
  57.9 0.0 collective-permute-done.2.x_before
  57.9 0.0 collective-permute-done.3.x_after
  57.9 0.6 copy-done.5
  58.4 0.0 copy-done.6
  58.4 0.0 copy-done.8
  58.5 12.7 %outer.1 = (f32[32,96,128]{2,1,0:T(8,128)}, f32[3,32,96,128]{3,2,1,0:T(8,128)}, f32[32,96,128]{2,1,0:T(8,128)}, f32[8,112,128]{2,1,0:T(8,128)}, f32[2,112,128]{2,1,0:T(8,128)}, /*index=5*/f32[2,112,128]{2,1,0:T(8,128)}) custom-call(bf16[256,384]{1,0:T(8,128)(2,1)} %constant.2.clone.weights, ...), custom_call_target="tpu_custom_call", output_to_operand_aliasing={{0}: (13, {}), {1}: (14, {}), {2}: (15, {})} | custom-call | flops 14300000256 | tf_op jit(solution)/shard_map/outer/pallas_call | solution.py:631
  71.2 1.9 %collective-permute-start.8 = (f32[2,112,128]{2,1,0:T(8,128)}, f32[2,112,128]{2,1,0:T(8,128)S(1)}, u32[]{:S(2)}, u32[]{:S(2)}) collective-permute-start(f32[2,112,128]{2,1,0:T(8,128)} %get-tuple-element.41), channel_id=1, source_target_pairs={{0,8},{8,16},{16,24},{24,32},{32,40},{40,48},{48,56},{56,64},{64,7... | collective-permute-start | bytes 344072 | tf_op jit(solution)/shard_map/ppermute | solution.py:566
  73.0 3.5 %collective-permute-start.9 = (f32[2,112,128]{2,1,0:T(8,128)}, f32[2,112,128]{2,1,0:T(8,128)S(1)}, u32[]{:S(2)}, u32[]{:S(2)}) collective-permute-start(f32[2,112,128]{2,1,0:T(8,128)} %get-tuple-element.42), channel_id=1, source_target_pairs={{0,120},{8,0},{16,8},{24,16},{32,24},{40,32},{48,40},{56,48},{64,5... | collective-permute-start | bytes 344072 | tf_op jit(solution)/shard_map/ppermute | solution.py:566
  76.6 11.8 %collective-permute-done.8.from_prev = f32[2,112,128]{2,1,0:T(8,128)S(1)} collective-permute-done((f32[2,112,128]{2,1,0:T(8,128)}, f32[2,112,128]{2,1,0:T(8,128)S(1)}, u32[]{:S(2)}, u32[]{:S(2)}) %collective-permute-start.8) | collective-permute-done | bytes 114720 | tf_op jit(solution)/shard_map/ppermute | solution.py:566
  88.4 0.0 copy-start.2
  88.4 3.0 %collective-permute-done.9.from_next = f32[2,112,128]{2,1,0:T(8,128)S(1)} collective-permute-done((f32[2,112,128]{2,1,0:T(8,128)}, f32[2,112,128]{2,1,0:T(8,128)S(1)}, u32[]{:S(2)}, u32[]{:S(2)}) %collective-permute-start.9) | collective-permute-done | bytes 114720 | tf_op jit(solution)/shard_map/ppermute | solution.py:566
  91.3 0.0 copy-start.3
  91.3 0.0 copy-done.2
  91.3 0.6 copy-done.3
  92.0 4.5 %rest.1 = f32[32,16,1024]{2,1,0:T(8,128)} custom-call(s32[12]{0:T(128)} %bitcast.8, f32[24,112,128]{2,1,0:T(8,128)} %get-tuple-element.39.sums_inner, f32[8,112,128]{2,1,0:T(8,128)} %get-tuple-element.40.sums_outer, f32[2,112,128]{2,1,0:T(8,128)} %copy-done.2, f32[2,112,128]{2,1,0:T(8,128)} %copy-done.3), custom_call_target="tpu_custom_call" | custom-call | flops 5500000256 | tf_op jit(solution)/shard_map/rest/pallas_call | solution.py:645
  96.5 0.0 all-to-all-done
  96.5 35.1 %all_to_all.10 = f32[16,2,16,1024]{3,2,1,0:T(8,128)S(1)} all-to-all(f32[16,2,16,1024]{3,2,1,0:T(8,128)} %bitcast.6), channel_id=1, replica_groups=mesh['box'=16,'grp'=8] {'box'}, dimensions={0} | all-to-all | bytes 4194304 | tf_op jit(solution)/shard_map/all_to_all | solution.py:616
  131.6 0.1 fusion
  131.7 2.5 %maximum_bitcast_fusion = f32[1,1,16,2,32,1024]{5,4,3,2,1,0:T(8,128)} fusion(f32[16,2,8,1024]{3,2,1,0:T(8,128)S(1)} %get-tuple-element.47, f32[16,2,16,1024]{3,2,1,0:T(8,128)S(1)} %all-to-all-done, f32[16,2,8,1024]{3,2,1,0:T(8,128)S(1)} %get-tuple-element.46), kind=kLoop, calls=%fused_computation | loop fusion | flops 2097152 | bytes 8388608 | tf_op jit(solution)/shard_map/broadcast_in_dim | solution.py:658
Async XLA Ops:
  4.4 19.0 %collective-permute-start.4 = (f32[5,3,8,128]{3,2,1,0:T(8,128)}, f32[5,3,8,128]{3,2,1,0:T(8,128)S(1)}, u32[]{:S(2)}, u32[]{:S(2)}) collective-permute-start(f32[5,3,8,128]{3,2,1,0:T(8,128)} %get-tuple-element.29), channel_id=1, source_target_pairs={{0,9},{1,10},{2,11},{3,12},{4,13},{5,14},{6,15},{7,8},{8,17},{9,18... | collective-permute-start | bytes 184328 | tf_op jit(solution)/shard_map/ppermute | solution.py:575
  5.4 52.4 %collective-permute-start.5 = (f32[5,3,8,128]{3,2,1,0:T(8,128)}, f32[5,3,8,128]{3,2,1,0:T(8,128)S(1)}, u32[]{:S(2)}, u32[]{:S(2)}) collective-permute-start(f32[5,3,8,128]{3,2,1,0:T(8,128)} %get-tuple-element.30), channel_id=1, source_target_pairs={{0,15},{1,8},{2,9},{3,10},{4,11},{5,12},{6,13},{7,14},{8,23},{9,16... | collective-permute-start | bytes 184328 | tf_op jit(solution)/shard_map/ppermute | solution.py:575
  8.0 49.8 %collective-permute-start.6 = (f32[5,3,8,128]{3,2,1,0:T(8,128)}, f32[5,3,8,128]{3,2,1,0:T(8,128)S(1)}, u32[]{:S(2)}, u32[]{:S(2)}) collective-permute-start(f32[5,3,8,128]{3,2,1,0:T(8,128)} %get-tuple-element.31), channel_id=1, source_target_pairs={{0,121},{1,122},{2,123},{3,124},{4,125},{5,126},{6,127},{7,120},{8... | collective-permute-start | bytes 184328 | tf_op jit(solution)/shard_map/ppermute | solution.py:575
  10.9 13.2 %collective-permute-start = (f32[6,32,8,128]{3,2,1,0:T(8,128)}, f32[6,32,8,128]{3,2,1,0:T(8,128)S(1)}, u32[]{:S(2)}, u32[]{:S(2)}) collective-permute-start(f32[6,32,8,128]{3,2,1,0:T(8,128)} %get-tuple-element.25), channel_id=1, source_target_pairs={{0,1},{1,2},{2,3},{3,4},{4,5},{5,6},{6,7},{7,0},{8,9},{9,10},{10,1... | collective-permute-start | bytes 2359304 | tf_op jit(solution)/shard_map/ppermute | solution.py:566
  13.4 10.0 %copy-start.7 = (f32[5,3,8,128]{3,2,1,0:T(8,128)S(1)}, f32[5,3,8,128]{3,2,1,0:T(8,128)}, u32[]{:S(2)}) copy-start(f32[5,3,8,128]{3,2,1,0:T(8,128)} %get-tuple-element.32) | copy-start | bytes 184324
  13.4 11.8 %collective-permute-start.1 = (f32[6,32,8,128]{3,2,1,0:T(8,128)}, f32[6,32,8,128]{3,2,1,0:T(8,128)S(1)}, u32[]{:S(2)}, u32[]{:S(2)}) collective-permute-start(f32[6,32,8,128]{3,2,1,0:T(8,128)} %get-tuple-element.26), channel_id=1, source_target_pairs={{0,7},{1,0},{2,1},{3,2},{4,3},{5,4},{6,5},{7,6},{8,15},{9,8},{10,9... | collective-permute-start | bytes 2359304 | tf_op jit(solution)/shard_map/ppermute | solution.py:566
  23.4 30.7 %copy-start.4 = (f32[5,3,8,128]{3,2,1,0:T(8,128)}, f32[5,3,8,128]{3,2,1,0:T(8,128)S(1)}, u32[]{:S(2)}) copy-start(f32[5,3,8,128]{3,2,1,0:T(8,128)S(1)} %collective-permute-done.4.c_bb) | copy-start | bytes 184324
  23.4 34.4 %collective-permute-start.7 = (f32[5,3,8,128]{3,2,1,0:T(8,128)S(1)}, f32[5,3,8,128]{3,2,1,0:T(8,128)S(1)}, u32[]{:S(2)}, u32[]{:S(2)}) collective-permute-start(f32[5,3,8,128]{3,2,1,0:T(8,128)S(1)} %copy-done.7), channel_id=1, source_target_pairs={{0,127},{1,120},{2,121},{3,122},{4,123},{5,124},{6,125},{7,126},{8... | collective-permute-start | bytes 184328 | tf_op jit(solution)/shard_map/ppermute | solution.py:575
  24.0 5.4 %copy-start = (f32[6,32,8,128]{3,2,1,0:T(8,128)}, f32[6,32,8,128]{3,2,1,0:T(8,128)S(1)}, u32[]{:S(2)}) copy-start(f32[6,32,8,128]{3,2,1,0:T(8,128)S(1)} %collective-permute-done.y_before) | copy-start | bytes 2359300
  24.0 33.8 %collective-permute-start.2 = (f32[5,3,96,128]{3,2,1,0:T(8,128)}, f32[5,3,96,128]{3,2,1,0:T(8,128)}, u32[]{:S(2)}, u32[]{:S(2)}) collective-permute-start(f32[5,3,96,128]{3,2,1,0:T(8,128)} %get-tuple-element.27), channel_id=1, source_target_pairs={{0,8},{8,16},{16,24},{24,32},{32,40},{40,48},{48,56},{56,64},{64,7... | collective-permute-start | bytes 2211848 | tf_op jit(solution)/shard_map/ppermute | solution.py:566
  25.1 4.3 %copy-start.1 = (f32[6,32,8,128]{3,2,1,0:T(8,128)}, f32[6,32,8,128]{3,2,1,0:T(8,128)S(1)}, u32[]{:S(2)}) copy-start(f32[6,32,8,128]{3,2,1,0:T(8,128)S(1)} %collective-permute-done.1.y_after) | copy-start | bytes 2359300
  25.1 32.7 %collective-permute-start.3 = (f32[5,3,96,128]{3,2,1,0:T(8,128)}, f32[5,3,96,128]{3,2,1,0:T(8,128)}, u32[]{:S(2)}, u32[]{:S(2)}) collective-permute-start(f32[5,3,96,128]{3,2,1,0:T(8,128)} %get-tuple-element.28), channel_id=1, source_target_pairs={{0,120},{8,0},{16,8},{24,16},{32,24},{40,32},{48,40},{56,48},{64,5... | collective-permute-start | bytes 2211848 | tf_op jit(solution)/shard_map/ppermute | solution.py:566
  54.1 42.5 %all-to-all-start = ((f32[16,2,16,1024]{3,2,1,0:T(8,128)}), f32[16,2,16,1024]{3,2,1,0:T(8,128)S(1)}, u32[]{:S(2)}, u32[]{:S(2)}) async-start(f32[16,2,16,1024]{3,2,1,0:T(8,128)} %bitcast.5), calls=%async_computation | async-start | bytes 4194304 | tf_op jit(solution)/shard_map/all_to_all | solution.py:616
  57.8 0.6 copy-start.5
  57.8 0.6 copy-start.6
  57.8 0.6 copy-start.8
  71.2 17.2 %collective-permute-start.8 = (f32[2,112,128]{2,1,0:T(8,128)}, f32[2,112,128]{2,1,0:T(8,128)S(1)}, u32[]{:S(2)}, u32[]{:S(2)}) collective-permute-start(f32[2,112,128]{2,1,0:T(8,128)} %get-tuple-element.41), channel_id=1, source_target_pairs={{0,8},{8,16},{16,24},{24,32},{32,40},{40,48},{48,56},{56,64},{64,7... | collective-permute-start | bytes 344072 | tf_op jit(solution)/shard_map/ppermute | solution.py:566
  73.0 18.3 %collective-permute-start.9 = (f32[2,112,128]{2,1,0:T(8,128)}, f32[2,112,128]{2,1,0:T(8,128)S(1)}, u32[]{:S(2)}, u32[]{:S(2)}) collective-permute-start(f32[2,112,128]{2,1,0:T(8,128)} %get-tuple-element.42), channel_id=1, source_target_pairs={{0,120},{8,0},{16,8},{24,16},{32,24},{40,32},{48,40},{56,48},{64,5... | collective-permute-start | bytes 344072 | tf_op jit(solution)/shard_map/ppermute | solution.py:566
  88.4 3.0 %copy-start.2 = (f32[2,112,128]{2,1,0:T(8,128)}, f32[2,112,128]{2,1,0:T(8,128)S(1)}, u32[]{:S(2)}) copy-start(f32[2,112,128]{2,1,0:T(8,128)S(1)} %collective-permute-done.8.from_prev) | copy-start | bytes 344068
  91.3 0.6 copy-start.3

commit v6 on v5

--- a/solution.py
+++ b/solution.py
@@ -296,12 +296,12 @@
         for own, before, after, src, dst in self.parts:
             q = self.q_ref.at[:, dst, rows_of(t)]
             sem = self.sems.at[t]
-            if kind == "before":
+            if len(own) == 1:
+                out.append(pltpu.make_async_copy(own[0].at[:, src, rows_of(t)], q, sem))
+            elif kind == "before":
                 out.append(pltpu.make_async_copy(before.at[pl.ds(0, 5), src], q, sem))
             elif kind == "after":
                 out.append(pltpu.make_async_copy(after.at[pl.ds(0, 5), src], q, sem))
-            elif len(own) == 1:
-                out.append(pltpu.make_async_copy(own[0].at[:, src, rows_of(t - 1)], q, sem))
             else:
                 density, momentum, energy = own
                 rows = rows_of(t - 1)
@@ -377,22 +377,29 @@
     return pltpu.make_async_copy(framed(t_ref).at[pl.ds(base, count), pl.ds(0, FRAME)], out, sem)
 
 
-def pack_kernel(density, momentum, energy, dm, y_last, y_first, x_last, x_first, c_ll, c_lf, c_fl, c_ff, sem):
+def field_copies(density, momentum, energy, planes, rows, out, to, sem):
+    return [
+        pltpu.make_async_copy(density.at[planes, rows], out.at[0, :, to], sem),
+        pltpu.make_async_copy(momentum.at[:, planes, rows], out.at[pl.ds(1, 3), :, to], sem),
+        pltpu.make_async_copy(energy.at[planes, rows], out.at[4, :, to], sem),
+    ]
+
+
+def pack_y_kernel(density, momentum, energy, dm, y_last, y_first, sem):
     copies = []
-
-    def fields(out, planes, rows):
-        copies.append(pltpu.make_async_copy(density.at[planes, rows], out.at[0], sem))
-        copies.append(pltpu.make_async_copy(momentum.at[:, planes, rows], out.at[pl.ds(1, 3)], sem))
-        copies.append(pltpu.make_async_copy(energy.at[planes, rows], out.at[4], sem))
-
-    ends = (pl.ds(NY - 8, 8), pl.ds(0, 8))
-    for out, rows in zip((y_last, y_first), ends):
-        fields(out, pl.ds(0, NX), rows)
+    for out, rows in ((y_last, pl.ds(NY - 8, 8)), (y_first, pl.ds(0, 8))):
+        copies += field_copies(density, momentum, energy, pl.ds(0, NX), rows, out, pl.ds(0, 8), sem)
         copies.append(pltpu.make_async_copy(dm.at[:, rows], out.at[5], sem))
-    for x_out, c_out, planes in ((x_last, (c_ll, c_lf), pl.ds(NX - 3, 3)), (x_first, (c_fl, c_ff), pl.ds(0, 3))):
-        fields(x_out, planes, pl.ds(0, NY))
-        for n, rows in enumerate(ends):
-            fields(c_out[n], planes, rows)
+    start_all(copies)
+    wait_all(copies)
+
+
+def pack_x_kernel(density, momentum, energy, y_before, y_after, x_last, x_first, sem):
+    copies = []
+    for out, planes in ((x_last, pl.ds(NX - 3, 3)), (x_first, pl.ds(0, 3))):
+        copies += field_copies(density, momentum, energy, planes, pl.ds(0, NY), out, pl.ds(8, NY), sem)
+        for side, to in ((y_before, pl.ds(0, 8)), (y_after, pl.ds(104, 8))):
+            copies.append(pltpu.make_async_copy(side.at[pl.ds(0, 5), planes], out.at[:, :, to], sem))
     start_all(copies)
     wait_all(copies)
 
@@ -473,15 +480,15 @@
         wait_all(leaving(g))
 
 
-def outer_kernel(weights, density, momentum, energy, dm, y_before, y_after, x_before, x_after, c_bb, c_ba, c_ab, c_aa,
+def outer_kernel(weights, density, momentum, energy, dm, y_before, y_after, x_before, x_after,
                  in_density, in_momentum, in_energy,
                  out_density, out_momentum, out_energy, out_sums, to_next, to_prev,
                  q_ref, s_ref, o_ref, dm_ref, t_ref, w_ref, swept_ref, edge_ref, sems, sem, out_sem):
     fields = (density, momentum, energy)
     tiles = Tiles(q_ref, sems, [
         (fields, y_before, y_after, pl.ds(25, 7), pl.ds(0, 7)),
-        ((x_after,), c_ab, c_aa, pl.ds(0, 3), pl.ds(7, 3)),
-        ((x_before,), c_bb, c_ba, pl.ds(0, 3), pl.ds(10, 3)),
+        ((x_after,), None, None, pl.ds(0, 3), pl.ds(7, 3)),
+        ((x_before,), None, None, pl.ds(0, 3), pl.ds(10, 3)),
         (fields, y_before, y_after, pl.ds(0, 7), pl.ds(13, 7)),
     ])
     tiles.start()
@@ -566,38 +573,22 @@
     return lax.ppermute(value, axis, [(i, (i + by) % size) for i in range(size)])
 
 
-def diagonal(value, by_box, by_grp):
-    boxes, grps = lax.axis_size("box"), lax.axis_size("grp")
-    pairs = []
-    for i in range(boxes):
-        for j in range(grps):
-            pairs.append((i * grps + j, (i + by_box) % boxes * grps + (j + by_grp) % grps))
-    return lax.ppermute(value, ("box", "grp"), pairs)
-
-
 def body(density, momentum, energy, dm_density, box_dest):
     dest = box_dest[0, 0, :, 0]
     fields = (density, momentum, energy)
     weights = lane_weights()
-    halo_shapes = (shape(6, NX, 8, NZ),) * 2 + (shape(5, 3, NY, NZ),) * 2 + (shape(5, 3, 8, NZ),) * 4
-    y_last, y_first, x_last, x_first, c_ll, c_lf, c_fl, c_ff = pl.pallas_call(
-        pack_kernel,
-        out_shape=halo_shapes,
+    y_last, y_first = pl.pallas_call(
+        pack_y_kernel,
+        out_shape=(shape(6, NX, 8, NZ),) * 2,
         in_specs=[ANY] * 4,
-        out_specs=[VMEM] * 8,
+        out_specs=[VMEM] * 2,
         scratch_shapes=[pltpu.SemaphoreType.DMA],
         compiler_params=params(),
-        cost_estimate=cost(2),
-        name="pack",
+        cost_estimate=cost(3),
+        name="pack_y",
     )(density, momentum, energy, dm_density)
     y_before = shifted(y_last, "grp", 1)
     y_after = shifted(y_first, "grp", -1)
-    x_before = shifted(x_last, "box", 1)
-    x_after = shifted(x_first, "box", -1)
-    c_bb = diagonal(c_ll, 1, 1)
-    c_ba = diagonal(c_lf, 1, -1)
-    c_ab = diagonal(c_fl, -1, 1)
-    c_aa = diagonal(c_ff, -1, -1)
 
     swept = pl.pallas_call(
         x_kernel,
@@ -612,6 +603,19 @@
         name="x_own",
     )(*fields)
 
+    x_last, x_first = pl.pallas_call(
+        pack_x_kernel,
+        out_shape=(shape(5, 3, FRAME, NZ),) * 2,
+        in_specs=[ANY] * 5,
+        out_specs=[VMEM] * 2,
+        scratch_shapes=[pltpu.SemaphoreType.DMA],
+        compiler_params=params(),
+        cost_estimate=cost(3),
+        name="pack_x",
+    )(*fields, y_before, y_after)
+    x_before = shifted(x_last, "box", 1)
+    x_after = shifted(x_first, "box", -1)
+
     def exchange(send, planes):
         return lax.all_to_all(send.reshape(16, 2, planes, 1024), "box", split_axis=0, concat_axis=0, tiled=True)
 
@@ -631,14 +635,14 @@
     outer = pl.pallas_call(
         outer_kernel,
         out_shape=FIELD_SHAPES + (shape(8, FRAME, NZ), shape(2, FRAME, NZ), shape(2, FRAME, NZ)),
-        in_specs=[ANY] * 16,
+        in_specs=[ANY] * 12,
         out_specs=[ANY] * 6,
         scratch_shapes=main_scratch(8, 20, FRAME) + semaphores(),
-        input_output_aliases={13: 0, 14: 1, 15: 2},
+        input_output_aliases={9: 0, 10: 1, 11: 2},
         compiler_params=params(),
         cost_estimate=cost(13),
         name="outer",
-    )(weights, *fields, dm_density, y_before, y_after, x_before, x_after, c_bb, c_ba, c_ab, c_aa, *made)
+    )(weights, *fields, dm_density, y_before, y_after, x_before, x_after, *made)
     new_density, new_momentum, new_energy, sums_outer, to_next, to_prev = outer
     from_prev = shifted(to_next, "box", 1)
     from_next = shifted(to_prev, "box", -1)

time: 136 us -> 133 us (0.978)
  starting transfers between devices: 24.1 us -> 16.3 us
  local copies, waits for them, and re-layouts: 1.4 us -> 3.43 us
  blocking collectives: 35.1 us -> 36.8 us
  Pallas kernels: 55.5 us -> 56.9 us
    ppermute x4 -> x0, starting transfers between devices: 7.13 us -> none  [diagonal(): return lax.ppermute(value, ('box', 'grp'), pairs)]
    unnamed x18 -> x10, local copies, waits for them, and re-layouts: 1.27 us -> 3.3 us
    all_to_all x1, blocking collectives: 35.1 us -> 36.8 us  [exchange(): lax.all_to_all(send.reshape(16, 2, planes, 1024), 'box', split_axis=0, co...]
    pallas_call x1 -> x2, Pallas kernels: 3.73 us -> 5.14 us  [the longest x1 2.6 us: body(): pl.pallas_call(pack_x_kernel, out_shape=(shape(5, 3, FRAME, NZ),) * 2, in...]
  transfers between devices with their start and end apart: 11 -> 7, of which waited for: 2 -> 2; matrix products, arithmetic and copies ran while one was open for 0% -> 0% of each run, Pallas kernels for 39% -> 39%
where the time goes in v6:
time: 133 us; the launch traced here: 132 us
  Pallas kernels  56.9 us (43%)
  blocking collectives  36.8 us (28%)
  starting transfers between devices  16.3 us (12%)
  waiting for transfers between devices  15.5 us (12%)
  local copies, waits for them, and re-layouts  3.43 us (3%)
  other arithmetic  2.6 us (2%)
    all_to_all x1, blocking collectives, exchange(): lax.all_to_all(send.reshape(16, 2, planes, 1024), 'box', split_axis=0, co...  36.8 us
    pallas_call x1, Pallas kernels, body(): pl.pallas_call(inner_kernel, out_shape=FIELD_SHAPES + (shape(WIDE, FRAME,...  24.6 us
    ppermute x6, waiting for transfers between devices, shifted(): lax.ppermute(value, axis, [(i, (i + by) % size) for i in range(size)])  15.5 us
    pallas_call x1, Pallas kernels, body(): pl.pallas_call(outer_kernel, out_shape=FIELD_SHAPES + (shape(8, FRAME, NZ...  12.7 us
    ppermute x6, starting transfers between devices, shifted(): lax.ppermute(value, axis, [(i, (i + by) % size) for i in range(size)])  12.6 us
    pallas_call x1, Pallas kernels, body(): pl.pallas_call(x_kernel, out_shape=shape(5, WIDE, NY, NZ), in_specs=[ANY]...  9.99 us
    pallas_call x1, Pallas kernels, body(): pl.pallas_call(rest_kernel, out_shape=shape(32, 16, 1024), in_specs=[SMEM...  4.49 us
    all_to_all x1, starting transfers between devices, exchange(): lax.all_to_all(send.reshape(16, 2, planes, 1024), 'box', split_axis=0, co...  3.73 us
  transfers between devices with their start and end apart: 7, of which 2 were waited for; matrix products, arithmetic and copies ran while one was open for 0% of the time, Pallas kernels for 39%

profile of v6, /device:TPU:32, one launch (start us, length us, event | category | flops | bytes accessed | tf_op | source)
XLA Modules:
  0.0 132.4 jit_solution(10912222226497816959)
XLA Ops:
  0.6 2.5 %pack_y.1 = (f32[6,32,8,128]{3,2,1,0:T(8,128)}, f32[6,32,8,128]{3,2,1,0:T(8,128)}) custom-call(f32[32,96,128]{2,1,0:T(8,128)} %density.7, f32[3,32,96,128]{3,2,1,0:T(8,128)} %momentum.7, f32[32,96,128]{2,1,0:T(8,128)} %energy.7, f32[32,96,128]{2,1,0:T(8,128)} %dm.5), custom_call_target="tpu_custom_call" | custom-call | flops 3300000000 | tf_op jit(solution)/shard_map/pack_y/pallas_call | solution.py:580
  3.2 0.0 collective-permute-start
  3.2 1.7 %collective-permute-start.1 = (f32[6,32,8,128]{3,2,1,0:T(8,128)}, f32[6,32,8,128]{3,2,1,0:T(8,128)S(1)}, u32[]{:S(2)}, u32[]{:S(2)}) collective-permute-start(f32[6,32,8,128]{3,2,1,0:T(8,128)} %get-tuple-element.22), channel_id=1, source_target_pairs={{0,7},{1,0},{2,1},{3,2},{4,3},{5,4},{6,5},{7,6},{8,15},{9,8},{10,9... | collective-permute-start | bytes 2359304 | tf_op jit(solution)/shard_map/ppermute | solution.py:573
  4.9 10.0 %x_own.1.swept = f32[5,24,96,128]{3,2,1,0:T(8,128)} custom-call(f32[32,96,128]{2,1,0:T(8,128)} %density.7, f32[3,32,96,128]{3,2,1,0:T(8,128)} %momentum.7, f32[32,96,128]{2,1,0:T(8,128)} %energy.7), custom_call_target="tpu_custom_call" | custom-call | flops 9900000256 | tf_op jit(solution)/shard_map/x_own/pallas_call | solution.py:593
  14.9 0.0 collective-permute-done.y_before
  14.9 0.0 copy-start.1
  15.0 0.0 collective-permute-done.1.y_after
  15.0 0.9 copy-done.1
  15.8 0.0 copy-start.2
  15.8 0.9 copy-done.2
  16.7 2.6 %pack_x.1 = (f32[5,3,112,128]{3,2,1,0:T(8,128)}, f32[5,3,112,128]{3,2,1,0:T(8,128)}) custom-call(f32[32,96,128]{2,1,0:T(8,128)} %density.7, f32[3,32,96,128]{3,2,1,0:T(8,128)} %momentum.7, f32[32,96,128]{2,1,0:T(8,128)} %energy.7, f32[6,32,8,128]{3,2,1,0:T(8,128)} %copy-done.1, f32[6,32,8,128]{3,2,1,0:T(8,128)} %copy-done.2), custom_call_target="tpu_custom_call" | custom-call | flops 3300000000 | tf_op jit(solution)/shard_map/pack_x/pallas_call | solution.py:606
  19.3 1.6 %collective-permute-start.2 = (f32[5,3,112,128]{3,2,1,0:T(8,128)}, f32[5,3,112,128]{3,2,1,0:T(8,128)S(1)}, u32[]{:S(2)}, u32[]{:S(2)}) collective-permute-start(f32[5,3,112,128]{3,2,1,0:T(8,128)} %get-tuple-element.23), channel_id=1, source_target_pairs={{0,8},{8,16},{16,24},{24,32},{32,40},{40,48},{48,56},{56,64},{64,7... | collective-permute-start | bytes 2580488 | tf_op jit(solution)/shard_map/ppermute | solution.py:573
  20.9 3.9 %collective-permute-start.3 = (f32[5,3,112,128]{3,2,1,0:T(8,128)}, f32[5,3,112,128]{3,2,1,0:T(8,128)}, u32[]{:S(2)}, u32[]{:S(2)}) collective-permute-start(f32[5,3,112,128]{3,2,1,0:T(8,128)} %get-tuple-element.24), channel_id=1, source_target_pairs={{0,120},{8,0},{16,8},{24,16},{32,24},{40,32},{48,40},{56,48},{64,5... | collective-permute-start | bytes 2580488 | tf_op jit(solution)/shard_map/ppermute | solution.py:573
  24.8 24.6 %inner.1 = (f32[32,96,128]{2,1,0:T(8,128)}, f32[3,32,96,128]{3,2,1,0:T(8,128)}, f32[32,96,128]{2,1,0:T(8,128)}, f32[24,112,128]{2,1,0:T(8,128)}, f32[32,16,1024]{2,1,0:T(8,128)}) custom-call(s32[12]{0:T(128)} %bitcast.7, bf16[256,384]{1,0:T(8,128)(2,1)} %constant.2.clone.weights, f32[5,24,96,128]{3,2,1,0:T(8,128)} %x_own.1.swept, f32[32,96,128]{2,1,0:T(8,128)} %dm.5, ...), custom_call_target="tpu_custom_call" | custom-call | flops 28600000512 | tf_op jit(solution)/shard_map/inner/pallas_call | solution.py:622
  49.4 3.7 %all-to-all-start = ((f32[16,2,16,1024]{3,2,1,0:T(8,128)}), f32[16,2,16,1024]{3,2,1,0:T(8,128)S(1)}, u32[]{:S(2)}, u32[]{:S(2)}) async-start(f32[16,2,16,1024]{3,2,1,0:T(8,128)} %bitcast.5), calls=%async_computation | async-start | bytes 4194304 | tf_op jit(solution)/shard_map/all_to_all | solution.py:620
  53.1 0.0 collective-permute-done.2.x_before
  53.1 0.0 copy-start
  53.1 0.0 collective-permute-done.3.x_after
  53.2 0.9 copy-done
  54.0 12.7 %outer.1 = (f32[32,96,128]{2,1,0:T(8,128)}, f32[3,32,96,128]{3,2,1,0:T(8,128)}, f32[32,96,128]{2,1,0:T(8,128)}, f32[8,112,128]{2,1,0:T(8,128)}, f32[2,112,128]{2,1,0:T(8,128)}, /*index=5*/f32[2,112,128]{2,1,0:T(8,128)}) custom-call(bf16[256,384]{1,0:T(8,128)(2,1)} %constant.2.clone.weights, ...), custom_call_target="tpu_custom_call", output_to_operand_aliasing={{0}: (9, {}), {1}: (10, {}), {2}: (11, {})} | custom-call | flops 14300000256 | tf_op jit(solution)/shard_map/outer/pallas_call | solution.py:635
  66.7 2.0 %collective-permute-start.4 = (f32[2,112,128]{2,1,0:T(8,128)}, f32[2,112,128]{2,1,0:T(8,128)S(1)}, u32[]{:S(2)}, u32[]{:S(2)}) collective-permute-start(f32[2,112,128]{2,1,0:T(8,128)} %get-tuple-element.33), channel_id=1, source_target_pairs={{0,8},{8,16},{16,24},{24,32},{32,40},{40,48},{48,56},{56,64},{64,7... | collective-permute-start | bytes 344072 | tf_op jit(solution)/shard_map/ppermute | solution.py:573
  68.7 3.5 %collective-permute-start.5 = (f32[2,112,128]{2,1,0:T(8,128)}, f32[2,112,128]{2,1,0:T(8,128)S(1)}, u32[]{:S(2)}, u32[]{:S(2)}) collective-permute-start(f32[2,112,128]{2,1,0:T(8,128)} %get-tuple-element.34), channel_id=1, source_target_pairs={{0,120},{8,0},{16,8},{24,16},{32,24},{40,32},{48,40},{56,48},{64,5... | collective-permute-start | bytes 344072 | tf_op jit(solution)/shard_map/ppermute | solution.py:573
  72.2 12.4 %collective-permute-done.4.from_prev = f32[2,112,128]{2,1,0:T(8,128)S(1)} collective-permute-done((f32[2,112,128]{2,1,0:T(8,128)}, f32[2,112,128]{2,1,0:T(8,128)S(1)}, u32[]{:S(2)}, u32[]{:S(2)}) %collective-permute-start.4) | collective-permute-done | bytes 114720 | tf_op jit(solution)/shard_map/ppermute | solution.py:573
  84.6 0.0 copy-start.3
  84.6 3.1 %collective-permute-done.5.from_next = f32[2,112,128]{2,1,0:T(8,128)S(1)} collective-permute-done((f32[2,112,128]{2,1,0:T(8,128)}, f32[2,112,128]{2,1,0:T(8,128)S(1)}, u32[]{:S(2)}, u32[]{:S(2)}) %collective-permute-start.5) | collective-permute-done | bytes 114720 | tf_op jit(solution)/shard_map/ppermute | solution.py:573
  87.7 0.0 copy-start.4
  87.7 0.0 copy-done.3
  87.7 0.6 copy-done.4
  88.3 4.5 %rest.1 = f32[32,16,1024]{2,1,0:T(8,128)} custom-call(s32[12]{0:T(128)} %bitcast.8, f32[24,112,128]{2,1,0:T(8,128)} %get-tuple-element.31.sums_inner, f32[8,112,128]{2,1,0:T(8,128)} %get-tuple-element.32.sums_outer, f32[2,112,128]{2,1,0:T(8,128)} %copy-done.3, f32[2,112,128]{2,1,0:T(8,128)} %copy-done.4), custom_call_target="tpu_custom_call" | custom-call | flops 5500000256 | tf_op jit(solution)/shard_map/rest/pallas_call | solution.py:649
  92.8 0.0 all-to-all-done
  92.8 36.8 %all_to_all.10 = f32[16,2,16,1024]{3,2,1,0:T(8,128)S(1)} all-to-all(f32[16,2,16,1024]{3,2,1,0:T(8,128)} %bitcast.6), channel_id=1, replica_groups=mesh['box'=16,'grp'=8] {'box'}, dimensions={0} | all-to-all | bytes 4194304 | tf_op jit(solution)/shard_map/all_to_all | solution.py:620
  129.7 0.1 fusion
  129.8 2.6 %maximum_bitcast_fusion = f32[1,1,16,2,32,1024]{5,4,3,2,1,0:T(8,128)} fusion(f32[16,2,8,1024]{3,2,1,0:T(8,128)S(1)} %get-tuple-element.39, f32[16,2,16,1024]{3,2,1,0:T(8,128)S(1)} %all-to-all-done, f32[16,2,8,1024]{3,2,1,0:T(8,128)S(1)} %get-tuple-element.38), kind=kLoop, calls=%fused_computation | loop fusion | flops 2097152 | bytes 8388608 | tf_op jit(solution)/shard_map/broadcast_in_dim | solution.py:662
Async XLA Ops:
  3.2 11.8 %collective-permute-start = (f32[6,32,8,128]{3,2,1,0:T(8,128)}, f32[6,32,8,128]{3,2,1,0:T(8,128)S(1)}, u32[]{:S(2)}, u32[]{:S(2)}) collective-permute-start(f32[6,32,8,128]{3,2,1,0:T(8,128)} %get-tuple-element.21), channel_id=1, source_target_pairs={{0,1},{1,2},{2,3},{3,4},{4,5},{5,6},{6,7},{7,0},{8,9},{9,10},{10,1... | collective-permute-start | bytes 2359304 | tf_op jit(solution)/shard_map/ppermute | solution.py:573
  3.2 11.8 %collective-permute-start.1 = (f32[6,32,8,128]{3,2,1,0:T(8,128)}, f32[6,32,8,128]{3,2,1,0:T(8,128)S(1)}, u32[]{:S(2)}, u32[]{:S(2)}) collective-permute-start(f32[6,32,8,128]{3,2,1,0:T(8,128)} %get-tuple-element.22), channel_id=1, source_target_pairs={{0,7},{1,0},{2,1},{3,2},{4,3},{5,4},{6,5},{7,6},{8,15},{9,8},{10,9... | collective-permute-start | bytes 2359304 | tf_op jit(solution)/shard_map/ppermute | solution.py:573
  14.9 0.9 copy-start.1
  15.8 0.9 copy-start.2
  19.3 33.8 %collective-permute-start.2 = (f32[5,3,112,128]{3,2,1,0:T(8,128)}, f32[5,3,112,128]{3,2,1,0:T(8,128)S(1)}, u32[]{:S(2)}, u32[]{:S(2)}) collective-permute-start(f32[5,3,112,128]{3,2,1,0:T(8,128)} %get-tuple-element.23), channel_id=1, source_target_pairs={{0,8},{8,16},{16,24},{24,32},{32,40},{40,48},{48,56},{56,64},{64,7... | collective-permute-start | bytes 2580488 | tf_op jit(solution)/shard_map/ppermute | solution.py:573
  20.9 32.2 %collective-permute-start.3 = (f32[5,3,112,128]{3,2,1,0:T(8,128)}, f32[5,3,112,128]{3,2,1,0:T(8,128)}, u32[]{:S(2)}, u32[]{:S(2)}) collective-permute-start(f32[5,3,112,128]{3,2,1,0:T(8,128)} %get-tuple-element.24), channel_id=1, source_target_pairs={{0,120},{8,0},{16,8},{24,16},{32,24},{40,32},{48,40},{56,48},{64,5... | collective-permute-start | bytes 2580488 | tf_op jit(solution)/shard_map/ppermute | solution.py:573
  49.4 43.5 %all-to-all-start = ((f32[16,2,16,1024]{3,2,1,0:T(8,128)}), f32[16,2,16,1024]{3,2,1,0:T(8,128)S(1)}, u32[]{:S(2)}, u32[]{:S(2)}) async-start(f32[16,2,16,1024]{3,2,1,0:T(8,128)} %bitcast.5), calls=%async_computation | async-start | bytes 4194304 | tf_op jit(solution)/shard_map/all_to_all | solution.py:620
  53.1 0.9 copy-start
  66.7 17.9 %collective-permute-start.4 = (f32[2,112,128]{2,1,0:T(8,128)}, f32[2,112,128]{2,1,0:T(8,128)S(1)}, u32[]{:S(2)}, u32[]{:S(2)}) collective-permute-start(f32[2,112,128]{2,1,0:T(8,128)} %get-tuple-element.33), channel_id=1, source_target_pairs={{0,8},{8,16},{16,24},{24,32},{32,40},{40,48},{48,56},{56,64},{64,7... | collective-permute-start | bytes 344072 | tf_op jit(solution)/shard_map/ppermute | solution.py:573
  68.7 19.0 %collective-permute-start.5 = (f32[2,112,128]{2,1,0:T(8,128)}, f32[2,112,128]{2,1,0:T(8,128)S(1)}, u32[]{:S(2)}, u32[]{:S(2)}) collective-permute-start(f32[2,112,128]{2,1,0:T(8,128)} %get-tuple-element.34), channel_id=1, source_target_pairs={{0,120},{8,0},{16,8},{24,16},{32,24},{40,32},{48,40},{56,48},{64,5... | collective-permute-start | bytes 344072 | tf_op jit(solution)/shard_map/ppermute | solution.py:573
  84.6 3.1 %copy-start.3 = (f32[2,112,128]{2,1,0:T(8,128)}, f32[2,112,128]{2,1,0:T(8,128)S(1)}, u32[]{:S(2)}) copy-start(f32[2,112,128]{2,1,0:T(8,128)S(1)} %collective-permute-done.4.from_prev) | copy-start | bytes 344068
  87.7 0.7 copy-start.4

commit v7 on v6

--- a/solution.py
+++ b/solution.py
@@ -25,7 +25,7 @@
 SOUND = math.sqrt(5.0 / 3.0)
 TINY = 1e-30
 COST = 1_100_000_000
-VMEM_LIMIT = 54 * 1024 * 1024
+VMEM_LIMIT = 64 * 1024 * 1024
 
 
 def limit(value, other):
@@ -162,7 +162,7 @@
     lax.fori_loop(0, tiles, tile, 0)
 
 
-U = 20
+U = 50
 PAIR = 2
 
 

time: 133 us -> 132 us (level)
  local copies, waits for them, and re-layouts: 3.43 us -> 0.14 us
  Pallas kernels: 56.9 us -> 55.3 us
  other arithmetic: 2.6 us -> 4.2 us
    unnamed x10 -> x0, local copies, waits for them, and re-layouts: 3.3 us -> none
    broadcast_in_dim x1, other arithmetic: 2.6 us -> 4.2 us  [body(): return (new_density, new_momentum, new_energy, kd[None, None])]
  transfers between devices with their start and end apart: 7 -> 7, of which waited for: 2 -> 2; matrix products, arithmetic and copies ran while one was open for 0% -> 0% of each run, Pallas kernels for 39% -> 38%
where the time goes in v7:
time: 132 us; the launch traced here: 131 us
  Pallas kernels  55.3 us (42%)
  blocking collectives  36.7 us (28%)
  starting transfers between devices  17 us (13%)
  waiting for transfers between devices  16.5 us (12%)
  other arithmetic  4.2 us (3%)
    all_to_all x1, blocking collectives, exchange(): lax.all_to_all(send.reshape(16, 2, planes, 1024), 'box', split_axis=0, co...  36.7 us
    pallas_call x1, Pallas kernels, body(): pl.pallas_call(inner_kernel, out_shape=FIELD_SHAPES + (shape(WIDE, FRAME,...  23.3 us
    ppermute x6, waiting for transfers between devices, shifted(): lax.ppermute(value, axis, [(i, (i + by) % size) for i in range(size)])  16.5 us
    ppermute x6, starting transfers between devices, shifted(): lax.ppermute(value, axis, [(i, (i + by) % size) for i in range(size)])  12.6 us
    pallas_call x1, Pallas kernels, body(): pl.pallas_call(outer_kernel, out_shape=FIELD_SHAPES + (shape(8, FRAME, NZ...  12.3 us
    pallas_call x1, Pallas kernels, body(): pl.pallas_call(x_kernel, out_shape=shape(5, WIDE, NY, NZ), in_specs=[ANY]...  10 us
    pallas_call x1, Pallas kernels, body(): pl.pallas_call(rest_kernel, out_shape=shape(32, 16, 1024), in_specs=[SMEM...  4.49 us
    all_to_all x1, starting transfers between devices, exchange(): lax.all_to_all(send.reshape(16, 2, planes, 1024), 'box', split_axis=0, co...  4.45 us
  transfers between devices with their start and end apart: 7, of which 2 were waited for; matrix products, arithmetic and copies ran while one was open for 0% of the time, Pallas kernels for 38%

profile of v7, /device:TPU:32, one launch (start us, length us, event | category | flops | bytes accessed | tf_op | source)
XLA Modules:
  0.0 130.6 jit_solution(12111184960203858468)
XLA Ops:
  0.6 2.5 %pack_y.1 = (f32[6,32,8,128]{3,2,1,0:T(8,128)}, f32[6,32,8,128]{3,2,1,0:T(8,128)}) custom-call(f32[32,96,128]{2,1,0:T(8,128)} %density.7, f32[3,32,96,128]{3,2,1,0:T(8,128)} %momentum.7, f32[32,96,128]{2,1,0:T(8,128)} %energy.7, f32[32,96,128]{2,1,0:T(8,128)} %dm.5), custom_call_target="tpu_custom_call" | custom-call | flops 3300000000 | tf_op jit(solution)/shard_map/pack_y/pallas_call | solution.py:580
  3.2 0.0 collective-permute-start
  3.2 1.7 %collective-permute-start.1 = (f32[6,32,8,128]{3,2,1,0:T(8,128)}, f32[6,32,8,128]{3,2,1,0:T(8,128)}, u32[]{:S(2)}, u32[]{:S(2)}) collective-permute-start(f32[6,32,8,128]{3,2,1,0:T(8,128)} %get-tuple-element.22), channel_id=1, source_target_pairs={{0,7},{1,0},{2,1},{3,2},{4,3},{5,4},{6,5},{7,6},{8,15},{9,8},{10,9... | collective-permute-start | bytes 2359304 | tf_op jit(solution)/shard_map/ppermute | solution.py:573
  4.9 10.0 %x_own.1.swept = f32[5,24,96,128]{3,2,1,0:T(8,128)} custom-call(f32[32,96,128]{2,1,0:T(8,128)} %density.7, f32[3,32,96,128]{3,2,1,0:T(8,128)} %momentum.7, f32[32,96,128]{2,1,0:T(8,128)} %energy.7), custom_call_target="tpu_custom_call" | custom-call | flops 9900000256 | tf_op jit(solution)/shard_map/x_own/pallas_call | solution.py:593
  14.9 0.0 collective-permute-done.y_before
  15.0 0.0 collective-permute-done.1.y_after
  15.0 2.6 %pack_x.1 = (f32[5,3,112,128]{3,2,1,0:T(8,128)}, f32[5,3,112,128]{3,2,1,0:T(8,128)}) custom-call(f32[32,96,128]{2,1,0:T(8,128)} %density.7, f32[3,32,96,128]{3,2,1,0:T(8,128)} %momentum.7, f32[32,96,128]{2,1,0:T(8,128)} %energy.7, f32[6,32,8,128]{3,2,1,0:T(8,128)} %collective-permute-done.y_before, f32[6,32,8,128]{3,2,1,0:T(8,128)} %collective-permute-done.1.y_after), custom_call_target="tpu_custom_call" | custom-call | flops 3300000000 | tf_op jit(solution)/shard_map/pack_x/pallas_call | solution.py:606
  17.6 1.6 %collective-permute-start.2 = (f32[5,3,112,128]{3,2,1,0:T(8,128)}, f32[5,3,112,128]{3,2,1,0:T(8,128)}, u32[]{:S(2)}, u32[]{:S(2)}) collective-permute-start(f32[5,3,112,128]{3,2,1,0:T(8,128)} %get-tuple-element.23), channel_id=1, source_target_pairs={{0,8},{8,16},{16,24},{24,32},{32,40},{40,48},{48,56},{56,64},{64,7... | collective-permute-start | bytes 2580488 | tf_op jit(solution)/shard_map/ppermute | solution.py:573
  19.1 3.9 %collective-permute-start.3 = (f32[5,3,112,128]{3,2,1,0:T(8,128)}, f32[5,3,112,128]{3,2,1,0:T(8,128)}, u32[]{:S(2)}, u32[]{:S(2)}) collective-permute-start(f32[5,3,112,128]{3,2,1,0:T(8,128)} %get-tuple-element.24), channel_id=1, source_target_pairs={{0,120},{8,0},{16,8},{24,16},{32,24},{40,32},{48,40},{56,48},{64,5... | collective-permute-start | bytes 2580488 | tf_op jit(solution)/shard_map/ppermute | solution.py:573
  23.0 23.3 %inner.1 = (f32[32,96,128]{2,1,0:T(8,128)}, f32[3,32,96,128]{3,2,1,0:T(8,128)}, f32[32,96,128]{2,1,0:T(8,128)}, f32[24,112,128]{2,1,0:T(8,128)}, f32[32,16,1024]{2,1,0:T(8,128)}) custom-call(s32[12]{0:T(128)} %bitcast.7, bf16[256,384]{1,0:T(8,128)(2,1)} %constant.2.clone.weights, f32[5,24,96,128]{3,2,1,0:T(8,128)} %x_own.1.swept, f32[32,96,128]{2,1,0:T(8,128)} %dm.5, ...), custom_call_target="tpu_custom_call" | custom-call | flops 28600000512 | tf_op jit(solution)/shard_map/inner/pallas_call | solution.py:622
  46.4 4.5 %all-to-all-start = ((f32[16,2,16,1024]{3,2,1,0:T(8,128)}), f32[16,2,16,1024]{3,2,1,0:T(8,128)}, u32[]{:S(2)}, u32[]{:S(2)}) async-start(f32[16,2,16,1024]{3,2,1,0:T(8,128)} %bitcast.5), calls=%async_computation | async-start | bytes 4194304 | tf_op jit(solution)/shard_map/all_to_all | solution.py:620
  50.8 0.0 collective-permute-done.2.x_before
  50.8 0.0 collective-permute-done.3.x_after
  50.8 12.3 %outer.1 = (f32[32,96,128]{2,1,0:T(8,128)}, f32[3,32,96,128]{3,2,1,0:T(8,128)}, f32[32,96,128]{2,1,0:T(8,128)}, f32[8,112,128]{2,1,0:T(8,128)}, f32[2,112,128]{2,1,0:T(8,128)}, /*index=5*/f32[2,112,128]{2,1,0:T(8,128)}) custom-call(bf16[256,384]{1,0:T(8,128)(2,1)} %constant.2.clone.weights, ...), custom_call_target="tpu_custom_call", output_to_operand_aliasing={{0}: (9, {}), {1}: (10, {}), {2}: (11, {})} | custom-call | flops 14300000256 | tf_op jit(solution)/shard_map/outer/pallas_call | solution.py:635
  63.2 1.8 %collective-permute-start.4 = (f32[2,112,128]{2,1,0:T(8,128)}, f32[2,112,128]{2,1,0:T(8,128)}, u32[]{:S(2)}, u32[]{:S(2)}) collective-permute-start(f32[2,112,128]{2,1,0:T(8,128)} %get-tuple-element.33), channel_id=1, source_target_pairs={{0,8},{8,16},{16,24},{24,32},{32,40},{40,48},{48,56},{56,64},{64,7... | collective-permute-start | bytes 344072 | tf_op jit(solution)/shard_map/ppermute | solution.py:573
  65.0 3.6 %collective-permute-start.5 = (f32[2,112,128]{2,1,0:T(8,128)}, f32[2,112,128]{2,1,0:T(8,128)}, u32[]{:S(2)}, u32[]{:S(2)}) collective-permute-start(f32[2,112,128]{2,1,0:T(8,128)} %get-tuple-element.34), channel_id=1, source_target_pairs={{0,120},{8,0},{16,8},{24,16},{32,24},{40,32},{48,40},{56,48},{64,5... | collective-permute-start | bytes 344072 | tf_op jit(solution)/shard_map/ppermute | solution.py:573
  68.6 13.3 %collective-permute-done.4.from_prev = f32[2,112,128]{2,1,0:T(8,128)} collective-permute-done((f32[2,112,128]{2,1,0:T(8,128)}, f32[2,112,128]{2,1,0:T(8,128)}, u32[]{:S(2)}, u32[]{:S(2)}) %collective-permute-start.4) | collective-permute-done | bytes 114720 | tf_op jit(solution)/shard_map/ppermute | solution.py:573
  81.9 3.2 %collective-permute-done.5.from_next = f32[2,112,128]{2,1,0:T(8,128)} collective-permute-done((f32[2,112,128]{2,1,0:T(8,128)}, f32[2,112,128]{2,1,0:T(8,128)}, u32[]{:S(2)}, u32[]{:S(2)}) %collective-permute-start.5) | collective-permute-done | bytes 114720 | tf_op jit(solution)/shard_map/ppermute | solution.py:573
  85.0 4.5 %rest.1 = f32[32,16,1024]{2,1,0:T(8,128)} custom-call(s32[12]{0:T(128)} %bitcast.8, f32[24,112,128]{2,1,0:T(8,128)} %get-tuple-element.31.sums_inner, f32[8,112,128]{2,1,0:T(8,128)} %get-tuple-element.32.sums_outer, f32[2,112,128]{2,1,0:T(8,128)} %collective-permute-done.4.from_prev, f32[2,112,128]{2,1,0:T(8,128)} %collective-permute-done.5.from_next), custom_call_target="tpu_custom_call" | custom-call | flops 5500000256 | tf_op jit(solution)/shard_map/rest/pallas_call | solution.py:649
  89.5 0.0 all-to-all-done
  89.5 36.7 %all_to_all.10 = f32[16,2,16,1024]{3,2,1,0:T(8,128)S(1)} all-to-all(f32[16,2,16,1024]{3,2,1,0:T(8,128)} %bitcast.6), channel_id=1, replica_groups=mesh['box'=16,'grp'=8] {'box'}, dimensions={0} | all-to-all | bytes 4194304 | tf_op jit(solution)/shard_map/all_to_all | solution.py:620
  126.3 0.1 fusion
  126.4 4.2 %maximum_bitcast_fusion = f32[1,1,16,2,32,1024]{5,4,3,2,1,0:T(8,128)} fusion(f32[16,2,8,1024]{3,2,1,0:T(8,128)S(1)} %get-tuple-element.39, f32[16,2,16,1024]{3,2,1,0:T(8,128)} %all-to-all-done, f32[16,2,8,1024]{3,2,1,0:T(8,128)S(1)} %get-tuple-element.38), kind=kLoop, calls=%fused_computation | loop fusion | flops 2097152 | bytes 8388608 | tf_op jit(solution)/shard_map/broadcast_in_dim | solution.py:662
Async XLA Ops:
  3.2 11.8 %collective-permute-start = (f32[6,32,8,128]{3,2,1,0:T(8,128)}, f32[6,32,8,128]{3,2,1,0:T(8,128)}, u32[]{:S(2)}, u32[]{:S(2)}) collective-permute-start(f32[6,32,8,128]{3,2,1,0:T(8,128)} %get-tuple-element.21), channel_id=1, source_target_pairs={{0,1},{1,2},{2,3},{3,4},{4,5},{5,6},{6,7},{7,0},{8,9},{9,10},{10,1... | collective-permute-start | bytes 2359304 | tf_op jit(solution)/shard_map/ppermute | solution.py:573
  3.2 11.7 %collective-permute-start.1 = (f32[6,32,8,128]{3,2,1,0:T(8,128)}, f32[6,32,8,128]{3,2,1,0:T(8,128)}, u32[]{:S(2)}, u32[]{:S(2)}) collective-permute-start(f32[6,32,8,128]{3,2,1,0:T(8,128)} %get-tuple-element.22), channel_id=1, source_target_pairs={{0,7},{1,0},{2,1},{3,2},{4,3},{5,4},{6,5},{7,6},{8,15},{9,8},{10,9... | collective-permute-start | bytes 2359304 | tf_op jit(solution)/shard_map/ppermute | solution.py:573
  17.6 33.2 %collective-permute-start.2 = (f32[5,3,112,128]{3,2,1,0:T(8,128)}, f32[5,3,112,128]{3,2,1,0:T(8,128)}, u32[]{:S(2)}, u32[]{:S(2)}) collective-permute-start(f32[5,3,112,128]{3,2,1,0:T(8,128)} %get-tuple-element.23), channel_id=1, source_target_pairs={{0,8},{8,16},{16,24},{24,32},{32,40},{40,48},{48,56},{56,64},{64,7... | collective-permute-start | bytes 2580488 | tf_op jit(solution)/shard_map/ppermute | solution.py:573
  19.1 31.7 %collective-permute-start.3 = (f32[5,3,112,128]{3,2,1,0:T(8,128)}, f32[5,3,112,128]{3,2,1,0:T(8,128)}, u32[]{:S(2)}, u32[]{:S(2)}) collective-permute-start(f32[5,3,112,128]{3,2,1,0:T(8,128)} %get-tuple-element.24), channel_id=1, source_target_pairs={{0,120},{8,0},{16,8},{24,16},{32,24},{40,32},{48,40},{56,48},{64,5... | collective-permute-start | bytes 2580488 | tf_op jit(solution)/shard_map/ppermute | solution.py:573
  46.4 43.2 %all-to-all-start = ((f32[16,2,16,1024]{3,2,1,0:T(8,128)}), f32[16,2,16,1024]{3,2,1,0:T(8,128)}, u32[]{:S(2)}, u32[]{:S(2)}) async-start(f32[16,2,16,1024]{3,2,1,0:T(8,128)} %bitcast.5), calls=%async_computation | async-start | bytes 4194304 | tf_op jit(solution)/shard_map/all_to_all | solution.py:620
  63.2 18.7 %collective-permute-start.4 = (f32[2,112,128]{2,1,0:T(8,128)}, f32[2,112,128]{2,1,0:T(8,128)}, u32[]{:S(2)}, u32[]{:S(2)}) collective-permute-start(f32[2,112,128]{2,1,0:T(8,128)} %get-tuple-element.33), channel_id=1, source_target_pairs={{0,8},{8,16},{16,24},{24,32},{32,40},{40,48},{48,56},{56,64},{64,7... | collective-permute-start | bytes 344072 | tf_op jit(solution)/shard_map/ppermute | solution.py:573
  65.0 20.1 %collective-permute-start.5 = (f32[2,112,128]{2,1,0:T(8,128)}, f32[2,112,128]{2,1,0:T(8,128)}, u32[]{:S(2)}, u32[]{:S(2)}) collective-permute-start(f32[2,112,128]{2,1,0:T(8,128)} %get-tuple-element.34), channel_id=1, source_target_pairs={{0,120},{8,0},{16,8},{24,16},{32,24},{40,32},{48,40},{56,48},{64,5... | collective-permute-start | bytes 344072 | tf_op jit(solution)/shard_map/ppermute | solution.py:573

commit v8 on v7

--- a/solution.py
+++ b/solution.py
@@ -25,7 +25,7 @@
 SOUND = math.sqrt(5.0 / 3.0)
 TINY = 1e-30
 COST = 1_100_000_000
-VMEM_LIMIT = 64 * 1024 * 1024
+MIB = 1024 * 1024
 
 
 def limit(value, other):
@@ -536,8 +536,8 @@
     return jax.ShapeDtypeStruct(dims, F32)
 
 
-def params():
-    return pltpu.CompilerParams(vmem_limit_bytes=VMEM_LIMIT)
+def params(mib):
+    return pltpu.CompilerParams(vmem_limit_bytes=mib * MIB)
 
 
 def cost(micros):
@@ -583,7 +583,7 @@
         in_specs=[ANY] * 4,
         out_specs=[VMEM] * 2,
         scratch_shapes=[pltpu.SemaphoreType.DMA],
-        compiler_params=params(),
+        compiler_params=params(64),
         cost_estimate=cost(3),
         name="pack_y",
     )(density, momentum, energy, dm_density)
@@ -598,7 +598,7 @@
         scratch_shapes=[
             pltpu.VMEM((5, WIDE + 6, NY, NZ), F32), pltpu.VMEM((5, WIDE, NY, NZ), F32),
             pltpu.SemaphoreType.DMA((NY // 8,)), pltpu.SemaphoreType.DMA],
-        compiler_params=params(),
+        compiler_params=params(64),
         cost_estimate=cost(9),
         name="x_own",
     )(*fields)
@@ -609,7 +609,7 @@
         in_specs=[ANY] * 5,
         out_specs=[VMEM] * 2,
         scratch_shapes=[pltpu.SemaphoreType.DMA],
-        compiler_params=params(),
+        compiler_params=params(64),
         cost_estimate=cost(3),
         name="pack_x",
     )(*fields, y_before, y_after)
@@ -625,7 +625,7 @@
         in_specs=[SMEM] + [ANY] * 5,
         out_specs=[ANY] * 4 + [VMEM],
         scratch_shapes=main_scratch(WIDE, WIDE + 6, 16) + smooth_scratch() + semaphores(),
-        compiler_params=params(),
+        compiler_params=params(64),
         cost_estimate=cost(26),
         name="inner",
     )(dest, weights, swept, dm_density, y_before, y_after)
@@ -639,7 +639,7 @@
         out_specs=[ANY] * 6,
         scratch_shapes=main_scratch(8, 20, FRAME) + semaphores(),
         input_output_aliases={9: 0, 10: 1, 11: 2},
-        compiler_params=params(),
+        compiler_params=params(54),
         cost_estimate=cost(13),
         name="outer",
     )(weights, *fields, dm_density, y_before, y_after, x_before, x_after, *made)
@@ -652,7 +652,7 @@
         in_specs=[SMEM] + [ANY] * 4,
         out_specs=VMEM,
         scratch_shapes=[pltpu.VMEM((24, FRAME, NZ), F32)] + smooth_scratch() + [pltpu.SemaphoreType.DMA],
-        compiler_params=params(),
+        compiler_params=params(54),
         cost_estimate=cost(5),
         name="rest",
     )(dest, sums_inner, sums_outer, from_prev, from_next)

time: 132 us -> 130 us (0.985)
  other arithmetic: 4.2 us -> 2.55 us
    broadcast_in_dim x1, other arithmetic: 4.2 us -> 2.55 us  [body(): return (new_density, new_momentum, new_energy, kd[None, None])]
  transfers between devices with their start and end apart: 7 -> 7, of which waited for: 2 -> 2; matrix products, arithmetic and copies ran while one was open for 0% -> 0% of each run, Pallas kernels for 38% -> 39%
where the time goes in v8:
time: 130 us; the launch traced here: 129 us
  Pallas kernels  55.3 us (43%)
  blocking collectives  36.6 us (28%)
  waiting for transfers between devices  16.8 us (13%)
  starting transfers between devices  16.3 us (13%)
  other arithmetic  2.55 us (2%)
    all_to_all x1, blocking collectives, exchange(): lax.all_to_all(send.reshape(16, 2, planes, 1024), 'box', split_axis=0, co...  36.6 us
    pallas_call x1, Pallas kernels, body(): pl.pallas_call(inner_kernel, out_shape=FIELD_SHAPES + (shape(WIDE, FRAME,...  23.4 us
    ppermute x6, waiting for transfers between devices, shifted(): lax.ppermute(value, axis, [(i, (i + by) % size) for i in range(size)])  16.8 us
    ppermute x6, starting transfers between devices, shifted(): lax.ppermute(value, axis, [(i, (i + by) % size) for i in range(size)])  12.6 us
    pallas_call x1, Pallas kernels, body(): pl.pallas_call(outer_kernel, out_shape=FIELD_SHAPES + (shape(8, FRAME, NZ...  12.3 us
    pallas_call x1, Pallas kernels, body(): pl.pallas_call(x_kernel, out_shape=shape(5, WIDE, NY, NZ), in_specs=[ANY]...  9.99 us
    pallas_call x1, Pallas kernels, body(): pl.pallas_call(rest_kernel, out_shape=shape(32, 16, 1024), in_specs=[SMEM...  4.49 us
    all_to_all x1, starting transfers between devices, exchange(): lax.all_to_all(send.reshape(16, 2, planes, 1024), 'box', split_axis=0, co...  3.74 us
  transfers between devices with their start and end apart: 7, of which 2 were waited for; matrix products, arithmetic and copies ran while one was open for 0% of the time, Pallas kernels for 39%

profile of v8, /device:TPU:32, one launch (start us, length us, event | category | flops | bytes accessed | tf_op | source)
XLA Modules:
  0.0 129.1 jit_solution(6260053740659252792)
XLA Ops:
  0.6 2.5 %pack_y.1 = (f32[6,32,8,128]{3,2,1,0:T(8,128)}, f32[6,32,8,128]{3,2,1,0:T(8,128)}) custom-call(f32[32,96,128]{2,1,0:T(8,128)} %density.7, f32[3,32,96,128]{3,2,1,0:T(8,128)} %momentum.7, f32[32,96,128]{2,1,0:T(8,128)} %energy.7, f32[32,96,128]{2,1,0:T(8,128)} %dm.5), custom_call_target="tpu_custom_call" | custom-call | flops 3300000000 | tf_op jit(solution)/shard_map/pack_y/pallas_call | solution.py:580
  3.2 0.0 collective-permute-start
  3.2 1.7 %collective-permute-start.1 = (f32[6,32,8,128]{3,2,1,0:T(8,128)}, f32[6,32,8,128]{3,2,1,0:T(8,128)}, u32[]{:S(2)}, u32[]{:S(2)}) collective-permute-start(f32[6,32,8,128]{3,2,1,0:T(8,128)} %get-tuple-element.22), channel_id=1, source_target_pairs={{0,7},{1,0},{2,1},{3,2},{4,3},{5,4},{6,5},{7,6},{8,15},{9,8},{10,9... | collective-permute-start | bytes 2359304 | tf_op jit(solution)/shard_map/ppermute | solution.py:573
  4.9 10.0 %x_own.1.swept = f32[5,24,96,128]{3,2,1,0:T(8,128)} custom-call(f32[32,96,128]{2,1,0:T(8,128)} %density.7, f32[3,32,96,128]{3,2,1,0:T(8,128)} %momentum.7, f32[32,96,128]{2,1,0:T(8,128)} %energy.7), custom_call_target="tpu_custom_call" | custom-call | flops 9900000256 | tf_op jit(solution)/shard_map/x_own/pallas_call | solution.py:593
  14.9 0.0 collective-permute-done.y_before
  14.9 0.0 collective-permute-done.1.y_after
  15.0 2.6 %pack_x.1 = (f32[5,3,112,128]{3,2,1,0:T(8,128)}, f32[5,3,112,128]{3,2,1,0:T(8,128)}) custom-call(f32[32,96,128]{2,1,0:T(8,128)} %density.7, f32[3,32,96,128]{3,2,1,0:T(8,128)} %momentum.7, f32[32,96,128]{2,1,0:T(8,128)} %energy.7, f32[6,32,8,128]{3,2,1,0:T(8,128)} %collective-permute-done.y_before, f32[6,32,8,128]{3,2,1,0:T(8,128)} %collective-permute-done.1.y_after), custom_call_target="tpu_custom_call" | custom-call | flops 3300000000 | tf_op jit(solution)/shard_map/pack_x/pallas_call | solution.py:606
  17.6 1.6 %collective-permute-start.2 = (f32[5,3,112,128]{3,2,1,0:T(8,128)}, f32[5,3,112,128]{3,2,1,0:T(8,128)}, u32[]{:S(2)}, u32[]{:S(2)}) collective-permute-start(f32[5,3,112,128]{3,2,1,0:T(8,128)} %get-tuple-element.23), channel_id=1, source_target_pairs={{0,8},{8,16},{16,24},{24,32},{32,40},{40,48},{48,56},{56,64},{64,7... | collective-permute-start | bytes 2580488 | tf_op jit(solution)/shard_map/ppermute | solution.py:573
  19.1 3.9 %collective-permute-start.3 = (f32[5,3,112,128]{3,2,1,0:T(8,128)}, f32[5,3,112,128]{3,2,1,0:T(8,128)}, u32[]{:S(2)}, u32[]{:S(2)}) collective-permute-start(f32[5,3,112,128]{3,2,1,0:T(8,128)} %get-tuple-element.24), channel_id=1, source_target_pairs={{0,120},{8,0},{16,8},{24,16},{32,24},{40,32},{48,40},{56,48},{64,5... | collective-permute-start | bytes 2580488 | tf_op jit(solution)/shard_map/ppermute | solution.py:573
  23.0 23.4 %inner.1 = (f32[32,96,128]{2,1,0:T(8,128)}, f32[3,32,96,128]{3,2,1,0:T(8,128)}, f32[32,96,128]{2,1,0:T(8,128)}, f32[24,112,128]{2,1,0:T(8,128)}, f32[32,16,1024]{2,1,0:T(8,128)}) custom-call(s32[12]{0:T(128)} %bitcast.7, bf16[256,384]{1,0:T(8,128)(2,1)} %constant.2.clone.weights, f32[5,24,96,128]{3,2,1,0:T(8,128)} %x_own.1.swept, f32[32,96,128]{2,1,0:T(8,128)} %dm.5, ...), custom_call_target="tpu_custom_call" | custom-call | flops 28600000512 | tf_op jit(solution)/shard_map/inner/pallas_call | solution.py:622
  46.3 3.7 %all-to-all-start = ((f32[16,2,16,1024]{3,2,1,0:T(8,128)}), f32[16,2,16,1024]{3,2,1,0:T(8,128)S(1)}, u32[]{:S(2)}, u32[]{:S(2)}) async-start(f32[16,2,16,1024]{3,2,1,0:T(8,128)} %bitcast.5), calls=%async_computation | async-start | bytes 4194304 | tf_op jit(solution)/shard_map/all_to_all | solution.py:620
  50.1 0.0 collective-permute-done.2.x_before
  50.1 0.0 collective-permute-done.3.x_after
  50.1 12.3 %outer.1 = (f32[32,96,128]{2,1,0:T(8,128)}, f32[3,32,96,128]{3,2,1,0:T(8,128)}, f32[32,96,128]{2,1,0:T(8,128)}, f32[8,112,128]{2,1,0:T(8,128)}, f32[2,112,128]{2,1,0:T(8,128)}, /*index=5*/f32[2,112,128]{2,1,0:T(8,128)}) custom-call(bf16[256,384]{1,0:T(8,128)(2,1)} %constant.2.clone.weights, ...), custom_call_target="tpu_custom_call", output_to_operand_aliasing={{0}: (9, {}), {1}: (10, {}), {2}: (11, {})} | custom-call | flops 14300000256 | tf_op jit(solution)/shard_map/outer/pallas_call | solution.py:635
  62.4 2.0 %collective-permute-start.4 = (f32[2,112,128]{2,1,0:T(8,128)}, f32[2,112,128]{2,1,0:T(8,128)S(1)}, u32[]{:S(2)}, u32[]{:S(2)}) collective-permute-start(f32[2,112,128]{2,1,0:T(8,128)} %get-tuple-element.33), channel_id=1, source_target_pairs={{0,8},{8,16},{16,24},{24,32},{32,40},{40,48},{48,56},{56,64},{64,7... | collective-permute-start | bytes 344072 | tf_op jit(solution)/shard_map/ppermute | solution.py:573
  64.4 3.4 %collective-permute-start.5 = (f32[2,112,128]{2,1,0:T(8,128)}, f32[2,112,128]{2,1,0:T(8,128)S(1)}, u32[]{:S(2)}, u32[]{:S(2)}) collective-permute-start(f32[2,112,128]{2,1,0:T(8,128)} %get-tuple-element.34), channel_id=1, source_target_pairs={{0,120},{8,0},{16,8},{24,16},{32,24},{40,32},{48,40},{56,48},{64,5... | collective-permute-start | bytes 344072 | tf_op jit(solution)/shard_map/ppermute | solution.py:573
  67.8 13.3 %collective-permute-done.4.from_prev = f32[2,112,128]{2,1,0:T(8,128)S(1)} collective-permute-done((f32[2,112,128]{2,1,0:T(8,128)}, f32[2,112,128]{2,1,0:T(8,128)S(1)}, u32[]{:S(2)}, u32[]{:S(2)}) %collective-permute-start.4) | collective-permute-done | bytes 114720 | tf_op jit(solution)/shard_map/ppermute | solution.py:573
  81.1 0.0 copy-start
  81.1 3.5 %collective-permute-done.5.from_next = f32[2,112,128]{2,1,0:T(8,128)S(1)} collective-permute-done((f32[2,112,128]{2,1,0:T(8,128)}, f32[2,112,128]{2,1,0:T(8,128)S(1)}, u32[]{:S(2)}, u32[]{:S(2)}) %collective-permute-start.5) | collective-permute-done | bytes 114720 | tf_op jit(solution)/shard_map/ppermute | solution.py:573
  84.6 0.0 copy-start.1
  84.6 0.0 copy-done
  84.6 0.6 copy-done.1
  85.3 4.5 %rest.1 = f32[32,16,1024]{2,1,0:T(8,128)} custom-call(s32[12]{0:T(128)} %bitcast.8, f32[24,112,128]{2,1,0:T(8,128)} %get-tuple-element.31.sums_inner, f32[8,112,128]{2,1,0:T(8,128)} %get-tuple-element.32.sums_outer, f32[2,112,128]{2,1,0:T(8,128)} %copy-done, f32[2,112,128]{2,1,0:T(8,128)} %copy-done.1), custom_call_target="tpu_custom_call" | custom-call | flops 5500000256 | tf_op jit(solution)/shard_map/rest/pallas_call | solution.py:649
  89.7 0.0 all-to-all-done
  89.8 36.6 %all_to_all.10 = f32[16,2,16,1024]{3,2,1,0:T(8,128)S(1)} all-to-all(f32[16,2,16,1024]{3,2,1,0:T(8,128)} %bitcast.6), channel_id=1, replica_groups=mesh['box'=16,'grp'=8] {'box'}, dimensions={0} | all-to-all | bytes 4194304 | tf_op jit(solution)/shard_map/all_to_all | solution.py:620
  126.4 0.1 fusion
  126.5 2.5 %maximum_bitcast_fusion = f32[1,1,16,2,32,1024]{5,4,3,2,1,0:T(8,128)} fusion(f32[16,2,8,1024]{3,2,1,0:T(8,128)S(1)} %get-tuple-element.39, f32[16,2,16,1024]{3,2,1,0:T(8,128)S(1)} %all-to-all-done, f32[16,2,8,1024]{3,2,1,0:T(8,128)S(1)} %get-tuple-element.38), kind=kLoop, calls=%fused_computation | loop fusion | flops 2097152 | bytes 8388608 | tf_op jit(solution)/shard_map/broadcast_in_dim | solution.py:662
Async XLA Ops:
  3.2 11.8 %collective-permute-start = (f32[6,32,8,128]{3,2,1,0:T(8,128)}, f32[6,32,8,128]{3,2,1,0:T(8,128)}, u32[]{:S(2)}, u32[]{:S(2)}) collective-permute-start(f32[6,32,8,128]{3,2,1,0:T(8,128)} %get-tuple-element.21), channel_id=1, source_target_pairs={{0,1},{1,2},{2,3},{3,4},{4,5},{5,6},{6,7},{7,0},{8,9},{9,10},{10,1... | collective-permute-start | bytes 2359304 | tf_op jit(solution)/shard_map/ppermute | solution.py:573
  3.2 11.7 %collective-permute-start.1 = (f32[6,32,8,128]{3,2,1,0:T(8,128)}, f32[6,32,8,128]{3,2,1,0:T(8,128)}, u32[]{:S(2)}, u32[]{:S(2)}) collective-permute-start(f32[6,32,8,128]{3,2,1,0:T(8,128)} %get-tuple-element.22), channel_id=1, source_target_pairs={{0,7},{1,0},{2,1},{3,2},{4,3},{5,4},{6,5},{7,6},{8,15},{9,8},{10,9... | collective-permute-start | bytes 2359304 | tf_op jit(solution)/shard_map/ppermute | solution.py:573
  17.6 32.5 %collective-permute-start.2 = (f32[5,3,112,128]{3,2,1,0:T(8,128)}, f32[5,3,112,128]{3,2,1,0:T(8,128)}, u32[]{:S(2)}, u32[]{:S(2)}) collective-permute-start(f32[5,3,112,128]{3,2,1,0:T(8,128)} %get-tuple-element.23), channel_id=1, source_target_pairs={{0,8},{8,16},{16,24},{24,32},{32,40},{40,48},{48,56},{56,64},{64,7... | collective-permute-start | bytes 2580488 | tf_op jit(solution)/shard_map/ppermute | solution.py:573
  19.1 31.0 %collective-permute-start.3 = (f32[5,3,112,128]{3,2,1,0:T(8,128)}, f32[5,3,112,128]{3,2,1,0:T(8,128)}, u32[]{:S(2)}, u32[]{:S(2)}) collective-permute-start(f32[5,3,112,128]{3,2,1,0:T(8,128)} %get-tuple-element.24), channel_id=1, source_target_pairs={{0,120},{8,0},{16,8},{24,16},{32,24},{40,32},{48,40},{56,48},{64,5... | collective-permute-start | bytes 2580488 | tf_op jit(solution)/shard_map/ppermute | solution.py:573
  46.3 43.4 %all-to-all-start = ((f32[16,2,16,1024]{3,2,1,0:T(8,128)}), f32[16,2,16,1024]{3,2,1,0:T(8,128)S(1)}, u32[]{:S(2)}, u32[]{:S(2)}) async-start(f32[16,2,16,1024]{3,2,1,0:T(8,128)} %bitcast.5), calls=%async_computation | async-start | bytes 4194304 | tf_op jit(solution)/shard_map/all_to_all | solution.py:620
  62.4 18.7 %collective-permute-start.4 = (f32[2,112,128]{2,1,0:T(8,128)}, f32[2,112,128]{2,1,0:T(8,128)S(1)}, u32[]{:S(2)}, u32[]{:S(2)}) collective-permute-start(f32[2,112,128]{2,1,0:T(8,128)} %get-tuple-element.33), channel_id=1, source_target_pairs={{0,8},{8,16},{16,24},{24,32},{32,40},{40,48},{48,56},{56,64},{64,7... | collective-permute-start | bytes 344072 | tf_op jit(solution)/shard_map/ppermute | solution.py:573
  64.4 20.2 %collective-permute-start.5 = (f32[2,112,128]{2,1,0:T(8,128)}, f32[2,112,128]{2,1,0:T(8,128)S(1)}, u32[]{:S(2)}, u32[]{:S(2)}) collective-permute-start(f32[2,112,128]{2,1,0:T(8,128)} %get-tuple-element.34), channel_id=1, source_target_pairs={{0,120},{8,0},{16,8},{24,16},{32,24},{40,32},{48,40},{56,48},{64,5... | collective-permute-start | bytes 344072 | tf_op jit(solution)/shard_map/ppermute | solution.py:573
  81.1 3.5 %copy-start = (f32[2,112,128]{2,1,0:T(8,128)}, f32[2,112,128]{2,1,0:T(8,128)S(1)}, u32[]{:S(2)}) copy-start(f32[2,112,128]{2,1,0:T(8,128)S(1)} %collective-permute-done.4.from_prev) | copy-start | bytes 344068
  84.6 0.6 copy-start.1

commit v9 on v8

--- a/solution.py
+++ b/solution.py
@@ -227,6 +227,17 @@
 
 
 def smooth(planes, dest_ref, x_ref, y_ref, send_ref, send_row):
+    average(planes, x_ref, y_ref, 0)
+    put_boxes(dest_ref, y_ref, 0, send_ref, send_row)
+
+
+def five_rows(load):
+    parts = [load(k) for k in range(-2, 3)]
+    return (((parts[0] + parts[1]) + (parts[3] + parts[4])) + parts[2]) * (1.0 / 125.0)
+
+
+def average(planes, x_ref, y_ref, y_base):
+
     def x_tile(t, _):
         row = pl.multiple_of(t * 8, 8)
         values = [planes(p, row) for p in range(12)]
@@ -240,13 +251,13 @@
     def y_plane(p, _):
         for t in range(NY // 8):
             start = p * FRAME + 8 + 8 * t
-            parts = [x_ref[pl.ds(start + k, 8), :] for k in range(-2, 3)]
-            total = ((parts[0] + parts[1]) + (parts[3] + parts[4])) + parts[2]
-            y_ref[pl.ds(p * NY + 8 * t, 8), :] = total * (1.0 / 125.0)
+            y_ref[pl.ds(y_base + p * NY + 8 * t, 8), :] = five_rows(lambda k: x_ref[pl.ds(start + k, 8), :])
         return 0
 
     lax.fori_loop(0, 8, y_plane, 0)
 
+
+def put_boxes(dest_ref, y_ref, y_base, send_ref, send_row):
     places = []
     dests = [dest_ref[k] for k in range(12)]
     for k in range(12):
@@ -265,7 +276,7 @@
 
     for by in range(BOX_Y):
         for m in range(8):
-            s = [y_ref[pl.ds(by * BOX + 4 * m + q, 8, stride=NY), :] for q in range(4)]
+            s = [y_ref[pl.ds(y_base + by * BOX + 4 * m + q, 8, stride=NY), :] for q in range(4)]
             moved = []
             for k in range(4):
                 mixed = pick([s[(b + k) % 4] for b in range(4)])
@@ -508,23 +519,40 @@
     wait_all(leaving)
 
 
-def rest_kernel(dest, sums_inner, sums_outer, from_prev, from_next, send, w_ref, x_ref, y_ref, sem):
-    def part(src, own, place, count):
+def near_kernel(sums_inner, sums_outer, part, w_ref, x_ref, sem):
+    def planes(src, own, place, count):
         return pltpu.make_async_copy(src.at[pl.ds(own, count)], w_ref.at[pl.ds(place, count)], sem)
 
     copies = [
-        part(from_prev, 0, 0, 2),
-        part(sums_outer, 4, 2, 4),
-        part(sums_inner, 0, 6, 6),
-        part(sums_inner, 18, 12, 6),
-        part(sums_outer, 0, 18, 4),
-        part(from_next, 0, 22, 2),
+        planes(sums_outer, 4, 2, 4),
+        planes(sums_inner, 0, 6, 6),
+        planes(sums_inner, 18, 12, 6),
+        planes(sums_outer, 0, 18, 4),
+    ]
+    start_all(copies)
+    for p in (0, 1, 22, 23):
+        w_ref[p] = jnp.zeros((FRAME, NZ), F32)
+    wait_all(copies)
+    for n in range(2):
+        average(lambda p, r: w_ref[12 * n + p, pl.ds(r, 8), :], x_ref, part, n * 8 * NY)
+
+
+def rest_kernel(dest, part, from_prev, from_next, send, y_ref, f_ref, sem):
+    copies = [
+        pltpu.make_async_copy(part, y_ref, sem),
+        pltpu.make_async_copy(from_prev, f_ref.at[pl.ds(0, 2)], sem),
+        pltpu.make_async_copy(from_next, f_ref.at[pl.ds(2, 2)], sem),
     ]
     start_all(copies)
     clear(send)
     wait_all(copies)
-    for row, base in ((0, 0), (8, 12)):
-        smooth(lambda p, r: w_ref[base + p, pl.ds(r, 8), :], dest, x_ref, y_ref, send, row)
+    for t in range(NY // 8):
+        mean = [five_rows(lambda k: f_ref[i, pl.ds(8 + 8 * t + k, 8), :]) for i in range(4)]
+        for plane, more in ((0, mean[0] + mean[1]), (1, mean[1]), (14, mean[2]), (15, mean[2] + mean[3])):
+            at = pl.ds(plane * NY + 8 * t, 8)
+            y_ref[at, :] = y_ref[at, :] + more
+    for n in range(2):
+        put_boxes(dest, y_ref, n * 8 * NY, send, 8 * n)
 
 
 ANY = pl.BlockSpec(memory_space=pl.ANY)
@@ -646,16 +674,26 @@
     new_density, new_momentum, new_energy, sums_outer, to_next, to_prev = outer
     from_prev = shifted(to_next, "box", 1)
     from_next = shifted(to_prev, "box", -1)
+    part = pl.pallas_call(
+        near_kernel,
+        out_shape=shape(16 * NY, NZ),
+        in_specs=[ANY] * 2,
+        out_specs=VMEM,
+        scratch_shapes=[pltpu.VMEM((24, FRAME, NZ), F32), pltpu.VMEM((8 * FRAME, NZ), F32), pltpu.SemaphoreType.DMA],
+        compiler_params=params(54),
+        cost_estimate=cost(3),
+        name="near",
+    )(sums_inner, sums_outer)
     send_rest = pl.pallas_call(
         rest_kernel,
         out_shape=shape(32, 16, 1024),
-        in_specs=[SMEM] + [ANY] * 4,
+        in_specs=[SMEM] + [ANY] * 3,
         out_specs=VMEM,
-        scratch_shapes=[pltpu.VMEM((24, FRAME, NZ), F32)] + smooth_scratch() + [pltpu.SemaphoreType.DMA],
+        scratch_shapes=[pltpu.VMEM((16 * NY, NZ), F32), pltpu.VMEM((4, FRAME, NZ), F32), pltpu.SemaphoreType.DMA],
         compiler_params=params(54),
-        cost_estimate=cost(5),
+        cost_estimate=cost(3),
         name="rest",
-    )(dest, sums_inner, sums_outer, from_prev, from_next)
+    )(dest, part, from_prev, from_next)
     send_rest, got_inner = lax.optimization_barrier((send_rest, got_inner))
     got_rest = exchange(send_rest, 16)
     kd = jnp.concatenate([got_rest[:, :, :8], got_inner, got_rest[:, :, 8:]], axis=2)

time: 130 us -> 130 us (level)
  waiting for transfers between devices: 16.8 us -> 14.1 us
  Pallas kernels: 55.3 us -> 57.3 us
    ppermute x6, waiting for transfers between devices: 16.8 us -> 14.1 us  [shifted(): lax.ppermute(value, axis, [(i, (i + by) % size) for i in range(size)])]
    pallas_call x0 -> x1, Pallas kernels: none -> 2.74 us  [body(): pl.pallas_call(near_kernel, out_shape=shape(16 * NY, NZ), in_specs=[ANY]...]
  transfers between devices with their start and end apart: 7 -> 7, of which waited for: 2 -> 2; matrix products, arithmetic and copies ran while one was open for 0% -> 0% of each run, Pallas kernels for 39% -> 40%
where the time goes in v9:
time: 130 us; the launch traced here: 129 us
  Pallas kernels  57.3 us (44%)
  blocking collectives  37.2 us (29%)
  starting transfers between devices  16.3 us (13%)
  waiting for transfers between devices  14.1 us (11%)
  other arithmetic  2.55 us (2%)
    all_to_all x1, blocking collectives, exchange(): lax.all_to_all(send.reshape(16, 2, planes, 1024), 'box', split_axis=0, co...  37.2 us
    pallas_call x1, Pallas kernels, body(): pl.pallas_call(inner_kernel, out_shape=FIELD_SHAPES + (shape(WIDE, FRAME,...  23.3 us
    ppermute x6, waiting for transfers between devices, shifted(): lax.ppermute(value, axis, [(i, (i + by) % size) for i in range(size)])  14.1 us
    ppermute x6, starting transfers between devices, shifted(): lax.ppermute(value, axis, [(i, (i + by) % size) for i in range(size)])  12.6 us
    pallas_call x1, Pallas kernels, body(): pl.pallas_call(outer_kernel, out_shape=FIELD_SHAPES + (shape(8, FRAME, NZ...  12.3 us
    pallas_call x1, Pallas kernels, body(): pl.pallas_call(x_kernel, out_shape=shape(5, WIDE, NY, NZ), in_specs=[ANY]...  9.99 us
    pallas_call x1, Pallas kernels, body(): pl.pallas_call(rest_kernel, out_shape=shape(32, 16, 1024), in_specs=[SMEM...  3.82 us
    all_to_all x1, starting transfers between devices, exchange(): lax.all_to_all(send.reshape(16, 2, planes, 1024), 'box', split_axis=0, co...  3.74 us
  transfers between devices with their start and end apart: 7, of which 2 were waited for; matrix products, arithmetic and copies ran while one was open for 0% of the time, Pallas kernels for 40%

profile of v9, /device:TPU:32, one launch (start us, length us, event | category | flops | bytes accessed | tf_op | source)
XLA Modules:
  0.0 129.0 jit_solution(16532082467773663491)
XLA Ops:
  0.6 2.5 %pack_y.1 = (f32[6,32,8,128]{3,2,1,0:T(8,128)}, f32[6,32,8,128]{3,2,1,0:T(8,128)}) custom-call(f32[32,96,128]{2,1,0:T(8,128)} %density.7, f32[3,32,96,128]{3,2,1,0:T(8,128)} %momentum.7, f32[32,96,128]{2,1,0:T(8,128)} %energy.7, f32[32,96,128]{2,1,0:T(8,128)} %dm.5), custom_call_target="tpu_custom_call" | custom-call | flops 3300000000 | tf_op jit(solution)/shard_map/pack_y/pallas_call | solution.py:608
  3.2 0.0 collective-permute-start
  3.2 1.7 %collective-permute-start.1 = (f32[6,32,8,128]{3,2,1,0:T(8,128)}, f32[6,32,8,128]{3,2,1,0:T(8,128)}, u32[]{:S(2)}, u32[]{:S(2)}) collective-permute-start(f32[6,32,8,128]{3,2,1,0:T(8,128)} %get-tuple-element.22), channel_id=1, source_target_pairs={{0,7},{1,0},{2,1},{3,2},{4,3},{5,4},{6,5},{7,6},{8,15},{9,8},{10,9... | collective-permute-start | bytes 2359304 | tf_op jit(solution)/shard_map/ppermute | solution.py:601
  4.9 10.0 %x_own.1.swept = f32[5,24,96,128]{3,2,1,0:T(8,128)} custom-call(f32[32,96,128]{2,1,0:T(8,128)} %density.7, f32[3,32,96,128]{3,2,1,0:T(8,128)} %momentum.7, f32[32,96,128]{2,1,0:T(8,128)} %energy.7), custom_call_target="tpu_custom_call" | custom-call | flops 9900000256 | tf_op jit(solution)/shard_map/x_own/pallas_call | solution.py:621
  14.9 0.0 collective-permute-done.y_before
  14.9 0.0 collective-permute-done.1.y_after
  15.0 2.6 %pack_x.1 = (f32[5,3,112,128]{3,2,1,0:T(8,128)}, f32[5,3,112,128]{3,2,1,0:T(8,128)}) custom-call(f32[32,96,128]{2,1,0:T(8,128)} %density.7, f32[3,32,96,128]{3,2,1,0:T(8,128)} %momentum.7, f32[32,96,128]{2,1,0:T(8,128)} %energy.7, f32[6,32,8,128]{3,2,1,0:T(8,128)} %collective-permute-done.y_before, f32[6,32,8,128]{3,2,1,0:T(8,128)} %collective-permute-done.1.y_after), custom_call_target="tpu_custom_call" | custom-call | flops 3300000000 | tf_op jit(solution)/shard_map/pack_x/pallas_call | solution.py:634
  17.6 1.6 %collective-permute-start.2 = (f32[5,3,112,128]{3,2,1,0:T(8,128)}, f32[5,3,112,128]{3,2,1,0:T(8,128)}, u32[]{:S(2)}, u32[]{:S(2)}) collective-permute-start(f32[5,3,112,128]{3,2,1,0:T(8,128)} %get-tuple-element.23), channel_id=1, source_target_pairs={{0,8},{8,16},{16,24},{24,32},{32,40},{40,48},{48,56},{56,64},{64,7... | collective-permute-start | bytes 2580488 | tf_op jit(solution)/shard_map/ppermute | solution.py:601
  19.1 3.9 %collective-permute-start.3 = (f32[5,3,112,128]{3,2,1,0:T(8,128)}, f32[5,3,112,128]{3,2,1,0:T(8,128)}, u32[]{:S(2)}, u32[]{:S(2)}) collective-permute-start(f32[5,3,112,128]{3,2,1,0:T(8,128)} %get-tuple-element.24), channel_id=1, source_target_pairs={{0,120},{8,0},{16,8},{24,16},{32,24},{40,32},{48,40},{56,48},{64,5... | collective-permute-start | bytes 2580488 | tf_op jit(solution)/shard_map/ppermute | solution.py:601
  23.0 23.3 %inner.1 = (f32[32,96,128]{2,1,0:T(8,128)}, f32[3,32,96,128]{3,2,1,0:T(8,128)}, f32[32,96,128]{2,1,0:T(8,128)}, f32[24,112,128]{2,1,0:T(8,128)}, f32[32,16,1024]{2,1,0:T(8,128)}) custom-call(s32[12]{0:T(128)} %bitcast.7, bf16[256,384]{1,0:T(8,128)(2,1)} %constant.2.clone.weights, f32[5,24,96,128]{3,2,1,0:T(8,128)} %x_own.1.swept, f32[32,96,128]{2,1,0:T(8,128)} %dm.5, ...), custom_call_target="tpu_custom_call" | custom-call | flops 28600000512 | tf_op jit(solution)/shard_map/inner/pallas_call | solution.py:650
  46.3 3.7 %all-to-all-start = ((f32[16,2,16,1024]{3,2,1,0:T(8,128)}), f32[16,2,16,1024]{3,2,1,0:T(8,128)S(1)}, u32[]{:S(2)}, u32[]{:S(2)}) async-start(f32[16,2,16,1024]{3,2,1,0:T(8,128)} %bitcast.5), calls=%async_computation | async-start | bytes 4194304 | tf_op jit(solution)/shard_map/all_to_all | solution.py:648
  50.1 0.0 collective-permute-done.2.x_before
  50.1 0.0 collective-permute-done.3.x_after
  50.1 12.3 %outer.1 = (f32[32,96,128]{2,1,0:T(8,128)}, f32[3,32,96,128]{3,2,1,0:T(8,128)}, f32[32,96,128]{2,1,0:T(8,128)}, f32[8,112,128]{2,1,0:T(8,128)}, f32[2,112,128]{2,1,0:T(8,128)}, /*index=5*/f32[2,112,128]{2,1,0:T(8,128)}) custom-call(bf16[256,384]{1,0:T(8,128)(2,1)} %constant.2.clone.weights, ...), custom_call_target="tpu_custom_call", output_to_operand_aliasing={{0}: (9, {}), {1}: (10, {}), {2}: (11, {})} | custom-call | flops 14300000256 | tf_op jit(solution)/shard_map/outer/pallas_call | solution.py:663
  62.4 2.0 %collective-permute-start.4 = (f32[2,112,128]{2,1,0:T(8,128)}, f32[2,112,128]{2,1,0:T(8,128)S(1)}, u32[]{:S(2)}, u32[]{:S(2)}) collective-permute-start(f32[2,112,128]{2,1,0:T(8,128)} %get-tuple-element.33), channel_id=1, source_target_pairs={{0,8},{8,16},{16,24},{24,32},{32,40},{40,48},{48,56},{56,64},{64,7... | collective-permute-start | bytes 344072 | tf_op jit(solution)/shard_map/ppermute | solution.py:601
  64.4 3.4 %collective-permute-start.5 = (f32[2,112,128]{2,1,0:T(8,128)}, f32[2,112,128]{2,1,0:T(8,128)S(1)}, u32[]{:S(2)}, u32[]{:S(2)}) collective-permute-start(f32[2,112,128]{2,1,0:T(8,128)} %get-tuple-element.34), channel_id=1, source_target_pairs={{0,120},{8,0},{16,8},{24,16},{32,24},{40,32},{48,40},{56,48},{64,5... | collective-permute-start | bytes 344072 | tf_op jit(solution)/shard_map/ppermute | solution.py:601
  67.8 2.7 %near.1.part = f32[1536,128]{1,0:T(8,128)} custom-call(f32[24,112,128]{2,1,0:T(8,128)} %get-tuple-element.31.sums_inner, f32[8,112,128]{2,1,0:T(8,128)} %get-tuple-element.32.sums_outer), custom_call_target="tpu_custom_call" | custom-call | flops 3300000000 | tf_op jit(solution)/shard_map/near/pallas_call | solution.py:677
  70.6 10.5 %collective-permute-done.4.from_prev = f32[2,112,128]{2,1,0:T(8,128)S(1)} collective-permute-done((f32[2,112,128]{2,1,0:T(8,128)}, f32[2,112,128]{2,1,0:T(8,128)S(1)}, u32[]{:S(2)}, u32[]{:S(2)}) %collective-permute-start.4) | collective-permute-done | bytes 114720 | tf_op jit(solution)/shard_map/ppermute | solution.py:601
  81.1 0.0 copy-start
  81.1 3.5 %collective-permute-done.5.from_next = f32[2,112,128]{2,1,0:T(8,128)S(1)} collective-permute-done((f32[2,112,128]{2,1,0:T(8,128)}, f32[2,112,128]{2,1,0:T(8,128)S(1)}, u32[]{:S(2)}, u32[]{:S(2)}) %collective-permute-start.5) | collective-permute-done | bytes 114720 | tf_op jit(solution)/shard_map/ppermute | solution.py:601
  84.6 0.0 copy-done
  84.6 0.0 copy-start.1
  84.6 0.7 copy-done.1
  85.3 3.8 %rest.1 = f32[32,16,1024]{2,1,0:T(8,128)} custom-call(s32[12]{0:T(128)} %bitcast.8, f32[1536,128]{1,0:T(8,128)} %near.1.part, f32[2,112,128]{2,1,0:T(8,128)} %copy-done, f32[2,112,128]{2,1,0:T(8,128)} %copy-done.1), custom_call_target="tpu_custom_call" | custom-call | flops 3300000000 | tf_op jit(solution)/shard_map/rest/pallas_call | solution.py:687
  89.1 0.0 all-to-all-done
  89.1 37.2 %all_to_all.10 = f32[16,2,16,1024]{3,2,1,0:T(8,128)S(1)} all-to-all(f32[16,2,16,1024]{3,2,1,0:T(8,128)} %bitcast.6), channel_id=1, replica_groups=mesh['box'=16,'grp'=8] {'box'}, dimensions={0} | all-to-all | bytes 4194304 | tf_op jit(solution)/shard_map/all_to_all | solution.py:648
  126.3 0.1 fusion
  126.4 2.5 %maximum_bitcast_fusion = f32[1,1,16,2,32,1024]{5,4,3,2,1,0:T(8,128)} fusion(f32[16,2,8,1024]{3,2,1,0:T(8,128)S(1)} %get-tuple-element.39, f32[16,2,16,1024]{3,2,1,0:T(8,128)S(1)} %all-to-all-done, f32[16,2,8,1024]{3,2,1,0:T(8,128)S(1)} %get-tuple-element.38), kind=kLoop, calls=%fused_computation | loop fusion | flops 2097152 | bytes 8388608 | tf_op jit(solution)/shard_map/broadcast_in_dim | solution.py:700
Async XLA Ops:
  3.2 11.8 %collective-permute-start = (f32[6,32,8,128]{3,2,1,0:T(8,128)}, f32[6,32,8,128]{3,2,1,0:T(8,128)}, u32[]{:S(2)}, u32[]{:S(2)}) collective-permute-start(f32[6,32,8,128]{3,2,1,0:T(8,128)} %get-tuple-element.21), channel_id=1, source_target_pairs={{0,1},{1,2},{2,3},{3,4},{4,5},{5,6},{6,7},{7,0},{8,9},{9,10},{10,1... | collective-permute-start | bytes 2359304 | tf_op jit(solution)/shard_map/ppermute | solution.py:601
  3.2 11.7 %collective-permute-start.1 = (f32[6,32,8,128]{3,2,1,0:T(8,128)}, f32[6,32,8,128]{3,2,1,0:T(8,128)}, u32[]{:S(2)}, u32[]{:S(2)}) collective-permute-start(f32[6,32,8,128]{3,2,1,0:T(8,128)} %get-tuple-element.22), channel_id=1, source_target_pairs={{0,7},{1,0},{2,1},{3,2},{4,3},{5,4},{6,5},{7,6},{8,15},{9,8},{10,9... | collective-permute-start | bytes 2359304 | tf_op jit(solution)/shard_map/ppermute | solution.py:601
  17.6 32.5 %collective-permute-start.2 = (f32[5,3,112,128]{3,2,1,0:T(8,128)}, f32[5,3,112,128]{3,2,1,0:T(8,128)}, u32[]{:S(2)}, u32[]{:S(2)}) collective-permute-start(f32[5,3,112,128]{3,2,1,0:T(8,128)} %get-tuple-element.23), channel_id=1, source_target_pairs={{0,8},{8,16},{16,24},{24,32},{32,40},{40,48},{48,56},{56,64},{64,7... | collective-permute-start | bytes 2580488 | tf_op jit(solution)/shard_map/ppermute | solution.py:601
  19.1 31.0 %collective-permute-start.3 = (f32[5,3,112,128]{3,2,1,0:T(8,128)}, f32[5,3,112,128]{3,2,1,0:T(8,128)}, u32[]{:S(2)}, u32[]{:S(2)}) collective-permute-start(f32[5,3,112,128]{3,2,1,0:T(8,128)} %get-tuple-element.24), channel_id=1, source_target_pairs={{0,120},{8,0},{16,8},{24,16},{32,24},{40,32},{48,40},{56,48},{64,5... | collective-permute-start | bytes 2580488 | tf_op jit(solution)/shard_map/ppermute | solution.py:601
  46.3 42.8 %all-to-all-start = ((f32[16,2,16,1024]{3,2,1,0:T(8,128)}), f32[16,2,16,1024]{3,2,1,0:T(8,128)S(1)}, u32[]{:S(2)}, u32[]{:S(2)}) async-start(f32[16,2,16,1024]{3,2,1,0:T(8,128)} %bitcast.5), calls=%async_computation | async-start | bytes 4194304 | tf_op jit(solution)/shard_map/all_to_all | solution.py:648
  62.4 18.7 %collective-permute-start.4 = (f32[2,112,128]{2,1,0:T(8,128)}, f32[2,112,128]{2,1,0:T(8,128)S(1)}, u32[]{:S(2)}, u32[]{:S(2)}) collective-permute-start(f32[2,112,128]{2,1,0:T(8,128)} %get-tuple-element.33), channel_id=1, source_target_pairs={{0,8},{8,16},{16,24},{24,32},{32,40},{40,48},{48,56},{56,64},{64,7... | collective-permute-start | bytes 344072 | tf_op jit(solution)/shard_map/ppermute | solution.py:601
  64.4 20.2 %collective-permute-start.5 = (f32[2,112,128]{2,1,0:T(8,128)}, f32[2,112,128]{2,1,0:T(8,128)S(1)}, u32[]{:S(2)}, u32[]{:S(2)}) collective-permute-start(f32[2,112,128]{2,1,0:T(8,128)} %get-tuple-element.34), channel_id=1, source_target_pairs={{0,120},{8,0},{16,8},{24,16},{32,24},{40,32},{48,40},{56,48},{64,5... | collective-permute-start | bytes 344072 | tf_op jit(solution)/shard_map/ppermute | solution.py:601
  81.1 3.5 %copy-start = (f32[2,112,128]{2,1,0:T(8,128)}, f32[2,112,128]{2,1,0:T(8,128)S(1)}, u32[]{:S(2)}) copy-start(f32[2,112,128]{2,1,0:T(8,128)S(1)} %collective-permute-done.4.from_prev) | copy-start | bytes 344068
  84.6 0.7 copy-start.1

commit v10 on v8

--- a/solution.py
+++ b/solution.py
@@ -445,9 +445,14 @@
     lax.fori_loop(0, NY // 8, end, 0)
 
 
+def half_copy(send, out, row, sem):
+    rows = pl.ds(row, 8)
+    return pltpu.make_async_copy(send.at[:, rows], out.at[:, rows], sem)
+
+
 def inner_kernel(dest, weights, swept, dm, y_before, y_after,
-                 out_density, out_momentum, out_energy, out_sums, send,
-                 q_ref, s_ref, o_ref, dm_ref, t_ref, w_ref, swept_ref, edge_ref, x_ref, y_ref, sems, sem, out_sem):
+                 out_density, out_momentum, out_energy, out_sums, send_out,
+                 q_ref, s_ref, o_ref, dm_ref, t_ref, w_ref, swept_ref, edge_ref, x_ref, y_ref, send, sems, sem, out_sem):
     held = pl.ds(1, WIDE + 6)
     s4 = s_ref.reshape(5, WIDE, STRIDE, NZ)
     outs = (out_density, out_momentum, out_energy)
@@ -475,7 +480,10 @@
     sums.start()
     for row, base in ((0, 2), (8, 10)):
         smooth(lambda p, r: t_ref[pl.ds((base + p) * STRIDE + r, 8), :], dest, x_ref, y_ref, send, row)
+        half_copy(send, send_out, row, sems.at[4 + row // 8]).start()
     sums.wait()
+    for row in (0, 8):
+        half_copy(send, send_out, row, sems.at[4 + row // 8]).wait()
     for g in range(WIDE // 8):
         wait_all(leaving(g))
 
@@ -508,7 +516,7 @@
     wait_all(leaving)
 
 
-def rest_kernel(dest, sums_inner, sums_outer, from_prev, from_next, send, w_ref, x_ref, y_ref, sem):
+def rest_kernel(dest, sums_inner, sums_outer, from_prev, from_next, send_out, w_ref, x_ref, y_ref, send, sem, out_sems):
     def part(src, own, place, count):
         return pltpu.make_async_copy(src.at[pl.ds(own, count)], w_ref.at[pl.ds(place, count)], sem)
 
@@ -525,6 +533,9 @@
     wait_all(copies)
     for row, base in ((0, 0), (8, 12)):
         smooth(lambda p, r: w_ref[base + p, pl.ds(r, 8), :], dest, x_ref, y_ref, send, row)
+        half_copy(send, send_out, row, out_sems.at[row // 8]).start()
+    for row in (0, 8):
+        half_copy(send, send_out, row, out_sems.at[row // 8]).wait()
 
 
 ANY = pl.BlockSpec(memory_space=pl.ANY)
@@ -623,8 +634,8 @@
         inner_kernel,
         out_shape=FIELD_SHAPES + (shape(WIDE, FRAME, NZ), shape(32, 16, 1024)),
         in_specs=[SMEM] + [ANY] * 5,
-        out_specs=[ANY] * 4 + [VMEM],
-        scratch_shapes=main_scratch(WIDE, WIDE + 6, 16) + smooth_scratch() + semaphores(),
+        out_specs=[ANY] * 5,
+        scratch_shapes=main_scratch(WIDE, WIDE + 6, 16) + smooth_scratch() + [pltpu.VMEM((32, 16, 1024), F32)] + semaphores(),
         compiler_params=params(64),
         cost_estimate=cost(26),
         name="inner",
@@ -650,8 +661,9 @@
         rest_kernel,
         out_shape=shape(32, 16, 1024),
         in_specs=[SMEM] + [ANY] * 4,
-        out_specs=VMEM,
-        scratch_shapes=[pltpu.VMEM((24, FRAME, NZ), F32)] + smooth_scratch() + [pltpu.SemaphoreType.DMA],
+        out_specs=ANY,
+        scratch_shapes=[pltpu.VMEM((24, FRAME, NZ), F32)] + smooth_scratch() + [
+            pltpu.VMEM((32, 16, 1024), F32), pltpu.SemaphoreType.DMA, pltpu.SemaphoreType.DMA((2,))],
         compiler_params=params(54),
         cost_estimate=cost(5),
         name="rest",

time: 130 us -> 129 us (level)
  transfers between devices with their start and end apart: 7 -> 7, of which waited for: 2 -> 2; matrix products, arithmetic and copies ran while one was open for 0% -> 0% of each run, Pallas kernels for 39% -> 38%
where the time goes in v10:
time: 129 us; the launch traced here: 128 us
  Pallas kernels  54.3 us (42%)
  blocking collectives  36.6 us (28%)
  waiting for transfers between devices  16.8 us (13%)
  starting transfers between devices  16.3 us (13%)
  other arithmetic  2.55 us (2%)
    all_to_all x1, blocking collectives, exchange(): lax.all_to_all(send.reshape(16, 2, planes, 1024), 'box', split_axis=0, co...  36.6 us
    pallas_call x1, Pallas kernels, body(): pl.pallas_call(inner_kernel, out_shape=FIELD_SHAPES + (shape(WIDE, FRAME,...  22.7 us
    ppermute x6, waiting for transfers between devices, shifted(): lax.ppermute(value, axis, [(i, (i + by) % size) for i in range(size)])  16.8 us
    ppermute x6, starting transfers between devices, shifted(): lax.ppermute(value, axis, [(i, (i + by) % size) for i in range(size)])  12.6 us
    pallas_call x1, Pallas kernels, body(): pl.pallas_call(outer_kernel, out_shape=FIELD_SHAPES + (shape(8, FRAME, NZ...  12.3 us
    pallas_call x1, Pallas kernels, body(): pl.pallas_call(x_kernel, out_shape=shape(5, WIDE, NY, NZ), in_specs=[ANY]...  9.99 us
    pallas_call x1, Pallas kernels, body(): pl.pallas_call(rest_kernel, out_shape=shape(32, 16, 1024), in_specs=[SMEM...  4.19 us
    all_to_all x1, starting transfers between devices, exchange(): lax.all_to_all(send.reshape(16, 2, planes, 1024), 'box', split_axis=0, co...  3.74 us
  transfers between devices with their start and end apart: 7, of which 2 were waited for; matrix products, arithmetic and copies ran while one was open for 0% of the time, Pallas kernels for 38%

profile of v10, /device:TPU:32, one launch (start us, length us, event | category | flops | bytes accessed | tf_op | source)
XLA Modules:
  0.0 128.1 jit_solution(11817613833429571954)
XLA Ops:
  0.6 2.5 %pack_y.1 = (f32[6,32,8,128]{3,2,1,0:T(8,128)}, f32[6,32,8,128]{3,2,1,0:T(8,128)}) custom-call(f32[32,96,128]{2,1,0:T(8,128)} %density.7, f32[3,32,96,128]{3,2,1,0:T(8,128)} %momentum.7, f32[32,96,128]{2,1,0:T(8,128)} %energy.7, f32[32,96,128]{2,1,0:T(8,128)} %dm.5), custom_call_target="tpu_custom_call" | custom-call | flops 3300000000 | tf_op jit(solution)/shard_map/pack_y/pallas_call | solution.py:591
  3.2 0.0 collective-permute-start
  3.2 1.7 %collective-permute-start.1 = (f32[6,32,8,128]{3,2,1,0:T(8,128)}, f32[6,32,8,128]{3,2,1,0:T(8,128)}, u32[]{:S(2)}, u32[]{:S(2)}) collective-permute-start(f32[6,32,8,128]{3,2,1,0:T(8,128)} %get-tuple-element.22), channel_id=1, source_target_pairs={{0,7},{1,0},{2,1},{3,2},{4,3},{5,4},{6,5},{7,6},{8,15},{9,8},{10,9... | collective-permute-start | bytes 2359304 | tf_op jit(solution)/shard_map/ppermute | solution.py:584
  4.9 10.0 %x_own.1.swept = f32[5,24,96,128]{3,2,1,0:T(8,128)} custom-call(f32[32,96,128]{2,1,0:T(8,128)} %density.7, f32[3,32,96,128]{3,2,1,0:T(8,128)} %momentum.7, f32[32,96,128]{2,1,0:T(8,128)} %energy.7), custom_call_target="tpu_custom_call" | custom-call | flops 9900000256 | tf_op jit(solution)/shard_map/x_own/pallas_call | solution.py:604
  14.9 0.0 collective-permute-done.y_before
  14.9 0.0 collective-permute-done.1.y_after
  15.0 2.6 %pack_x.1 = (f32[5,3,112,128]{3,2,1,0:T(8,128)}, f32[5,3,112,128]{3,2,1,0:T(8,128)}) custom-call(f32[32,96,128]{2,1,0:T(8,128)} %density.7, f32[3,32,96,128]{3,2,1,0:T(8,128)} %momentum.7, f32[32,96,128]{2,1,0:T(8,128)} %energy.7, f32[6,32,8,128]{3,2,1,0:T(8,128)} %collective-permute-done.y_before, f32[6,32,8,128]{3,2,1,0:T(8,128)} %collective-permute-done.1.y_after), custom_call_target="tpu_custom_call" | custom-call | flops 3300000000 | tf_op jit(solution)/shard_map/pack_x/pallas_call | solution.py:617
  17.6 1.6 %collective-permute-start.2 = (f32[5,3,112,128]{3,2,1,0:T(8,128)}, f32[5,3,112,128]{3,2,1,0:T(8,128)}, u32[]{:S(2)}, u32[]{:S(2)}) collective-permute-start(f32[5,3,112,128]{3,2,1,0:T(8,128)} %get-tuple-element.23), channel_id=1, source_target_pairs={{0,8},{8,16},{16,24},{24,32},{32,40},{40,48},{48,56},{56,64},{64,7... | collective-permute-start | bytes 2580488 | tf_op jit(solution)/shard_map/ppermute | solution.py:584
  19.1 3.9 %collective-permute-start.3 = (f32[5,3,112,128]{3,2,1,0:T(8,128)}, f32[5,3,112,128]{3,2,1,0:T(8,128)}, u32[]{:S(2)}, u32[]{:S(2)}) collective-permute-start(f32[5,3,112,128]{3,2,1,0:T(8,128)} %get-tuple-element.24), channel_id=1, source_target_pairs={{0,120},{8,0},{16,8},{24,16},{32,24},{40,32},{48,40},{56,48},{64,5... | collective-permute-start | bytes 2580488 | tf_op jit(solution)/shard_map/ppermute | solution.py:584
  23.0 22.7 %inner.1 = (f32[32,96,128]{2,1,0:T(8,128)}, f32[3,32,96,128]{3,2,1,0:T(8,128)}, f32[32,96,128]{2,1,0:T(8,128)}, f32[24,112,128]{2,1,0:T(8,128)}, f32[32,16,1024]{2,1,0:T(8,128)}) custom-call(s32[12]{0:T(128)} %bitcast.7, bf16[256,384]{1,0:T(8,128)(2,1)} %constant.2.clone.weights, f32[5,24,96,128]{3,2,1,0:T(8,128)} %x_own.1.swept, f32[32,96,128]{2,1,0:T(8,128)} %dm.5, ...), custom_call_target="tpu_custom_call" | custom-call | flops 28600000512 | tf_op jit(solution)/shard_map/inner/pallas_call | solution.py:633
  45.7 3.7 %all-to-all-start = ((f32[16,2,16,1024]{3,2,1,0:T(8,128)}), f32[16,2,16,1024]{3,2,1,0:T(8,128)S(1)}, u32[]{:S(2)}, u32[]{:S(2)}) async-start(f32[16,2,16,1024]{3,2,1,0:T(8,128)} %bitcast.5), calls=%async_computation | async-start | bytes 4194304 | tf_op jit(solution)/shard_map/all_to_all | solution.py:631
  49.4 0.0 collective-permute-done.2.x_before
  49.4 0.0 collective-permute-done.3.x_after
  49.4 12.3 %outer.1 = (f32[32,96,128]{2,1,0:T(8,128)}, f32[3,32,96,128]{3,2,1,0:T(8,128)}, f32[32,96,128]{2,1,0:T(8,128)}, f32[8,112,128]{2,1,0:T(8,128)}, f32[2,112,128]{2,1,0:T(8,128)}, /*index=5*/f32[2,112,128]{2,1,0:T(8,128)}) custom-call(bf16[256,384]{1,0:T(8,128)(2,1)} %constant.2.clone.weights, ...), custom_call_target="tpu_custom_call", output_to_operand_aliasing={{0}: (9, {}), {1}: (10, {}), {2}: (11, {})} | custom-call | flops 14300000256 | tf_op jit(solution)/shard_map/outer/pallas_call | solution.py:646
  61.8 2.0 %collective-permute-start.4 = (f32[2,112,128]{2,1,0:T(8,128)}, f32[2,112,128]{2,1,0:T(8,128)S(1)}, u32[]{:S(2)}, u32[]{:S(2)}) collective-permute-start(f32[2,112,128]{2,1,0:T(8,128)} %get-tuple-element.33), channel_id=1, source_target_pairs={{0,8},{8,16},{16,24},{24,32},{32,40},{40,48},{48,56},{56,64},{64,7... | collective-permute-start | bytes 344072 | tf_op jit(solution)/shard_map/ppermute | solution.py:584
  63.7 3.4 %collective-permute-start.5 = (f32[2,112,128]{2,1,0:T(8,128)}, f32[2,112,128]{2,1,0:T(8,128)S(1)}, u32[]{:S(2)}, u32[]{:S(2)}) collective-permute-start(f32[2,112,128]{2,1,0:T(8,128)} %get-tuple-element.34), channel_id=1, source_target_pairs={{0,120},{8,0},{16,8},{24,16},{32,24},{40,32},{48,40},{56,48},{64,5... | collective-permute-start | bytes 344072 | tf_op jit(solution)/shard_map/ppermute | solution.py:584
  67.2 13.3 %collective-permute-done.4.from_prev = f32[2,112,128]{2,1,0:T(8,128)S(1)} collective-permute-done((f32[2,112,128]{2,1,0:T(8,128)}, f32[2,112,128]{2,1,0:T(8,128)S(1)}, u32[]{:S(2)}, u32[]{:S(2)}) %collective-permute-start.4) | collective-permute-done | bytes 114720 | tf_op jit(solution)/shard_map/ppermute | solution.py:584
  80.4 0.0 copy-start
  80.4 3.5 %collective-permute-done.5.from_next = f32[2,112,128]{2,1,0:T(8,128)S(1)} collective-permute-done((f32[2,112,128]{2,1,0:T(8,128)}, f32[2,112,128]{2,1,0:T(8,128)S(1)}, u32[]{:S(2)}, u32[]{:S(2)}) %collective-permute-start.5) | collective-permute-done | bytes 114720 | tf_op jit(solution)/shard_map/ppermute | solution.py:584
  84.0 0.0 copy-start.1
  84.0 0.0 copy-done
  84.0 0.6 copy-done.1
  84.6 4.2 %rest.1 = f32[32,16,1024]{2,1,0:T(8,128)} custom-call(s32[12]{0:T(128)} %bitcast.8, f32[24,112,128]{2,1,0:T(8,128)} %get-tuple-element.31.sums_inner, f32[8,112,128]{2,1,0:T(8,128)} %get-tuple-element.32.sums_outer, f32[2,112,128]{2,1,0:T(8,128)} %copy-done, f32[2,112,128]{2,1,0:T(8,128)} %copy-done.1), custom_call_target="tpu_custom_call" | custom-call | flops 5500000256 | tf_op jit(solution)/shard_map/rest/pallas_call | solution.py:660
  88.8 0.0 all-to-all-done
  88.8 36.6 %all_to_all.10 = f32[16,2,16,1024]{3,2,1,0:T(8,128)S(1)} all-to-all(f32[16,2,16,1024]{3,2,1,0:T(8,128)} %bitcast.6), channel_id=1, replica_groups=mesh['box'=16,'grp'=8] {'box'}, dimensions={0} | all-to-all | bytes 4194304 | tf_op jit(solution)/shard_map/all_to_all | solution.py:631
  125.4 0.1 fusion
  125.5 2.5 %maximum_bitcast_fusion = f32[1,1,16,2,32,1024]{5,4,3,2,1,0:T(8,128)} fusion(f32[16,2,8,1024]{3,2,1,0:T(8,128)S(1)} %get-tuple-element.39, f32[16,2,16,1024]{3,2,1,0:T(8,128)S(1)} %all-to-all-done, f32[16,2,8,1024]{3,2,1,0:T(8,128)S(1)} %get-tuple-element.38), kind=kLoop, calls=%fused_computation | loop fusion | flops 2097152 | bytes 8388608 | tf_op jit(solution)/shard_map/broadcast_in_dim | solution.py:674
Async XLA Ops:
  3.2 11.8 %collective-permute-start = (f32[6,32,8,128]{3,2,1,0:T(8,128)}, f32[6,32,8,128]{3,2,1,0:T(8,128)}, u32[]{:S(2)}, u32[]{:S(2)}) collective-permute-start(f32[6,32,8,128]{3,2,1,0:T(8,128)} %get-tuple-element.21), channel_id=1, source_target_pairs={{0,1},{1,2},{2,3},{3,4},{4,5},{5,6},{6,7},{7,0},{8,9},{9,10},{10,1... | collective-permute-start | bytes 2359304 | tf_op jit(solution)/shard_map/ppermute | solution.py:584
  3.2 11.7 %collective-permute-start.1 = (f32[6,32,8,128]{3,2,1,0:T(8,128)}, f32[6,32,8,128]{3,2,1,0:T(8,128)}, u32[]{:S(2)}, u32[]{:S(2)}) collective-permute-start(f32[6,32,8,128]{3,2,1,0:T(8,128)} %get-tuple-element.22), channel_id=1, source_target_pairs={{0,7},{1,0},{2,1},{3,2},{4,3},{5,4},{6,5},{7,6},{8,15},{9,8},{10,9... | collective-permute-start | bytes 2359304 | tf_op jit(solution)/shard_map/ppermute | solution.py:584
  17.6 31.9 %collective-permute-start.2 = (f32[5,3,112,128]{3,2,1,0:T(8,128)}, f32[5,3,112,128]{3,2,1,0:T(8,128)}, u32[]{:S(2)}, u32[]{:S(2)}) collective-permute-start(f32[5,3,112,128]{3,2,1,0:T(8,128)} %get-tuple-element.23), channel_id=1, source_target_pairs={{0,8},{8,16},{16,24},{24,32},{32,40},{40,48},{48,56},{56,64},{64,7... | collective-permute-start | bytes 2580488 | tf_op jit(solution)/shard_map/ppermute | solution.py:584
  19.1 30.3 %collective-permute-start.3 = (f32[5,3,112,128]{3,2,1,0:T(8,128)}, f32[5,3,112,128]{3,2,1,0:T(8,128)}, u32[]{:S(2)}, u32[]{:S(2)}) collective-permute-start(f32[5,3,112,128]{3,2,1,0:T(8,128)} %get-tuple-element.24), channel_id=1, source_target_pairs={{0,120},{8,0},{16,8},{24,16},{32,24},{40,32},{48,40},{56,48},{64,5... | collective-permute-start | bytes 2580488 | tf_op jit(solution)/shard_map/ppermute | solution.py:584
  45.7 43.1 %all-to-all-start = ((f32[16,2,16,1024]{3,2,1,0:T(8,128)}), f32[16,2,16,1024]{3,2,1,0:T(8,128)S(1)}, u32[]{:S(2)}, u32[]{:S(2)}) async-start(f32[16,2,16,1024]{3,2,1,0:T(8,128)} %bitcast.5), calls=%async_computation | async-start | bytes 4194304 | tf_op jit(solution)/shard_map/all_to_all | solution.py:631
  61.8 18.7 %collective-permute-start.4 = (f32[2,112,128]{2,1,0:T(8,128)}, f32[2,112,128]{2,1,0:T(8,128)S(1)}, u32[]{:S(2)}, u32[]{:S(2)}) collective-permute-start(f32[2,112,128]{2,1,0:T(8,128)} %get-tuple-element.33), channel_id=1, source_target_pairs={{0,8},{8,16},{16,24},{24,32},{32,40},{40,48},{48,56},{56,64},{64,7... | collective-permute-start | bytes 344072 | tf_op jit(solution)/shard_map/ppermute | solution.py:584
  63.7 20.2 %collective-permute-start.5 = (f32[2,112,128]{2,1,0:T(8,128)}, f32[2,112,128]{2,1,0:T(8,128)S(1)}, u32[]{:S(2)}, u32[]{:S(2)}) collective-permute-start(f32[2,112,128]{2,1,0:T(8,128)} %get-tuple-element.34), channel_id=1, source_target_pairs={{0,120},{8,0},{16,8},{24,16},{32,24},{40,32},{48,40},{56,48},{64,5... | collective-permute-start | bytes 344072 | tf_op jit(solution)/shard_map/ppermute | solution.py:584
  80.4 3.5 %copy-start = (f32[2,112,128]{2,1,0:T(8,128)}, f32[2,112,128]{2,1,0:T(8,128)S(1)}, u32[]{:S(2)}) copy-start(f32[2,112,128]{2,1,0:T(8,128)S(1)} %collective-permute-done.4.from_prev) | copy-start | bytes 344068
  84.0 0.6 copy-start.1
